TPU v7x, 256 devices: a whole 4x4x8 slice. The times are simulated.
256 devices in a mesh: segment: 4 (over y_lo, core), tile: 64 (over x, y_hi, z).
Axes of the slice: x: 4, y: 4 (y_hi: 2, y_lo: 2; y = y_hi * 2 + y_lo), z: 8, core: 2. Of those that a mesh axis runs over, the one named last changes fastest.
Arguments:
- slide_pixels: bfloat16 [128, 4096, 208], P('segment', 'tile'), may hold values from -6 to 6
- taps_fine: float32 [3, 3, 208], replicated, may hold values from -2 to 2
- mix_fine: bfloat16 [208, 208], replicated, may hold values from -0.4375 to 0.4375
- reduce_weight: bfloat16 [832, 416], replicated, may hold values from -0.21875 to 0.21875
- taps_coarse: float32 [5, 5, 416], replicated, may hold values from -1.25 to 1.25
- mix_coarse: bfloat16 [416, 416], replicated, may hold values from -0.3125 to 0.3125
- cotangent: bfloat16 [64, 2048, 416], P('segment', 'tile'), may hold values from -6 to 6
Outputs:
- section_out: bfloat16 [64, 2048, 416], P('segment', 'tile')
- pixel_grad: bfloat16 [128, 4096, 208], P('segment', 'tile')
- grad_taps_fine: float32 [3, 3, 208], replicated
- grad_mix_fine: float32 [208, 208], replicated
- grad_reduce: float32 [832, 416], replicated
- grad_taps_coarse: float32 [5, 5, 416], replicated
- grad_mix_coarse: float32 [416, 416], replicated
All inputs are finite; a program needn't handle non-finite values.
Results may differ from a plain program's by a relative error of at most 0.022.
Values may be sent and summed in bfloat16 or wider, within the bound.
No kernel may reach another device: no remote copies, remote signals or barrier semaphores. Data moves between devices by JAX's collectives and lax.ppermute only.
A program may use at most 64 MiB of HBM per device.

v0:
```python
import jax
import jax.numpy as jnp
from jax import lax
from jax.sharding import PartitionSpec as P


def with_halo(block, sides, width):
    for axis, dim in sides:
        count = lax.axis_size(axis)
        forward = [(i, i + 1) for i in range(count - 1)]
        backward = [(target, source) for source, target in forward]
        low = lax.ppermute(
            lax.slice_in_dim(block, block.shape[dim] - width, None, axis=dim), axis, forward
        )
        high = lax.ppermute(lax.slice_in_dim(block, 0, width, axis=dim), axis, backward)
        block = jnp.concatenate([low, block, high], axis=dim)
    return block


def depthwise(padded, taps, stride, height, breadth):
    kernel_size = taps.shape[0]
    accumulated = jnp.zeros((height, breadth, taps.shape[2]), jnp.float32)
    for row_tap in range(kernel_size):
        for col_tap in range(kernel_size):
            window = padded[
                row_tap * stride : row_tap * stride + height,
                col_tap * stride : col_tap * stride + breadth,
            ]
            accumulated = accumulated + taps[row_tap, col_tap] * window.astype(jnp.float32)
    return accumulated


def transposed(padded, taps, stride, margin, height, breadth):
    kernel_size = taps.shape[0]
    accumulated = jnp.zeros((height, breadth, taps.shape[2]), jnp.float32)
    for row_tap in range(kernel_size):
        for col_tap in range(kernel_size):
            row_start = 2 * margin - row_tap * stride
            col_start = 2 * margin - col_tap * stride
            window = padded[row_start : row_start + height, col_start : col_start + breadth]
            accumulated = accumulated + taps[row_tap, col_tap] * window.astype(jnp.float32)
    return accumulated


def tap_grads(gradient, padded, kernel_size, stride):
    height, breadth = (gradient.shape[0], gradient.shape[1])
    gradient_wide = gradient.astype(jnp.float32)
    outer = []
    for row_tap in range(kernel_size):
        inner = []
        for col_tap in range(kernel_size):
            window = padded[
                row_tap * stride : row_tap * stride + height,
                col_tap * stride : col_tap * stride + breadth,
            ]
            inner.append(jnp.sum(gradient_wide * window.astype(jnp.float32), axis=(0, 1)))
        outer.append(jnp.stack(inner))
    return jnp.stack(outer)


def unshuffle(field):
    height, breadth, chans = field.shape
    return (
        field.reshape(height // 2, 2, breadth // 2, 2, chans)
        .transpose(0, 2, 1, 3, 4)
        .reshape(height // 2, breadth // 2, 4 * chans)
    )


def reshuffle(field):
    height, breadth, wide = field.shape
    chans = wide // 4
    return (
        field.reshape(height, breadth, 2, 2, chans)
        .transpose(0, 2, 1, 3, 4)
        .reshape(2 * height, 2 * breadth, chans)
    )


def pixel_product(left, right):
    return lax.dot_general(
        left, right, (((0, 1), (0, 1)), ((), ())), preferred_element_type=jnp.float32
    )


def silu_slope(field):
    value = field.astype(jnp.float32)
    sigmoid = jax.nn.sigmoid(value)
    return sigmoid * (1.0 + value * (1.0 - sigmoid))


def shards(slide_pixels, taps_fine, mix_fine, reduce_weight, taps_coarse, mix_coarse, cotangent):
    zero_bf = jnp.zeros((), jnp.bfloat16)
    height, breadth = (slide_pixels.shape[0], slide_pixels.shape[1])
    half_height, half_breadth = (height // 2, breadth // 2)
    devices_all = lax.axis_size("segment") * lax.axis_size("tile")
    scale_fine = float(height * breadth * devices_all) ** (-0.5)
    scale_coarse = float(half_height * half_breadth * devices_all) ** (-0.5)
    relu_fine = jnp.maximum(slide_pixels, zero_bf)
    padded_fine = with_halo(relu_fine, (("segment", 0), ("tile", 1)), 1)
    depth_fine = depthwise(padded_fine, taps_fine, 1, height, breadth).astype(jnp.bfloat16)
    section_fine = (
        slide_pixels.astype(jnp.float32)
        + jnp.dot(depth_fine, mix_fine, preferred_element_type=jnp.float32)
    ).astype(jnp.bfloat16)
    pre_fine = unshuffle(section_fine)
    unshuffled = jax.nn.silu(pre_fine.astype(jnp.float32)).astype(jnp.bfloat16)
    reduced = jnp.dot(unshuffled, reduce_weight, preferred_element_type=jnp.float32).astype(
        jnp.bfloat16
    )
    act_coarse = jax.nn.silu(reduced.astype(jnp.float32)).astype(jnp.bfloat16)
    padded_coarse = with_halo(act_coarse, (("segment", 0), ("tile", 1)), 4)
    depth_coarse = depthwise(padded_coarse, taps_coarse, 2, half_height, half_breadth).astype(
        jnp.bfloat16
    )
    section_out = (
        reduced.astype(jnp.float32)
        + jnp.dot(depth_coarse, mix_coarse, preferred_element_type=jnp.float32)
    ).astype(jnp.bfloat16)
    term_mix_coarse = pixel_product(depth_coarse, cotangent)
    delta_coarse = jnp.dot(cotangent, mix_coarse.T, preferred_element_type=jnp.float32).astype(
        jnp.bfloat16
    )
    term_taps_coarse = tap_grads(delta_coarse, padded_coarse, 5, 2)
    delta_padded = with_halo(delta_coarse, (("segment", 0), ("tile", 1)), 4)
    back_coarse = transposed(delta_padded, taps_coarse, 2, 4, half_height, half_breadth).astype(
        jnp.bfloat16
    )
    delta_reduced = (
        cotangent.astype(jnp.float32) + back_coarse.astype(jnp.float32) * silu_slope(reduced)
    ).astype(jnp.bfloat16)
    term_reduce = pixel_product(unshuffled, delta_reduced)
    spread = jnp.dot(delta_reduced, reduce_weight.T, preferred_element_type=jnp.float32)
    delta_fine = reshuffle(spread * silu_slope(pre_fine)).astype(jnp.bfloat16)
    term_mix_fine = pixel_product(depth_fine, delta_fine)
    delta_depth = jnp.dot(delta_fine, mix_fine.T, preferred_element_type=jnp.float32).astype(
        jnp.bfloat16
    )
    term_taps_fine = tap_grads(delta_depth, padded_fine, 3, 1)
    padded_back = with_halo(delta_depth, (("segment", 0), ("tile", 1)), 1)
    back_fine = transposed(padded_back, taps_fine, 1, 1, height, breadth)
    pixel_grad = (
        delta_fine.astype(jnp.float32) + jnp.where(slide_pixels > 0, back_fine, 0.0)
    ).astype(jnp.bfloat16)
    term_taps_fine, term_mix_fine, term_reduce, term_taps_coarse, term_mix_coarse = lax.psum(
        (term_taps_fine, term_mix_fine, term_reduce, term_taps_coarse, term_mix_coarse),
        ("segment", "tile"),
    )
    return (
        section_out,
        pixel_grad,
        term_taps_fine * scale_fine,
        term_mix_fine * scale_fine,
        term_reduce * scale_coarse,
        term_taps_coarse * scale_coarse,
        term_mix_coarse * scale_coarse,
    )


def solution(mesh):
    return jax.shard_map(
        shards,
        mesh=mesh,
        in_specs=(P("segment", "tile", None), P(), P(), P(), P(), P(), P("segment", "tile", None)),
        out_specs=(P("segment", "tile", None), P("segment", "tile", None), P(), P(), P(), P(), P()),
        check_vma=False,
    )
```

profile of v0, /device:TPU:1, one launch (start us, length us, event | category | flops | bytes accessed | tf_op | source)
XLA Modules:
  0.0 489.0 jit_solution(179755665181385385)
XLA Ops:
  7.2 1.4 broadcast_maximum_fusion
  8.6 4.6 collective-permute-start
  13.2 1.9 collective-permute-start.1
  15.2 3.3 collective-permute-done.1
  18.5 3.5 collective-permute-start.2
  22.1 1.3 collective-permute-start.3
  23.5 3.4 collective-permute-done.3
  26.9 0.6 maximum_maximum_fusion
  27.6 2.8 fusion.8
  30.5 1.0 copy-done.12
  31.5 1.8 fusion.26
  33.3 2.5 reshape.25
  35.8 2.1 copy.14
  37.9 4.0 reshape.24
  41.9 1.6 fusion.55
  43.6 3.3 collective-permute-start.4
  46.9 1.9 collective-permute-start.5
  48.8 0.7 fusion.115
  49.5 3.7 collective-permute-done.5
  53.3 3.5 collective-permute-start.6
  56.8 1.5 collective-permute-start.7
  58.3 0.6 fusion.116
  58.9 4.6 collective-permute-done.7
  64.0 2.4 fusion.95
  66.4 0.7 fusion.113
  67.1 1.8 fusion.98
  69.0 1.1 fusion.96
  70.1 0.7 stack.177
  70.8 0.6 bitcast_dynamic-update-slice_fusion.4
  71.4 2.9 collective-permute-start.8
  74.3 2.0 collective-permute-start.9
  76.4 5.6 %fusion.100 = bf16[16,32,416]{2,1,0:T(8,128)(2,1)S(1)} fusion(bf16[16,32,416]{2,1,0:T(8,128)(2,1)} %copy-done.6, bf16[4,32,416]{2,1,0:T(8,128)(2,1)S(1)} %collective-permute-done.5, bf16[4,32,416]{2,1,0:T(8,128)(2,1)S(1)} %collective-permute-done.4, f32[416]{0:T(512)} %bitcast.171, f32[416]{0:T(512)} %bitcast.173, f32[416]{0:T(512)S(1)} %bitcast.127, ...), kind=kLoop, calls=%fused_computation.192 | loop fusion | flops 16826368 | bytes 9626240 | tf_op jit(solution)/shard_map/convert_element_type | solution.py:113
  82.1 1.3 convolution_bitcast_fusion.1
  83.5 1.2 fusion.27
  85.1 0.7 stack.191
  85.8 0.7 stack.198
  86.6 0.7 stack.205
  87.3 0.9 pad_maximum_fusion.14
  88.2 1.3 collective-permute-start.10
  89.5 5.7 %collective-permute-start.11 = (bf16[24,4,416]{2,1,0:T(4,128)(2,1)S(1)}, bf16[24,4,416]{2,1,0:T(4,128)(2,1)S(1)}, u32[]{:S(2)}, u32[]{:S(2)}) collective-permute-start(bf16[24,4,416]{2,1,0:T(4,128)(2,1)S(1)} %get-tuple-element.68), channel_id=1, source_target_pairs={{0,1},{1,2},{2,3},{3,4},{4,5},{5,6},{6,7},{7,8},{8,9},{9,10},{10,1... | collective-permute-start | bytes 239624 | tf_op jit(solution)/shard_map/ppermute | solution.py:12
  95.7 1.8 collective-permute-done.11
  97.5 1.6 pad_maximum_fusion.7
  99.3 5.5 %fusion.60 = bf16[16,32,416]{2,1,0:T(8,128)(2,1)S(1)} fusion(bf16[16,32,416]{2,1,0:T(8,128)(2,1)S(1)} %copy-done.13, bf16[16,32,416]{2,1,0:T(8,128)(2,1)S(1)} %copy-done.19, bf16[24,36,416]{2,1,0:T(8,128)(2,1)S(1)} %get-tuple-element.66, f32[416]{0:T(512)S(1)} %bitcast.172, f32[416]{0:T(512)S(1)} %bitcast.174, ...), kind=kLoop, calls=%fused_computation.148 | loop fusion | flops 19595264 | bytes 10478208 | tf_op jit(solution)/shard_map/convert_element_type | solution.py:131
  104.8 0.9 multiply_convert_fusion
  105.8 1.9 convolution_bitcast_fusion
  107.7 1.0 convert_element_type.396
  108.6 2.0 copy.15
  110.7 3.0 convert_element_type.398
  113.6 2.7 convolution_bitcast_fusion.2
  116.3 5.7 %fusion.17 = (f32[208]{0:T(256)S(1)}, f32[208]{0:T(256)S(1)}, f32[208]{0:T(256)S(1)}, f32[208]{0:T(256)S(1)}, f32[208]{0:T(256)S(1)}, /*index=5*/f32[208]{0:T(25...) fusion(bf16[34,65,208]{2,1,0:T(8,128)(2,1)S(1)} %copy-done.4, ...), kind=kOutput, calls=%fused_computation.62 | convolution fusion | flops 190838960 | bytes 8666944 | tf_op jit(solution)/shard_map/dot_general | solution.py:136
  122.1 1.0 copy-done.7
  123.1 3.7 collective-permute-start.12
  126.7 1.9 collective-permute-start.13
  128.7 89.9 %all-reduce = (f32[3,3,208]{2,1,0:T(4,128)S(1)}, f32[5,5,416]{2,1,0:T(8,128)S(1)}) all-reduce(f32[3,3,208]{2,1,0:T(4,128)S(1)} %pad_maximum_fusion.24, f32[5,5,416]{2,1,0:T(8,128)S(1)} %bitcast_dynamic-update-slice_fusion), channel_id=1, replica_groups=mesh['segment'=4,'tile'=64] {'segment','tile'}, use_global_device_ids=true, to_apply=%region_9.10 | all-reduce | flops 12272 | bytes 98176 | tf_op jit(solution)/shard_map/psum | solution.py:145
  218.6 0.6 broadcast_multiply_fusion.3
  219.5 1.4 collective-permute-start.14
  220.9 4.6 collective-permute-start.15
  225.5 0.6 broadcast_multiply_fusion.4
  226.3 0.6 pad_maximum_fusion.1
  227.0 4.0 fusion.16
  231.0 246.1 %all-reduce.4.cloned.1.call-done = (f32[208,208]{1,0:T(8,128)}, f32[832,416]{0,1:T(8,128)}, f32[416,416]{1,0:T(8,128)}) async-done(((f32[208,208]{1,0:T(8,128)}, f32[832,416]{0,1:T(8,128)}, f32[416,416]{1,0:T(8,128)}), (f32[208,208]{1,0:T(8,128)}, f32[832,416]{0,1:T(8,128)}, f32[416,416]{1,0:T(8,128)})) %all-reduce.4.cloned.1.call-update) | async-done | bytes 2249744 | tf_op jit(solution)/shard_map/psum | solution.py:145
  477.0 1.7 broadcast_multiply_fusion.2
  478.8 2.1 broadcast_multiply_fusion.1
  480.9 1.2 broadcast_multiply_fusion
  (197 shorter events, 1.9 us)
Async XLA Ops:
  7.2 34.7 %copy-start = (bf16[832,416]{0,1:T(8,128)(2,1)S(1)}, bf16[832,416]{0,1:T(8,128)(2,1)}, u32[]{:S(2)}) copy-start(bf16[832,416]{0,1:T(8,128)(2,1)} %param.10) | copy-start | bytes 2076676
  7.2 16.2 %copy-start.81 = (f32[3,3,208]{2,1,0:T(4,128)S(1)}, f32[3,3,208]{2,1,0:T(4,128)}, u32[]{:S(2)}) copy-start(f32[3,3,208]{2,1,0:T(4,128)} %param.8) | copy-start | bytes 22468
  7.2 469.9 %all-reduce.4.cloned.1.call-start = ((), (), s32[]{:S(2)}) async-start(), calls=%async_computation | async-start | bytes 5111808 | tf_op jit(solution)/shard_map/psum | solution.py:145
  8.6 18.9 %copy-start.1 = (bf16[32,64,208]{2,1,0:T(8,128)(2,1)}, bf16[32,64,208]{2,1,0:T(8,128)(2,1)S(1)}, u32[]{:S(2)}) copy-start(bf16[32,64,208]{2,1,0:T(8,128)(2,1)S(1)} %broadcast_maximum_fusion) | copy-start | bytes 2555908
  8.6 6.5 %collective-permute-start = (bf16[1,64,208]{2,1,0:T(8,128)(2,1)S(1)}, bf16[1,64,208]{2,1,0:T(8,128)(2,1)S(1)}, u32[]{:S(2)}, u32[]{:S(2)}) collective-permute-start(bf16[1,64,208]{2,1,0:T(8,128)(2,1)S(1)} %get-tuple-element.63), channel_id=1, source_target_pairs={{0,64},{64,128},{128,192},{1,65},{65,129},{129,193},{2,66},{66,130... | collective-permute-start | bytes 79880 | tf_op jit(solution)/shard_map/ppermute | solution.py:12
  13.2 5.2 %collective-permute-start.1 = (bf16[1,64,208]{2,1,0:T(8,128)(2,1)S(1)}, bf16[1,64,208]{2,1,0:T(8,128)(2,1)S(1)}, u32[]{:S(2)}, u32[]{:S(2)}) collective-permute-start(bf16[1,64,208]{2,1,0:T(8,128)(2,1)S(1)} %get-tuple-element.64), channel_id=1, source_target_pairs={{64,0},{128,64},{192,128},{65,1},{129,65},{193,129},{66,2},{130,66... | collective-permute-start | bytes 79880 | tf_op jit(solution)/shard_map/ppermute | solution.py:15
  18.5 9.1 %copy-start.22 = (bf16[1,64,208]{2,1,0:T(8,128)(2,1)}, bf16[1,64,208]{2,1,0:T(8,128)(2,1)S(1)}, u32[]{:S(2)}) copy-start(bf16[1,64,208]{2,1,0:T(8,128)(2,1)S(1)} %collective-permute-done.1) | copy-start | bytes 79876
  18.5 5.0 %collective-permute-start.2 = (bf16[34,1,208]{2,1,0:T(2,128)(2,1)S(1)}, bf16[34,1,208]{2,1,0:T(2,128)(2,1)S(1)}, u32[]{:S(2)}, u32[]{:S(2)}) collective-permute-start(bf16[34,1,208]{2,1,0:T(2,128)(2,1)S(1)} %get-tuple-element.59), channel_id=1, source_target_pairs={{0,1},{1,2},{2,3},{3,4},{4,5},{5,6},{6,7},{7,8},{8,9},{9,10},{10,1... | collective-permute-start | bytes 42440 | tf_op jit(solution)/shard_map/ppermute | solution.py:12
  22.1 4.9 collective-permute-start.3
  23.4 7.0 %copy-start.51 = (f32[1,1,208]{2,1,0:T(1,128)}, f32[1,1,208]{2,1,0:T(1,128)S(1)}, u32[]{:S(2)}) copy-start(f32[1,1,208]{2,1,0:T(1,128)S(1)} %get-tuple-element.102) | copy-start | bytes 2500
  23.4 7.0 %copy-start.53 = (f32[1,1,208]{2,1,0:T(1,128)}, f32[1,1,208]{2,1,0:T(1,128)S(1)}, u32[]{:S(2)}) copy-start(f32[1,1,208]{2,1,0:T(1,128)S(1)} %get-tuple-element.103) | copy-start | bytes 2500
  23.4 7.0 %copy-start.55 = (f32[1,1,208]{2,1,0:T(1,128)}, f32[1,1,208]{2,1,0:T(1,128)S(1)}, u32[]{:S(2)}) copy-start(f32[1,1,208]{2,1,0:T(1,128)S(1)} %get-tuple-element.104) | copy-start | bytes 2500
  23.4 7.0 %copy-start.57 = (f32[1,1,208]{2,1,0:T(1,128)}, f32[1,1,208]{2,1,0:T(1,128)S(1)}, u32[]{:S(2)}) copy-start(f32[1,1,208]{2,1,0:T(1,128)S(1)} %get-tuple-element.105) | copy-start | bytes 2500
  43.5 25.4 %copy-start.6 = (bf16[16,32,416]{2,1,0:T(8,128)(2,1)}, bf16[16,32,416]{2,1,0:T(8,128)(2,1)S(1)}, u32[]{:S(2)}) copy-start(bf16[16,32,416]{2,1,0:T(8,128)(2,1)S(1)} %get-tuple-element.111) | copy-start | bytes 1277956
  43.6 20.5 %copy-start.17 = (bf16[16,32,416]{2,1,0:T(8,128)(2,1)S(1)}, bf16[16,32,416]{2,1,0:T(8,128)(2,1)}, u32[]{:S(2)}) copy-start(bf16[16,32,416]{2,1,0:T(8,128)(2,1)} %param.13) | copy-start | bytes 1277956
  43.6 20.5 %copy-start.20 = (bf16[416,416]{1,0:T(8,128)(2,1)S(1)}, bf16[416,416]{1,0:T(8,128)(2,1)}, u32[]{:S(2)}) copy-start(bf16[416,416]{1,0:T(8,128)(2,1)} %param.12) | copy-start | bytes 1038340
  43.6 5.9 %collective-permute-start.4 = (bf16[4,32,416]{2,1,0:T(8,128)(2,1)S(1)}, bf16[4,32,416]{2,1,0:T(8,128)(2,1)S(1)}, u32[]{:S(2)}, u32[]{:S(2)}) collective-permute-start(bf16[4,32,416]{2,1,0:T(8,128)(2,1)S(1)} %get-tuple-element.75), channel_id=1, source_target_pairs={{0,64},{64,128},{128,192},{1,65},{65,129},{129,193},{2,66},{66,130... | collective-permute-start | bytes 319496 | tf_op jit(solution)/shard_map/ppermute | solution.py:12
  46.9 6.3 %collective-permute-start.5 = (bf16[4,32,416]{2,1,0:T(8,128)(2,1)S(1)}, bf16[4,32,416]{2,1,0:T(8,128)(2,1)S(1)}, u32[]{:S(2)}, u32[]{:S(2)}) collective-permute-start(bf16[4,32,416]{2,1,0:T(8,128)(2,1)S(1)} %get-tuple-element.76), channel_id=1, source_target_pairs={{64,0},{128,64},{192,128},{65,1},{129,65},{193,129},{66,2},{130,66... | collective-permute-start | bytes 319496 | tf_op jit(solution)/shard_map/ppermute | solution.py:15
  53.3 5.6 %collective-permute-start.6 = (bf16[24,4,416]{2,1,0:T(4,128)(2,1)S(1)}, bf16[24,4,416]{2,1,0:T(4,128)(2,1)S(1)}, u32[]{:S(2)}, u32[]{:S(2)}) collective-permute-start(bf16[24,4,416]{2,1,0:T(4,128)(2,1)S(1)} %get-tuple-element.71), channel_id=1, source_target_pairs={{0,1},{1,2},{2,3},{3,4},{4,5},{5,6},{6,7},{7,8},{8,9},{9,10},{10,1... | collective-permute-start | bytes 239624 | tf_op jit(solution)/shard_map/ppermute | solution.py:12
  56.8 6.7 %collective-permute-start.7 = (bf16[24,4,416]{2,1,0:T(4,128)(2,1)S(1)}, bf16[24,4,416]{2,1,0:T(4,128)(2,1)S(1)}, u32[]{:S(2)}, u32[]{:S(2)}) collective-permute-start(bf16[24,4,416]{2,1,0:T(4,128)(2,1)S(1)} %get-tuple-element.72), channel_id=1, source_target_pairs={{1,0},{2,1},{3,2},{4,3},{5,4},{6,5},{7,6},{8,7},{9,8},{10,9},{11,1... | collective-permute-start | bytes 239624 | tf_op jit(solution)/shard_map/ppermute | solution.py:15
  71.4 15.9 %collective-permute-start.8 = (bf16[4,32,416]{2,1,0:T(8,128)(2,1)}, bf16[4,32,416]{2,1,0:T(8,128)(2,1)}, u32[]{:S(2)}, u32[]{:S(2)}) collective-permute-start(bf16[4,32,416]{2,1,0:T(8,128)(2,1)} %get-tuple-element.73), channel_id=1, source_target_pairs={{0,64},{64,128},{128,192},{1,65},{65,129},{129,193},{2,66},{66,130... | collective-permute-start | bytes 319496 | tf_op jit(solution)/shard_map/ppermute | solution.py:12
  74.3 13.0 %collective-permute-start.9 = (bf16[4,32,416]{2,1,0:T(8,128)(2,1)}, bf16[4,32,416]{2,1,0:T(8,128)(2,1)}, u32[]{:S(2)}, u32[]{:S(2)}) collective-permute-start(bf16[4,32,416]{2,1,0:T(8,128)(2,1)} %get-tuple-element.74), channel_id=1, source_target_pairs={{64,0},{128,64},{192,128},{65,1},{129,65},{193,129},{66,2},{130,66... | collective-permute-start | bytes 319496 | tf_op jit(solution)/shard_map/ppermute | solution.py:15
  84.8 14.2 %copy-start.19 = (bf16[16,32,416]{2,1,0:T(8,128)(2,1)S(1)}, bf16[16,32,416]{2,1,0:T(8,128)(2,1)}, u32[]{:S(2)}) copy-start(bf16[16,32,416]{2,1,0:T(8,128)(2,1)} %param.13) | copy-start | bytes 1277956
  84.8 14.2 %copy-start.28 = (f32[1,1,416]{2,1,0:T(1,128)S(1)}, f32[1,1,416]{2,1,0:T(1,128)}, u32[]{:S(2)}) copy-start(f32[1,1,416]{2,1,0:T(1,128)} %get-tuple-element.79) | copy-start | bytes 4996
  84.8 14.2 %copy-start.29 = (f32[1,1,416]{2,1,0:T(1,128)S(1)}, f32[1,1,416]{2,1,0:T(1,128)}, u32[]{:S(2)}) copy-start(f32[1,1,416]{2,1,0:T(1,128)} %get-tuple-element.80) | copy-start | bytes 4996
  84.9 14.2 %copy-start.30 = (f32[1,1,416]{2,1,0:T(1,128)S(1)}, f32[1,1,416]{2,1,0:T(1,128)}, u32[]{:S(2)}) copy-start(f32[1,1,416]{2,1,0:T(1,128)} %get-tuple-element.81) | copy-start | bytes 4996
  84.9 14.2 %copy-start.31 = (f32[1,1,416]{2,1,0:T(1,128)S(1)}, f32[1,1,416]{2,1,0:T(1,128)}, u32[]{:S(2)}) copy-start(f32[1,1,416]{2,1,0:T(1,128)} %get-tuple-element.82) | copy-start | bytes 4996
  84.9 14.2 %copy-start.32 = (f32[1,1,416]{2,1,0:T(1,128)S(1)}, f32[1,1,416]{2,1,0:T(1,128)}, u32[]{:S(2)}) copy-start(f32[1,1,416]{2,1,0:T(1,128)} %get-tuple-element.83) | copy-start | bytes 4996
  84.9 14.2 %copy-start.33 = (f32[1,1,416]{2,1,0:T(1,128)S(1)}, f32[1,1,416]{2,1,0:T(1,128)}, u32[]{:S(2)}) copy-start(f32[1,1,416]{2,1,0:T(1,128)} %get-tuple-element.84) | copy-start | bytes 4996
  84.9 14.2 %copy-start.34 = (f32[1,1,416]{2,1,0:T(1,128)S(1)}, f32[1,1,416]{2,1,0:T(1,128)}, u32[]{:S(2)}) copy-start(f32[1,1,416]{2,1,0:T(1,128)} %get-tuple-element.85) | copy-start | bytes 4996
  84.9 14.2 %copy-start.35 = (f32[1,1,416]{2,1,0:T(1,128)S(1)}, f32[1,1,416]{2,1,0:T(1,128)}, u32[]{:S(2)}) copy-start(f32[1,1,416]{2,1,0:T(1,128)} %get-tuple-element.86) | copy-start | bytes 4996
  84.9 14.2 %copy-start.36 = (f32[1,1,416]{2,1,0:T(1,128)S(1)}, f32[1,1,416]{2,1,0:T(1,128)}, u32[]{:S(2)}) copy-start(f32[1,1,416]{2,1,0:T(1,128)} %get-tuple-element.87) | copy-start | bytes 4996
  84.9 14.2 %copy-start.37 = (f32[1,1,416]{2,1,0:T(1,128)S(1)}, f32[1,1,416]{2,1,0:T(1,128)}, u32[]{:S(2)}) copy-start(f32[1,1,416]{2,1,0:T(1,128)} %get-tuple-element.88) | copy-start | bytes 4996
  84.9 14.2 %copy-start.38 = (f32[1,1,416]{2,1,0:T(1,128)S(1)}, f32[1,1,416]{2,1,0:T(1,128)}, u32[]{:S(2)}) copy-start(f32[1,1,416]{2,1,0:T(1,128)} %get-tuple-element.89) | copy-start | bytes 4996
  84.9 14.2 %copy-start.39 = (f32[1,1,416]{2,1,0:T(1,128)S(1)}, f32[1,1,416]{2,1,0:T(1,128)}, u32[]{:S(2)}) copy-start(f32[1,1,416]{2,1,0:T(1,128)} %get-tuple-element.90) | copy-start | bytes 4996
  85.0 14.2 %copy-start.40 = (f32[1,1,416]{2,1,0:T(1,128)S(1)}, f32[1,1,416]{2,1,0:T(1,128)}, u32[]{:S(2)}) copy-start(f32[1,1,416]{2,1,0:T(1,128)} %get-tuple-element.91) | copy-start | bytes 4996
  85.0 14.2 %copy-start.41 = (f32[1,1,416]{2,1,0:T(1,128)S(1)}, f32[1,1,416]{2,1,0:T(1,128)}, u32[]{:S(2)}) copy-start(f32[1,1,416]{2,1,0:T(1,128)} %get-tuple-element.92) | copy-start | bytes 4996
  85.0 14.2 %copy-start.42 = (f32[1,1,416]{2,1,0:T(1,128)S(1)}, f32[1,1,416]{2,1,0:T(1,128)}, u32[]{:S(2)}) copy-start(f32[1,1,416]{2,1,0:T(1,128)} %get-tuple-element.93) | copy-start | bytes 4996
  85.0 14.2 %copy-start.43 = (f32[1,1,416]{2,1,0:T(1,128)S(1)}, f32[1,1,416]{2,1,0:T(1,128)}, u32[]{:S(2)}) copy-start(f32[1,1,416]{2,1,0:T(1,128)} %get-tuple-element.94) | copy-start | bytes 4996
  85.0 14.2 %copy-start.44 = (f32[1,1,416]{2,1,0:T(1,128)S(1)}, f32[1,1,416]{2,1,0:T(1,128)}, u32[]{:S(2)}) copy-start(f32[1,1,416]{2,1,0:T(1,128)} %get-tuple-element.95) | copy-start | bytes 4996
  85.0 14.2 %copy-start.45 = (f32[1,1,416]{2,1,0:T(1,128)S(1)}, f32[1,1,416]{2,1,0:T(1,128)}, u32[]{:S(2)}) copy-start(f32[1,1,416]{2,1,0:T(1,128)} %get-tuple-element.96) | copy-start | bytes 4996
  85.0 14.2 %copy-start.46 = (f32[1,1,416]{2,1,0:T(1,128)S(1)}, f32[1,1,416]{2,1,0:T(1,128)}, u32[]{:S(2)}) copy-start(f32[1,1,416]{2,1,0:T(1,128)} %get-tuple-element.97) | copy-start | bytes 4996
  85.0 14.2 %copy-start.47 = (f32[1,1,416]{2,1,0:T(1,128)S(1)}, f32[1,1,416]{2,1,0:T(1,128)}, u32[]{:S(2)}) copy-start(f32[1,1,416]{2,1,0:T(1,128)} %get-tuple-element.98) | copy-start | bytes 4996
  85.0 14.2 %copy-start.48 = (f32[1,1,416]{2,1,0:T(1,128)S(1)}, f32[1,1,416]{2,1,0:T(1,128)}, u32[]{:S(2)}) copy-start(f32[1,1,416]{2,1,0:T(1,128)} %get-tuple-element.99) | copy-start | bytes 4996
  85.0 14.2 %copy-start.49 = (f32[1,1,416]{2,1,0:T(1,128)S(1)}, f32[1,1,416]{2,1,0:T(1,128)}, u32[]{:S(2)}) copy-start(f32[1,1,416]{2,1,0:T(1,128)} %get-tuple-element.100) | copy-start | bytes 4996
  85.1 14.2 %copy-start.50 = (f32[1,1,416]{2,1,0:T(1,128)S(1)}, f32[1,1,416]{2,1,0:T(1,128)}, u32[]{:S(2)}) copy-start(f32[1,1,416]{2,1,0:T(1,128)} %get-tuple-element.101) | copy-start | bytes 4996
  88.2 7.5 %collective-permute-start.10 = (bf16[24,4,416]{2,1,0:T(4,128)(2,1)S(1)}, bf16[24,4,416]{2,1,0:T(4,128)(2,1)S(1)}, u32[]{:S(2)}, u32[]{:S(2)}) collective-permute-start(bf16[24,4,416]{2,1,0:T(4,128)(2,1)S(1)} %get-tuple-element.67), channel_id=1, source_target_pairs={{1,0},{2,1},{3,2},{4,3},{5,4},{6,5},{7,6},{8,7},{9,8},{10,9},{11,1... | collective-permute-start | bytes 239624 | tf_op jit(solution)/shard_map/ppermute | solution.py:15
  89.5 8.0 %collective-permute-start.11 = (bf16[24,4,416]{2,1,0:T(4,128)(2,1)S(1)}, bf16[24,4,416]{2,1,0:T(4,128)(2,1)S(1)}, u32[]{:S(2)}, u32[]{:S(2)}) collective-permute-start(bf16[24,4,416]{2,1,0:T(4,128)(2,1)S(1)} %get-tuple-element.68), channel_id=1, source_target_pairs={{0,1},{1,2},{2,3},{3,4},{4,5},{5,6},{6,7},{7,8},{8,9},{9,10},{10,1... | collective-permute-start | bytes 239624 | tf_op jit(solution)/shard_map/ppermute | solution.py:12
  123.1 96.2 %copy-start.8 = (bf16[32,64,208]{2,1,0:T(8,128)(2,1)S(1)}, bf16[32,64,208]{2,1,0:T(8,128)(2,1)}, u32[]{:S(2)}) copy-start(bf16[32,64,208]{2,1,0:T(8,128)(2,1)} %copy-done.7) | copy-start | bytes 2555908
  123.1 96.2 %collective-permute-start.12 = (bf16[1,64,208]{2,1,0:T(8,128)(2,1)S(1)}, bf16[1,64,208]{2,1,0:T(8,128)(2,1)S(1)}, u32[]{:S(2)}, u32[]{:S(2)}) collective-permute-start(bf16[1,64,208]{2,1,0:T(8,128)(2,1)S(1)} %get-tuple-element.61), channel_id=1, source_target_pairs={{0,64},{64,128},{128,192},{1,65},{65,129},{129,193},{2,66},{66,130... | collective-permute-start | bytes 79880 | tf_op jit(solution)/shard_map/ppermute | solution.py:12
  126.7 92.6 %collective-permute-start.13 = (bf16[1,64,208]{2,1,0:T(8,128)(2,1)S(1)}, bf16[1,64,208]{2,1,0:T(8,128)(2,1)S(1)}, u32[]{:S(2)}, u32[]{:S(2)}) collective-permute-start(bf16[1,64,208]{2,1,0:T(8,128)(2,1)S(1)} %get-tuple-element.62), channel_id=1, source_target_pairs={{64,0},{128,64},{192,128},{65,1},{129,65},{193,129},{66,2},{130,66... | collective-permute-start | bytes 79880 | tf_op jit(solution)/shard_map/ppermute | solution.py:15
  219.4 7.5 %copy-start.9 = (bf16[32,64,208]{2,1,0:T(8,128)(2,1)S(1)}, bf16[32,64,208]{2,1,0:T(8,128)(2,1)}, u32[]{:S(2)}) copy-start(bf16[32,64,208]{2,1,0:T(8,128)(2,1)} %convert_element_type.398) | copy-start | bytes 2555908
  219.4 7.5 %copy-start.11 = (bf16[32,64,208]{2,1,0:T(8,128)(2,1)S(1)}, bf16[32,64,208]{2,1,0:T(8,128)(2,1)}, u32[]{:S(2)}) copy-start(bf16[32,64,208]{2,1,0:T(8,128)(2,1)} %param.7) | copy-start | bytes 2555908
  219.4 7.5 %copy-start.52 = (f32[1,1,208]{2,1,0:T(1,128)S(1)}, f32[1,1,208]{2,1,0:T(1,128)}, u32[]{:S(2)}) copy-start(f32[1,1,208]{2,1,0:T(1,128)} %copy-done.51) | copy-start | bytes 2500
  219.4 7.5 %copy-start.54 = (f32[1,1,208]{2,1,0:T(1,128)S(1)}, f32[1,1,208]{2,1,0:T(1,128)}, u32[]{:S(2)}) copy-start(f32[1,1,208]{2,1,0:T(1,128)} %copy-done.53) | copy-start | bytes 2500
  219.4 7.5 %copy-start.56 = (f32[1,1,208]{2,1,0:T(1,128)S(1)}, f32[1,1,208]{2,1,0:T(1,128)}, u32[]{:S(2)}) copy-start(f32[1,1,208]{2,1,0:T(1,128)} %copy-done.55) | copy-start | bytes 2500
  219.4 7.5 %copy-start.58 = (f32[1,1,208]{2,1,0:T(1,128)S(1)}, f32[1,1,208]{2,1,0:T(1,128)}, u32[]{:S(2)}) copy-start(f32[1,1,208]{2,1,0:T(1,128)} %copy-done.57) | copy-start | bytes 2500
  219.5 7.5 %copy-start.60 = (f32[1,1,208]{2,1,0:T(1,128)S(1)}, f32[1,1,208]{2,1,0:T(1,128)}, u32[]{:S(2)}) copy-start(f32[1,1,208]{2,1,0:T(1,128)} %copy-done.59) | copy-start | bytes 2500
  219.5 7.5 %copy-start.62 = (f32[1,1,208]{2,1,0:T(1,128)S(1)}, f32[1,1,208]{2,1,0:T(1,128)}, u32[]{:S(2)}) copy-start(f32[1,1,208]{2,1,0:T(1,128)} %copy-done.61) | copy-start | bytes 2500
  219.5 7.5 %copy-start.64 = (f32[1,1,208]{2,1,0:T(1,128)S(1)}, f32[1,1,208]{2,1,0:T(1,128)}, u32[]{:S(2)}) copy-start(f32[1,1,208]{2,1,0:T(1,128)} %copy-done.63) | copy-start | bytes 2500
  219.5 7.5 %copy-start.66 = (f32[1,1,208]{2,1,0:T(1,128)S(1)}, f32[1,1,208]{2,1,0:T(1,128)}, u32[]{:S(2)}) copy-start(f32[1,1,208]{2,1,0:T(1,128)} %copy-done.65) | copy-start | bytes 2500
  219.5 7.5 %copy-start.68 = (f32[1,1,208]{2,1,0:T(1,128)S(1)}, f32[1,1,208]{2,1,0:T(1,128)}, u32[]{:S(2)}) copy-start(f32[1,1,208]{2,1,0:T(1,128)} %copy-done.67) | copy-start | bytes 2500
  219.5 6.6 %collective-permute-start.14 = (bf16[34,1,208]{2,1,0:T(2,128)(2,1)S(1)}, bf16[34,1,208]{2,1,0:T(2,128)(2,1)S(1)}, u32[]{:S(2)}, u32[]{:S(2)}) collective-permute-start(bf16[34,1,208]{2,1,0:T(2,128)(2,1)S(1)} %get-tuple-element.55), channel_id=1, source_target_pairs={{1,0},{2,1},{3,2},{4,3},{5,4},{6,5},{7,6},{8,7},{9,8},{10,9},{11,1... | collective-permute-start | bytes 42440 | tf_op jit(solution)/shard_map/ppermute | solution.py:15
  220.9 5.3 %collective-permute-start.15 = (bf16[34,1,208]{2,1,0:T(2,128)(2,1)S(1)}, bf16[34,1,208]{2,1,0:T(2,128)(2,1)S(1)}, u32[]{:S(2)}, u32[]{:S(2)}) collective-permute-start(bf16[34,1,208]{2,1,0:T(2,128)(2,1)S(1)} %get-tuple-element.56), channel_id=1, source_target_pairs={{0,1},{1,2},{2,3},{3,4},{4,5},{5,6},{6,7},{7,8},{8,9},{9,10},{10,1... | collective-permute-start | bytes 42440 | tf_op jit(solution)/shard_map/ppermute | solution.py:12
  (38 other events, 140.6 us)
Sparse Core Ops, SparseCore 0:
  219.4 257.5 all-reduce.3
where the time goes:
time: 491 us; the launch traced here: 489 us
  waiting for transfers between devices  263 us (54%)
  blocking collectives  89.9 us (18%)
  starting transfers between devices  45.2 us (9%)
  other arithmetic  33 us (7%)
  local copies, waits for them, and re-layouts  22.4 us (5%)
  matrix products  19.5 us (4%)
  between operations  15.6 us (3%)
    psum x1, waiting for transfers between devices, shards(): lax.psum((term_taps_fine, term_mix_fine, term_reduce, term_taps_coarse, t...  246 us
    psum x1, blocking collectives, shards(): lax.psum((term_taps_fine, term_mix_fine, term_reduce, term_taps_coarse, t...  89.9 us
    ppermute x8, starting transfers between devices, with_halo(): lax.ppermute(lax.slice_in_dim(block, block.shape[dim] - width, None, axis...  31.9 us
    ppermute x8, waiting for transfers between devices, with_halo(): lax.ppermute(lax.slice_in_dim(block, 0, width, axis=dim), axis, backward)  15.4 us
    ppermute x8, starting transfers between devices, with_halo(): lax.ppermute(lax.slice_in_dim(block, 0, width, axis=dim), axis, backward)  13.3 us
  transfers between devices with their start and end apart: 17, of which 8 were waited for; matrix products, arithmetic and copies ran while one was open for 4% of the time, Pallas kernels for 0%

commit v1 on v0

v1 whole, which is shorter than its diff:
```python
import functools

import jax
import jax.numpy as jnp
from jax import lax
from jax.experimental import pallas as pl
from jax.experimental.pallas import tpu as pltpu
from jax.sharding import Mesh, PartitionSpec as P

ROWS = ("yl", "core")
COLS = ("x", "yh", "z")
PLANE = ("yl", "x", "yh")
BF = jnp.bfloat16
F4 = jnp.float32
LIMIT = 56 * 1024 * 1024
RED, MIXC, MIXF, TAPC, TAPF, TOTAL = 0, 832, 1248, 1456, 1488, 1536
SOURCE = ((2, 0, 1), (0, 1, 3))


def dot(left, right):
    return jnp.dot(left, right, preferred_element_type=F4)


def dot_nt(left, right):
    return lax.dot_general(left, right, (((1,), (1,)), ((), ())), preferred_element_type=F4)


def dot_tn(left, right):
    return lax.dot_general(left, right, (((0,), (0,)), ((), ())), preferred_element_type=F4)


def picker(rows, columns, source):
    row = lax.broadcasted_iota(jnp.int32, (rows, columns), 0)
    column = lax.broadcasted_iota(jnp.int32, (rows, columns), 1)
    return jnp.where(column == source(row), 1.0, 0.0).astype(BF)


def fine_source(row):
    kind, m = row // 32, row % 32
    even, odd = 2 * m, 2 * m + 1
    before = jnp.where(m == 0, 64, 2 * m - 1)
    after = jnp.where(m == 31, 65, 2 * m + 2)
    return jnp.where(kind == 0, even, jnp.where(kind == 1, odd, jnp.where(kind == 2, before, after)))


def phase_source(row):
    kind, m = row // 32, row % 32
    before = jnp.where(m == 0, 64, 32 + m - 1)
    after = jnp.where(m == 31, 65, m + 1)
    return jnp.where(kind == 0, before, after)


def weave_source(row):
    return jnp.where(row % 2 == 0, row // 2, 32 + row // 2)


def coarse_source(row):
    shift, m = row // 32, row % 32
    at = m + 2 * shift - 4
    return jnp.where(at < 0, 36 + at, jnp.where(at > 31, 4 + at, at))


def sigmoid(value):
    return 1.0 / (1.0 + jnp.exp(-value))


def fine_rows(slide_ref, top_ref, bottom_ref, lr_ref, shifted, keep=None):
    pick = picker(128, 80, fine_source)

    def put(r, row):
        got = dot(pick, jnp.concatenate([row, lr_ref[r]], axis=0))
        shifted[:, r] = jnp.maximum(got, 0.0).reshape(4, 32, got.shape[1])
        return got

    put(0, top_ref[0])
    put(33, bottom_ref[0])

    def step(i, carry):
        for p in range(2):
            got = put(2 * i + p + 1, slide_ref[2 * i + p])
            if keep is not None:
                keep[2 * p, i] = got[:32].astype(BF)
                keep[2 * p + 1, i] = got[32:64].astype(BF)
        return carry

    lax.fori_loop(0, 16, step, 0)


def fine_conv(i, shifted, taps_ref, flip, put):
    for p in range(2):
        for q in range(2):
            total = None
            for a in range(3):
                for b in range(3):
                    u, v = (2 - a, 2 - b) if flip else (a, b)
                    term = taps_ref[u, v : v + 1, :] * shifted[SOURCE[q][b], 2 * i + p + a]
                    total = term if total is None else total + term
            put(2 * p + q, total)


def fine_forward(
    slide_ref, top_ref, bottom_ref, lr_ref, taps_ref, mix_ref, weight_ref,
    slide_out, depth_out, pre_out, reduced_out, act_out, shifted, total,
):
    fine_rows(slide_ref, top_ref, bottom_ref, lr_ref, shifted, slide_out)

    def conv(i, carry):
        def put(k, value):
            depth_out[k, i] = value.astype(BF)

        fine_conv(i, shifted, taps_ref, False, put)
        return carry

    lax.fori_loop(0, 16, conv, 0)
    chans = mix_ref.shape[0]
    wide = weight_ref.shape[1]
    for k in range(4):
        mixed = dot(depth_out[k].reshape(512, chans), mix_ref[...])
        pre = (slide_out[k].reshape(512, chans).astype(F4) + mixed).astype(BF)
        pre_out[k] = pre
        value = pre.astype(F4)
        unshuffled = (value * sigmoid(value)).astype(BF)
        part = dot(unshuffled, weight_ref[k * chans : (k + 1) * chans, :])
        if k == 0:
            total[...] = part
        else:
            total[...] += part
    reduced = total[...].astype(BF)
    reduced_out[...] = reduced
    value = reduced.astype(F4)
    act_out[...] = (value * sigmoid(value)).astype(BF).reshape(16, 32, wide)


def coarse_rows(row_of, lr_of, shifted):
    pick = picker(160, 48, coarse_source)

    def step(r, carry):
        got = dot(pick, jnp.concatenate([row_of(r), lr_of(r)], axis=0))
        shifted[:, r] = got.reshape(5, 32, got.shape[1])
        return carry

    lax.fori_loop(0, 24, step, 0)


def backward(
    cot_ref, tb_ref, lr_ref, mixc_ref, tapsc_ref, reduced_ref, pre_ref, depth_ref, weight_ref, mix_ref,
    slide_ref, top_ref, bottom_ref, lrf_ref,
    deltac_out, dfine_out, ddepth_out, gred_out, gmix_out, gtaps_out,
    delta, delta_lr, shiftc, delta_red, shifted,
):
    wide = mixc_ref.shape[0]
    chans = mix_ref.shape[0]
    mixc = mixc_ref[...]
    inner = dot_nt(cot_ref[...].reshape(512, wide), mixc).astype(BF).reshape(16, 32, wide)
    delta[4:20] = inner
    deltac_out[...] = inner
    edge = dot_nt(tb_ref[...].reshape(256, wide), mixc).astype(BF).reshape(8, 32, wide)
    delta[0:4] = edge[:4]
    delta[20:24] = edge[4:]
    delta_lr[...] = dot_nt(lr_ref[...].reshape(384, wide), mixc).astype(BF).reshape(24, 16, wide)
    coarse_rows(lambda r: delta[r], lambda r: delta_lr[r], shiftc)

    def conv(i, carry):
        total = None
        for a in range(5):
            for b in range(5):
                term = tapsc_ref[4 - a, 4 - b : 5 - b, :] * shiftc[b, i + 2 * a]
                total = term if total is None else total + term
        back = total.astype(BF).astype(F4)
        value = reduced_ref[i].astype(F4)
        s = sigmoid(value)
        slope = s * (1.0 + value * (1.0 - s))
        delta_red[i] = (cot_ref[i].astype(F4) + back * slope).astype(BF)
        return carry

    lax.fori_loop(0, 16, conv, 0)
    fine_rows(slide_ref, top_ref, bottom_ref, lrf_ref, shifted)
    red = delta_red[...].reshape(512, wide)
    for k in range(4):
        value = pre_ref[k].astype(F4)
        s = sigmoid(value)
        unshuffled = (value * s).astype(BF)
        gred_out[k * chans : (k + 1) * chans, :] = dot_tn(unshuffled, red).astype(BF)
        spread = dot_nt(red, weight_ref[k * chans : (k + 1) * chans, :])
        dfine = (spread * (s * (1.0 + value * (1.0 - s)))).astype(BF)
        dfine_out[k] = dfine.reshape(16, 32, chans)
        part = dot_tn(depth_ref[k], dfine)
        if k == 0:
            gmix_out[...] = part
        else:
            gmix_out[...] += part
        ddepth_out[k] = dot_nt(dfine, mix_ref[...]).astype(BF).reshape(16, 32, chans)

    def taps(i, sums):
        for p in range(2):
            for q in range(2):
                grad = ddepth_out[2 * p + q, i].astype(F4)
                fresh = []
                for a in range(3):
                    for b in range(3):
                        term = grad * shifted[SOURCE[q][b], 2 * i + p + a]
                        fresh.append(sums[3 * a + b] + jnp.sum(term.reshape(4, 8, chans), axis=0))
                sums = tuple(fresh)
        return sums

    sums = lax.fori_loop(0, 16, taps, tuple(jnp.zeros((8, chans), F4) for _ in range(9)))
    gtaps_out[...] = jnp.zeros_like(gtaps_out)
    for at in range(9):
        gtaps_out[at : at + 1, :] = jnp.sum(sums[at], axis=0, keepdims=True)


def coarse_forward(
    act_ref, top_ref, bottom_ref, lr_ref, taps_ref, mix_ref, reduced_ref, cot_ref, deltac_ref,
    gred_ref, gmixf_ref, gtapsf_ref, core_ref,
    section_out, mine_out, other_out, shifted, sums, depth, rows, packed,
):
    wide = mix_ref.shape[0]
    rows[0:4] = top_ref[...]
    rows[4:20] = act_ref[...]
    rows[20:24] = bottom_ref[...]
    coarse_rows(lambda r: rows[r], lambda r: lr_ref[r], shifted)
    sums[...] = jnp.zeros_like(sums)

    def conv(i, carry):
        total = None
        grad = deltac_ref[i].astype(F4)
        for a in range(5):
            for b in range(5):
                at = 5 * a + b
                window = shifted[b, i + 2 * a]
                term = taps_ref[a, b : b + 1, :] * window
                total = term if total is None else total + term
                sums[at] += jnp.sum((grad * window).reshape(4, 8, wide), axis=0)
        depth[i] = total.astype(BF)
        return carry

    lax.fori_loop(0, 16, conv, 0)
    flat = depth[...].reshape(512, wide)
    section_out[...] = (reduced_ref[...].reshape(512, wide).astype(F4) + dot(flat, mix_ref[...])).astype(BF).reshape(16, 32, wide)
    fine = gmixf_ref.shape[0]
    packed[RED:MIXC, :] = gred_ref[...]
    packed[MIXC:MIXF, :] = dot_tn(flat, cot_ref[...].reshape(512, wide)).astype(BF)
    packed[MIXF:, :] = jnp.zeros((TOTAL - MIXF, wide), BF)
    packed[MIXF:TAPC, 0:fine] = gmixf_ref[...].astype(BF)
    taps = jnp.concatenate([jnp.sum(sums[...], axis=1), jnp.zeros((7, wide), F4)], axis=0)
    packed[TAPC:TAPF, :] = taps.astype(BF)
    packed[TAPF : TAPF + 16, 0:fine] = gtapsf_ref[...].astype(BF)
    core = core_ref[0]
    half = TOTAL // 2
    mine_out[...] = packed[pl.ds(pl.multiple_of(core * half, half), half), :]
    other_out[...] = packed[pl.ds(pl.multiple_of((1 - core) * half, half), half), :]


def unpack(
    near_ref, far_ref, core_ref, tapsf_out, mixf_out, red_out, tapsc_out, mixc_out, packed, *, fine, coarse
):
    core = core_ref[0]
    half = TOTAL // 2
    packed[pl.ds(pl.multiple_of(core * half, half), half), :] = near_ref[...]
    packed[pl.ds(pl.multiple_of((1 - core) * half, half), half), :] = far_ref[...]
    chans = mixf_out.shape[0]
    red_out[...] = packed[RED:MIXC, :].astype(F4) * coarse
    mixc_out[...] = packed[MIXC:MIXF, :].astype(F4) * coarse
    mixf_out[...] = packed[MIXF:TAPC, 0:chans].astype(F4) * fine
    taps = packed[TAPC:TAPF, :].astype(F4) * coarse
    for a in range(5):
        tapsc_out[a] = taps[5 * a : 5 * a + 5]
    taps = packed[TAPF : TAPF + 16, 0:chans].astype(F4) * fine
    for a in range(3):
        tapsf_out[a] = taps[3 * a : 3 * a + 3]


def fine_backward(
    ddepth_ref, top_ref, bottom_ref, lr_ref, taps_ref, dfine_ref, slide_ref, out_ref, shifted
):
    chans = taps_ref.shape[2]
    pick = picker(64, 80, phase_source)
    weave = picker(64, 64, weave_source)

    def put(r, even, odd):
        got = dot(pick, jnp.concatenate([even, odd, lr_ref[r]], axis=0))
        shifted[0, r] = even.astype(F4)
        shifted[1, r] = odd.astype(F4)
        shifted[2, r] = got[:32]
        shifted[3, r] = got[32:]

    put(0, top_ref[0], top_ref[1])
    put(33, bottom_ref[0], bottom_ref[1])

    def fill(i, carry):
        for p in range(2):
            put(2 * i + p + 1, ddepth_ref[2 * p, i], ddepth_ref[2 * p + 1, i])
        return carry

    lax.fori_loop(0, 16, fill, 0)

    def conv(i, carry):
        found = {}

        def put_one(k, value):
            slide = slide_ref[k, i].astype(F4)
            kept = jnp.where(slide > 0, value, 0.0)
            found[k] = (dfine_ref[k, i].astype(F4) + kept).astype(BF)

        fine_conv(i, shifted, taps_ref, True, put_one)
        for p in range(2):
            both = jnp.concatenate([found[2 * p], found[2 * p + 1]], axis=0)
            out_ref[2 * i + p] = dot(weave, both).astype(BF)
        return carry

    lax.fori_loop(0, 16, conv, 0)


def call(body, outs, scratch, flops, *operands):
    def spec(kind):
        return pl.BlockSpec(memory_space=pltpu.SMEM if kind == jnp.int32 else pltpu.VMEM)

    return pl.pallas_call(
        body,
        out_shape=[jax.ShapeDtypeStruct(shape, kind) for shape, kind in outs],
        in_specs=[spec(operand.dtype) for operand in operands],
        out_specs=[spec(kind) for _, kind in outs],
        scratch_shapes=[pltpu.VMEM(shape, kind) for shape, kind in scratch],
        compiler_params=pltpu.CompilerParams(vmem_limit_bytes=LIMIT),
        cost_estimate=pl.CostEstimate(flops=flops, bytes_accessed=8_000_000, transcendentals=0),
    )(*operands)


def swap(first, last, axes):
    count = lax.axis_size(axes)
    even = lax.axis_index(axes) % 2 == 0
    near = lax.ppermute(jnp.where(even, last, first), axes, [(i, i ^ 1) for i in range(count)])
    far = [(i, i + 1) for i in range(1, count - 1, 2)]
    far = far + [(j, i) for i, j in far]
    away = lax.ppermute(jnp.where(even, first, last), axes, far)
    return jnp.where(even, away, near), jnp.where(even, near, away)


def halos(coarse, fine_top, fine_bottom, fine_left, fine_right):
    height, breadth, wide = coarse.shape
    chans = fine_top.shape[-1]

    def widen(rows):
        return jnp.pad(rows, ((0, 0), (0, wide - chans)))

    first = jnp.concatenate([coarse[:4].reshape(4 * breadth, wide), widen(fine_top)], axis=0)
    last = jnp.concatenate([coarse[-4:].reshape(4 * breadth, wide), widen(fine_bottom)], axis=0)
    low, high = swap(first, last, ROWS)
    split = 4 * breadth
    top, bottom = low[:split].reshape(4, breadth, wide), high[:split].reshape(4, breadth, wide)
    fine_low, fine_high = low[split:, :chans], high[split:, :chans]

    def column(at, edge, pixels):
        parts = [
            jnp.concatenate([top[:, at + s], coarse[:, at + s], bottom[:, at + s]], axis=0)
            for s in range(4)
        ]
        ends = [fine_low[edge : edge + 1], pixels, fine_high[edge : edge + 1]]
        return jnp.concatenate(parts + [widen(jnp.concatenate(ends, axis=0))], axis=0)

    left, right = swap(
        column(0, 0, fine_left),
        column(breadth - 4, fine_low.shape[0] - 1, fine_right),
        COLS,
    )
    tall = height + 8

    def spread(block):
        return block[: 4 * tall].reshape(4, tall, wide).transpose(1, 0, 2)

    sides_coarse = sides(spread(left), spread(right))
    sides_fine = sides(left[4 * tall :, None, :chans], right[4 * tall :, None, :chans])
    return top, bottom, sides_coarse, fine_low, fine_high, sides_fine


def reduce_terms(mine, other):
    total, wide = mine.shape
    core = lax.axis_index("core")
    plane = lax.axis_size(PLANE)
    depth = lax.axis_size("z")
    trade = [(0, 1), (1, 0)]
    mine = mine.astype(F4) + lax.ppermute(other, "core", trade).astype(F4)
    chunk = total // plane
    got = lax.all_to_all(mine.astype(BF).reshape(plane, chunk, wide), PLANE, 0, 0, tiled=True)
    mine = jnp.sum(got.astype(F4), axis=0).astype(BF)
    got = lax.all_to_all(jnp.broadcast_to(mine, (depth, chunk, wide)), "z", 0, 0, tiled=True)
    mine = jnp.sum(got.astype(F4), axis=0).astype(BF)
    got = lax.all_to_all(jnp.broadcast_to(mine, (plane, chunk, wide)), PLANE, 0, 0, tiled=True)
    got = got.reshape(total, wide)
    return got, lax.ppermute(got, "core", trade)


def sides(left, right):
    both = jnp.concatenate([left, right], axis=1)
    return jnp.pad(both, ((0, 0), (0, 16 - both.shape[1]), (0, 0)))


def shards(slide_pixels, taps_fine, mix_fine, reduce_weight, taps_coarse, mix_coarse, cotangent):
    height, breadth, chans = slide_pixels.shape
    wide = cotangent.shape[2]
    devices_all = lax.axis_size(ROWS) * lax.axis_size(COLS)
    scale_fine = float(height * breadth * devices_all) ** (-0.5)
    scale_coarse = float(height * breadth // 4 * devices_all) ** (-0.5)
    core = lax.axis_index("core").astype(jnp.int32).reshape(1)
    ctop, cbottom, clr, top, bottom, lr = halos(
        cotangent, slide_pixels[0], slide_pixels[-1], slide_pixels[:, 0], slide_pixels[:, -1]
    )
    top, bottom = top[None], bottom[None]

    slide, depth, pre, reduced, act = call(
        fine_forward,
        [
            ((4, 16, 32, chans), BF),
            ((4, 16, 32, chans), BF),
            ((4, 512, chans), BF),
            ((512, wide), BF),
            ((16, 32, wide), BF),
        ],
        [((4, 34, 32, chans), F4), ((512, wide), F4)],
        4_000_000_000,
        slide_pixels, top, bottom, lr, taps_fine, mix_fine, reduce_weight,
    )
    reduced = reduced.reshape(16, 32, wide)

    delta_coarse, dfine, ddepth, term_reduce, term_mix_fine, term_taps_fine = call(
        backward,
        [
            ((16, 32, wide), BF),
            ((4, 16, 32, chans), BF),
            ((4, 16, 32, chans), BF),
            ((4 * chans, wide), BF),
            ((chans, chans), F4),
            ((16, chans), F4),
        ],
        [
            ((24, 32, wide), BF),
            ((24, 16, wide), BF),
            ((5, 24, 32, wide), F4),
            ((16, 32, wide), BF),
            ((4, 34, 32, chans), F4),
        ],
        8_000_000_000,
        cotangent, jnp.concatenate([ctop, cbottom], axis=0), clr, mix_coarse, taps_coarse, reduced, pre,
        depth.reshape(4, 512, chans), reduce_weight, mix_fine, slide_pixels, top, bottom, lr,
    )

    inner = ddepth.reshape(2, 2, 16, 32, chans)
    atop, abottom, alr, dtop, dbottom, dlr = halos(
        act,
        ddepth[:2, 0].reshape(breadth, chans),
        ddepth[2:, 15].reshape(breadth, chans),
        inner[:, 0, :, 0].transpose(1, 0, 2).reshape(height, chans),
        inner[:, 1, :, 31].transpose(1, 0, 2).reshape(height, chans),
    )
    section_out, mine, other = call(
        coarse_forward,
        [((16, 32, wide), BF), ((TOTAL // 2, wide), BF), ((TOTAL // 2, wide), BF)],
        [
            ((5, 24, 32, wide), F4),
            ((25, 8, wide), F4),
            ((16, 32, wide), BF),
            ((24, 32, wide), BF),
            ((TOTAL, wide), BF),
        ],
        4_000_000_000,
        act, atop, abottom, alr, taps_coarse, mix_coarse, reduced, cotangent, delta_coarse,
        term_reduce, term_mix_fine, term_taps_fine, core,
    )
    (pixel_grad,) = call(
        fine_backward,
        [((height, breadth, chans), BF)],
        [((4, 34, 32, chans), F4)],
        2_000_000_000,
        ddepth, dtop.reshape(2, 32, chans), dbottom.reshape(2, 32, chans), dlr, taps_fine, dfine, slide,
    )
    near, far = reduce_terms(mine, other)
    grads = call(
        functools.partial(unpack, fine=scale_fine, coarse=scale_coarse),
        [
            ((3, 3, chans), F4),
            ((chans, chans), F4),
            ((4 * chans, wide), F4),
            ((5, 5, wide), F4),
            ((wide, wide), F4),
        ],
        [((TOTAL, wide), BF)],
        1_000_000,
        near, far, core,
    )
    return (section_out, pixel_grad, *grads)


def solution(mesh):
    fine = Mesh(mesh.devices.reshape(2, 2, 4, 2, 8), ("yl", "core", "x", "yh", "z"))
    tiles = P(ROWS, COLS, None)
    return jax.shard_map(
        shards,
        mesh=fine,
        in_specs=(tiles, P(), P(), P(), P(), P(), tiles),
        out_specs=(tiles, tiles, P(), P(), P(), P(), P()),
        check_vma=False,
    )
```

time: 491 us -> 173 us (0.35)
  waiting for transfers between devices: 263 us -> 21.6 us
  Pallas kernels: 0 us -> 53 us
  blocking collectives: 89.9 us -> 43.4 us
  other arithmetic: 33 us -> 4.87 us
  matrix products: 19.5 us -> 0 us
  starting transfers between devices: 45.2 us -> 29 us
  between operations: 15.6 us -> 1.48 us
    psum x1 -> x0, waiting for transfers between devices: 246 us -> none  [shards(): lax.psum((term_taps_fine, term_mix_fine, term_reduce, term_taps_coarse, t...]
    psum x1 -> x0, blocking collectives: 89.9 us -> none  [shards(): lax.psum((term_taps_fine, term_mix_fine, term_reduce, term_taps_coarse, t...]
    pallas_call x0 -> x5, Pallas kernels: none -> 53 us  [call(): pl.pallas_call(body, out_shape=[jax.ShapeDtypeStruct(shape, kind) for sha...]
    all_to_all x0 -> x2, blocking collectives: none -> 43.4 us  [the longest x1 27.1 us: reduce_terms(): lax.all_to_all(mine.astype(BF).reshape(plane, chunk, wide), PLANE, 0, 0,...]
    ppermute x16 -> x10, starting transfers between devices: 45.1 us -> 23.8 us  [the longest x4 12.3 us: swap(): lax.ppermute(jnp.where(even, last, first), axes, [(i, i ^ 1) for i in ran...]
    dot_general x9 -> x0, matrix products: 19.5 us -> none  [the longest x3 5.88 us: pixel_product(): lax.dot_general(left, right, (((0, 1), (0, 1)), ((), ())), preferred_elem...]
    convert_element_type x4 -> x1, other arithmetic: 17.9 us -> 0.21 us  [reduce_terms(): mine.astype(BF).reshape(plane, chunk, wide)]
    convert_element_type x6 -> x0, local copies, waits for them, and re-layouts: 14.6 us -> none  [the longest x3 8.64 us: shards(): unshuffled = jax.nn.silu(pre_fine.astype(jnp.float32)).astype(jnp.bfloat16)]
  transfers between devices with their start and end apart: 17 -> 11, of which waited for: 8 -> 6; matrix products, arithmetic and copies ran while one was open for 4% -> 3% of each run, Pallas kernels for 0% -> 5%
where the time goes in v1:
time: 173 us; the launch traced here: 172 us
  Pallas kernels  53 us (31%)
  blocking collectives  43.4 us (25%)
  starting transfers between devices  29 us (17%)
  waiting for transfers between devices  21.6 us (12%)
  local copies, waits for them, and re-layouts  18.6 us (11%)
  other arithmetic  4.87 us (3%)
    pallas_call x5, Pallas kernels, call(): pl.pallas_call(body, out_shape=[jax.ShapeDtypeStruct(shape, kind) for sha...  53 us
    all_to_all x1, blocking collectives, reduce_terms(): lax.all_to_all(mine.astype(BF).reshape(plane, chunk, wide), PLANE, 0, 0,...  27.1 us
    all_to_all x1, blocking collectives, reduce_terms(): lax.all_to_all(jnp.broadcast_to(mine, (depth, chunk, wide)), 'z', 0, 0, t...  16.3 us
    ppermute x4, starting transfers between devices, swap(): lax.ppermute(jnp.where(even, last, first), axes, [(i, i ^ 1) for i in ran...  12.3 us
    all_to_all x1, waiting for transfers between devices, reduce_terms(): lax.all_to_all(jnp.broadcast_to(mine, (plane, chunk, wide)), PLANE, 0, 0,...  10.2 us
    ppermute x4, starting transfers between devices, swap(): away = lax.ppermute(jnp.where(even, first, last), axes, far)  7.52 us
    all_to_all x1, starting transfers between devices, reduce_terms(): lax.all_to_all(jnp.broadcast_to(mine, (plane, chunk, wide)), PLANE, 0, 0,...  5.21 us
    ppermute x4, waiting for transfers between devices, swap(): away = lax.ppermute(jnp.where(even, first, last), axes, far)  5.14 us
  transfers between devices with their start and end apart: 11, of which 6 were waited for; matrix products, arithmetic and copies ran while one was open for 3% of the time, Pallas kernels for 5%

profile of v1, /device:TPU:1, one launch (start us, length us, event | category | flops | bytes accessed | tf_op | source)
XLA Modules:
  0.0 171.9 jit_solution(14927611332860655930)
XLA Ops:
  0.6 0.0 copy-start.3
  0.7 0.9 slice_bitcast_fusion.3
  1.5 1.0 fusion.46
  2.5 0.1 broadcast_select_fusion.6
  2.6 3.3 %collective-permute-start.1 = (bf16[192,416]{1,0:T(8,128)(2,1)S(1)}, bf16[192,416]{1,0:T(8,128)(2,1)S(1)}, u32[]{:S(2)}, u32[]{:S(2)}) collective-permute-start(bf16[192,416]{1,0:T(8,128)(2,1)S(1)} %get-tuple-element.135), channel_id=1, source_target_pairs={{0,64},{64,0},{128,192},{192,128},{1,65},{65,1},{129,193},{193,129... | collective-permute-start | bytes 479240 | tf_op jit(solution)/shard_map/ppermute | solution.py:332
  5.9 1.9 %collective-permute-start = (bf16[192,416]{1,0:T(8,128)(2,1)S(1)}, bf16[192,416]{1,0:T(8,128)(2,1)S(1)}, u32[]{:S(2)}, u32[]{:S(2)}) collective-permute-start(bf16[192,416]{1,0:T(8,128)(2,1)S(1)} %get-tuple-element.136), channel_id=1, source_target_pairs={{64,128},{128,64},{65,129},{129,65},{66,130},{130,66},{67,131},{13... | collective-permute-start | bytes 479240 | tf_op jit(solution)/shard_map/ppermute | solution.py:335
  7.9 1.0 fusion.42
  8.9 0.2 fusion.45
  9.2 1.5 copy.315.weight_ref
  10.8 2.2 %collective-permute-done = bf16[192,416]{1,0:T(8,128)(2,1)S(1)} collective-permute-done((bf16[192,416]{1,0:T(8,128)(2,1)S(1)}, bf16[192,416]{1,0:T(8,128)(2,1)S(1)}, u32[]{:S(2)}, u32[]{:S(2)}) %collective-permute-start) | collective-permute-done | bytes 159776 | tf_op jit(solution)/shard_map/ppermute | solution.py:335
  13.0 0.6 slice_bitcast_fusion
  13.6 0.1 fusion.54
  13.7 0.1 fusion.53
  13.9 0.6 concatenate.56
  14.5 0.6 concatenate.54
  15.1 0.7 collective-permute-start.2
  15.8 2.9 %collective-permute-start.3 = (bf16[130,416]{1,0:T(8,128)(2,1)S(1)}, bf16[130,416]{1,0:T(8,128)(2,1)S(1)}, u32[]{:S(2)}, u32[]{:S(2)}) collective-permute-start(bf16[130,416]{1,0:T(8,128)(2,1)S(1)} %get-tuple-element.144), channel_id=1, source_target_pairs={{0,1},{1,0},{2,3},{3,2},{4,5},{5,4},{6,7},{7,6},{8,9},{9,8},{10,11... | collective-permute-start | bytes 324488 | tf_op jit(solution)/shard_map/ppermute | solution.py:332
  18.7 0.7 pad_maximum_fusion.tb_ref
  19.4 1.7 collective-permute-done.3
  21.2 0.1 copy.443
  21.3 0.1 copy.442
  21.4 0.9 fusion.8.lr_ref
  22.3 0.8 fusion.14.lr_ref.lrf_ref
  23.1 8.6 %shard_map.126 = (bf16[4,16,32,208]{3,2,1,0:T(8,128)(2,1)}, bf16[4,16,32,208]{3,2,1,0:T(8,128)(2,1)}, bf16[4,512,208]{2,1,0:T(8,128)(2,1)}, bf16[512,416]{1,0:T(8,128)(2,1)}, bf16[16,32,416]{2,1,0:T(8,128)(2,1)}) custom-call(bf16[32,64,208]{2,1,0:T(8,128)(2,1)} %slide_ref.3, bf16[1,64,208]{2,1,0:T(8,128)(2,1)} %get-tuple-element.186.top_ref, ...), custom_call_target="tpu_custom_call" | custom-call | flops 4000000000 | bytes 8000000 | tf_op jit(solution)/shard_map/pallas_call | solution.py:318
  31.7 19.7 %shard_map.127 = (bf16[16,32,416]{2,1,0:T(8,128)(2,1)}, bf16[4,16,32,208]{3,2,1,0:T(8,128)(2,1)}, bf16[4,16,32,208]{3,2,1,0:T(8,128)(2,1)}, bf16[832,416]{1,0:T(...) custom-call(bf16[16,32,416]{2,1,0:T(8,128)(2,1)} %cot_ref.3, bf16[8,32,416]{2,1,0:T(8,128)(2,1)} %pad_maximum_fusion.tb_ref, ...), custom_call_target="tpu_custom_call" | custom-call | flops 8000000000 | bytes 8000000 | tf_op jit(solution)/shard_map/pallas_call | solution.py:318
  51.4 0.8 fusion.41
  52.2 1.0 fusion.40
  53.4 0.1 broadcast_select_fusion.2
  53.5 0.1 collective-permute-start.5
  53.6 4.3 %collective-permute-start.4 = (bf16[192,416]{1,0:T(8,128)(2,1)S(1)}, bf16[192,416]{1,0:T(8,128)(2,1)S(1)}, u32[]{:S(2)}, u32[]{:S(2)}) collective-permute-start(bf16[192,416]{1,0:T(8,128)(2,1)S(1)} %get-tuple-element.134), channel_id=1, source_target_pairs={{64,128},{128,64},{65,129},{129,65},{66,130},{130,66},{67,131},{13... | collective-permute-start | bytes 479240 | tf_op jit(solution)/shard_map/ppermute | solution.py:335
  57.8 0.2 fusion.43
  58.2 3.0 %collective-permute-done.4 = bf16[192,416]{1,0:T(8,128)(2,1)S(1)} collective-permute-done((bf16[192,416]{1,0:T(8,128)(2,1)S(1)}, bf16[192,416]{1,0:T(8,128)(2,1)S(1)}, u32[]{:S(2)}, u32[]{:S(2)}) %collective-permute-start.4) | collective-permute-done | bytes 159776 | tf_op jit(solution)/shard_map/ppermute | solution.py:335
  61.3 0.1 fusion.52
  61.5 0.1 fusion.51
  61.7 0.6 concatenate.65
  62.3 0.6 concatenate.63
  62.9 0.7 collective-permute-start.6
  63.6 6.0 %collective-permute-start.7 = (bf16[130,416]{1,0:T(8,128)(2,1)S(1)}, bf16[130,416]{1,0:T(8,128)(2,1)S(1)}, u32[]{:S(2)}, u32[]{:S(2)}) collective-permute-start(bf16[130,416]{1,0:T(8,128)(2,1)S(1)} %get-tuple-element.140), channel_id=1, source_target_pairs={{0,1},{1,0},{2,3},{3,2},{4,5},{5,4},{6,7},{7,6},{8,9},{9,8},{10,11... | collective-permute-start | bytes 324488 | tf_op jit(solution)/shard_map/ppermute | solution.py:332
  69.6 2.4 %collective-permute-done.7 = bf16[130,416]{1,0:T(8,128)(2,1)S(1)} collective-permute-done((bf16[130,416]{1,0:T(8,128)(2,1)S(1)}, bf16[130,416]{1,0:T(8,128)(2,1)S(1)}, u32[]{:S(2)}, u32[]{:S(2)}) %collective-permute-start.7) | collective-permute-done | bytes 108192 | tf_op jit(solution)/shard_map/ppermute | solution.py:332
  72.1 0.1 copy.441
  72.1 0.1 copy.440
  72.2 0.9 fusion.9.lr_ref
  73.1 12.1 %shard_map.128 = (bf16[16,32,416]{2,1,0:T(8,128)(2,1)}, bf16[768,416]{1,0:T(8,128)(2,1)}, bf16[768,416]{1,0:T(8,128)(2,1)}) custom-call(bf16[16,32,416]{2,1,0:T(8,128)(2,1)} %get-tuple-element.26.act_ref, bf16[4,32,416]{2,1,0:T(8,128)(2,1)} %bitcast.206, bf16[4,32,416]{2,1,0:T(8,128)(2,1)} %bitcast.204, bf16[24,16,416]{2,1,0:T(8,128)(2,1)} %fusion.9.lr_ref, ...), custom_call_target="tpu_custom_call" | custom-call | flops 4000000000 | bytes 8000000 | tf_op jit(solution)/shard_map/pallas_call | solution.py:318
  85.2 1.5 copy.327
  86.6 0.1 collective-permute-start.8
  86.7 2.1 %collective-permute-done.8 = bf16[768,416]{0,1:T(8,128)(2,1)S(1)} collective-permute-done((bf16[768,416]{0,1:T(8,128)(2,1)S(1)}, bf16[768,416]{0,1:T(8,128)(2,1)S(1)}, u32[]{:S(2)}, u32[]{:S(2)}) %collective-permute-start.8) | collective-permute-done | bytes 639008 | tf_op jit(solution)/shard_map/ppermute | solution.py:382
  88.8 0.3 copy.328
  89.1 0.2 add_convert_fusion
  89.3 27.1 %all_to_all.15 = bf16[16,48,416]{2,1,0:T(8,128)(2,1)S(1)} all-to-all(bf16[16,48,416]{2,1,0:T(8,128)(2,1)S(1)} %bitcast.186), channel_id=1, replica_groups=mesh['yl'=2,'core'=2,'x'=4,'yh'=2,'z'=8] {'yl','x','yh'}, dimensions={0} | all-to-all | bytes 1277952 | tf_op jit(solution)/shard_map/all_to_all | solution.py:384
  116.4 0.1 reduce_sum.24
  116.5 16.3 %all_to_all.16 = bf16[8,48,416]{2,1,0:T(8,128)(2,1)S(1)} all-to-all(bf16[8,48,416]{2,1,0:T(8,128)(2,1)S(1)} %broadcast_in_dim.30), channel_id=1, replica_groups=mesh['yl'=2,'core'=2,'x'=4,'yh'=2,'z'=8] {'z'}, dimensions={0} | all-to-all | bytes 638976 | tf_op jit(solution)/shard_map/all_to_all | solution.py:386
  132.8 0.1 reduce_sum.25
  132.9 1.0 broadcast_in_dim.31
  133.9 5.2 %all-to-all-start.2 = ((bf16[16,48,416]{2,1,0:T(8,128)(2,1)}), bf16[16,48,416]{2,1,0:T(8,128)(2,1)S(1)}, u32[]{:S(2)}, u32[]{:S(2)}) async-start(bf16[16,48,416]{2,1,0:T(8,128)(2,1)} %broadcast_in_dim.31), calls=%async_computation.2 | async-start | bytes 1572864 | tf_op jit(solution)/shard_map/all_to_all | solution.py:388
  139.1 0.6 slice.399
  139.7 0.6 slice.398
  140.3 10.2 %all-to-all-done.2 = bf16[16,48,416]{2,1,0:T(8,128)(2,1)S(1)} async-done(((bf16[16,48,416]{2,1,0:T(8,128)(2,1)}), bf16[16,48,416]{2,1,0:T(8,128)(2,1)S(1)}, u32[]{:S(2)}, u32[]{:S(2)}) %all-to-all-start.2) | async-done | bytes 639008 | tf_op jit(solution)/shard_map/all_to_all | solution.py:388
  150.6 0.2 copy.329
  150.8 3.9 %collective-permute-start.9 = (bf16[768,416]{0,1:T(8,128)(2,1)S(1)}, bf16[768,416]{0,1:T(8,128)(2,1)S(1)}, u32[]{:S(2)}, u32[]{:S(2)}) collective-permute-start(bf16[768,416]{0,1:T(8,128)(2,1)S(1)} %copy.329), channel_id=1, source_target_pairs={{0,64},{64,0},{1,65},{65,1},{2,66},{66,2},{3,67},{67,3},{4,68},{68... | collective-permute-start | bytes 1916936 | tf_op jit(solution)/shard_map/ppermute | solution.py:390
  154.8 0.8 fusion.15.lr_ref
  155.6 9.4 %shard_map.129 = bf16[32,64,208]{2,1,0:T(8,128)(2,1)} custom-call(bf16[4,16,32,208]{3,2,1,0:T(8,128)(2,1)} %get-tuple-element.30.ddepth_ref, bf16[2,32,208]{2,1,0:T(8,128)(2,1)} %bitcast.220, bf16[2,32,208]{2,1,0:T(8,128)(2,1)} %bitcast.219, bf16[34,16,208]{2,1,0:T(8,128)(2,1)} %fusion.15.lr_ref, f32[3,3,208]{2,1,0:T(4,128)} %taps_ref.5, ...), custom_call_target="tpu_custom_call" | custom-call | flops 2000000000 | bytes 8000000 | tf_op jit(solution)/shard_map/pallas_call | solution.py:318
  165.0 1.2 copy.330.far_ref
  166.1 3.2 %shard_map.130 = (f32[3,3,208]{2,1,0:T(4,128)}, f32[208,208]{1,0:T(8,128)}, f32[832,416]{1,0:T(8,128)}, f32[5,5,416]{2,1,0:T(8,128)}, f32[416,416]{1,0:T(8,128)}) custom-call(bf16[768,416]{1,0:T(8,128)(2,1)} %bitcast.185, bf16[768,416]{1,0:T(8,128)(2,1)} %copy.330.far_ref, s32[1]{0:T(128)} %bitcast.41.core_ref), custom_call_target="tpu_custom_call" | custom-call | flops 1000000 | bytes 8000000 | tf_op jit(solution)/shard_map/pallas_call | solution.py:318
  169.3 2.6 %copy.331 = f32[832,416]{0,1:T(8,128)} copy(f32[832,416]{1,0:T(8,128)} %get-tuple-element.98) | data formatting | bytes 2768896
  (92 shorter events, 0.8 us)
Async XLA Ops:
  0.6 8.3 %copy-start.3 = (bf16[16,32,416]{2,1,0:T(8,128)(2,1)S(1)}, bf16[16,32,416]{2,1,0:T(8,128)(2,1)}, u32[]{:S(2)}) copy-start(bf16[16,32,416]{2,1,0:T(8,128)(2,1)} %cot_ref.3) | copy-start | bytes 1277956
  0.6 8.5 %copy-start.2 = (bf16[832,416]{0,1:T(8,128)(2,1)S(1)}, bf16[832,416]{0,1:T(8,128)(2,1)}, u32[]{:S(2)}) copy-start(bf16[832,416]{0,1:T(8,128)(2,1)} %param.10) | copy-start | bytes 2076676
  2.6 8.1 %collective-permute-start.1 = (bf16[192,416]{1,0:T(8,128)(2,1)S(1)}, bf16[192,416]{1,0:T(8,128)(2,1)S(1)}, u32[]{:S(2)}, u32[]{:S(2)}) collective-permute-start(bf16[192,416]{1,0:T(8,128)(2,1)S(1)} %get-tuple-element.135), channel_id=1, source_target_pairs={{0,64},{64,0},{128,192},{192,128},{1,65},{65,1},{129,193},{193,129... | collective-permute-start | bytes 479240 | tf_op jit(solution)/shard_map/ppermute | solution.py:332
  5.9 7.0 %collective-permute-start = (bf16[192,416]{1,0:T(8,128)(2,1)S(1)}, bf16[192,416]{1,0:T(8,128)(2,1)S(1)}, u32[]{:S(2)}, u32[]{:S(2)}) collective-permute-start(bf16[192,416]{1,0:T(8,128)(2,1)S(1)} %get-tuple-element.136), channel_id=1, source_target_pairs={{64,128},{128,64},{65,129},{129,65},{66,130},{130,66},{67,131},{13... | collective-permute-start | bytes 479240 | tf_op jit(solution)/shard_map/ppermute | solution.py:335
  15.1 4.3 %collective-permute-start.2 = (bf16[130,416]{1,0:T(8,128)(2,1)S(1)}, bf16[130,416]{1,0:T(8,128)(2,1)S(1)}, u32[]{:S(2)}, u32[]{:S(2)}) collective-permute-start(bf16[130,416]{1,0:T(8,128)(2,1)S(1)} %get-tuple-element.143), channel_id=1, source_target_pairs={{1,2},{3,4},{5,6},{7,8},{9,10},{11,12},{13,14},{15,16},{17,18},{19... | collective-permute-start | bytes 324488 | tf_op jit(solution)/shard_map/ppermute | solution.py:335
  15.8 5.3 %collective-permute-start.3 = (bf16[130,416]{1,0:T(8,128)(2,1)S(1)}, bf16[130,416]{1,0:T(8,128)(2,1)S(1)}, u32[]{:S(2)}, u32[]{:S(2)}) collective-permute-start(bf16[130,416]{1,0:T(8,128)(2,1)S(1)} %get-tuple-element.144), channel_id=1, source_target_pairs={{0,1},{1,0},{2,3},{3,2},{4,5},{5,4},{6,7},{7,6},{8,9},{9,8},{10,11... | collective-permute-start | bytes 324488 | tf_op jit(solution)/shard_map/ppermute | solution.py:332
  31.7 21.7 %copy-start.4 = (bf16[16,32,416]{2,1,0:T(8,128)(2,1)S(1)}, bf16[16,32,416]{2,1,0:T(8,128)(2,1)}, u32[]{:S(2)}) copy-start(bf16[16,32,416]{2,1,0:T(8,128)(2,1)} %get-tuple-element.26.act_ref) | copy-start | bytes 1277956
  53.5 4.7 %collective-permute-start.5 = (bf16[192,416]{1,0:T(8,128)(2,1)S(1)}, bf16[192,416]{1,0:T(8,128)(2,1)S(1)}, u32[]{:S(2)}, u32[]{:S(2)}) collective-permute-start(bf16[192,416]{1,0:T(8,128)(2,1)S(1)} %get-tuple-element.133), channel_id=1, source_target_pairs={{0,64},{64,0},{128,192},{192,128},{1,65},{65,1},{129,193},{193,129... | collective-permute-start | bytes 479240 | tf_op jit(solution)/shard_map/ppermute | solution.py:332
  53.6 7.6 %collective-permute-start.4 = (bf16[192,416]{1,0:T(8,128)(2,1)S(1)}, bf16[192,416]{1,0:T(8,128)(2,1)S(1)}, u32[]{:S(2)}, u32[]{:S(2)}) collective-permute-start(bf16[192,416]{1,0:T(8,128)(2,1)S(1)} %get-tuple-element.134), channel_id=1, source_target_pairs={{64,128},{128,64},{65,129},{129,65},{66,130},{130,66},{67,131},{13... | collective-permute-start | bytes 479240 | tf_op jit(solution)/shard_map/ppermute | solution.py:335
  61.2 10.9 %copy-start.5 = (bf16[128,416]{1,0:T(8,128)(2,1)}, bf16[128,416]{1,0:T(8,128)(2,1)S(1)}, u32[]{:S(2)}) copy-start(bf16[128,416]{1,0:T(8,128)(2,1)S(1)} %slice.373) | copy-start | bytes 319492
  61.3 11.8 %copy-start.6 = (bf16[128,416]{1,0:T(8,128)(2,1)}, bf16[128,416]{1,0:T(8,128)(2,1)S(1)}, u32[]{:S(2)}) copy-start(bf16[128,416]{1,0:T(8,128)(2,1)S(1)} %slice.372) | copy-start | bytes 319492
  62.9 6.7 %collective-permute-start.6 = (bf16[130,416]{1,0:T(8,128)(2,1)S(1)}, bf16[130,416]{1,0:T(8,128)(2,1)S(1)}, u32[]{:S(2)}, u32[]{:S(2)}) collective-permute-start(bf16[130,416]{1,0:T(8,128)(2,1)S(1)} %get-tuple-element.139), channel_id=1, source_target_pairs={{1,2},{3,4},{5,6},{7,8},{9,10},{11,12},{13,14},{15,16},{17,18},{19... | collective-permute-start | bytes 324488 | tf_op jit(solution)/shard_map/ppermute | solution.py:335
  63.6 8.4 %collective-permute-start.7 = (bf16[130,416]{1,0:T(8,128)(2,1)S(1)}, bf16[130,416]{1,0:T(8,128)(2,1)S(1)}, u32[]{:S(2)}, u32[]{:S(2)}) collective-permute-start(bf16[130,416]{1,0:T(8,128)(2,1)S(1)} %get-tuple-element.140), channel_id=1, source_target_pairs={{0,1},{1,0},{2,3},{3,2},{4,5},{5,4},{6,7},{7,6},{8,9},{9,8},{10,11... | collective-permute-start | bytes 324488 | tf_op jit(solution)/shard_map/ppermute | solution.py:332
  85.2 3.9 %copy-start.1 = (bf16[768,416]{1,0:T(8,128)(2,1)S(1)}, bf16[768,416]{1,0:T(8,128)(2,1)}, u32[]{:S(2)}) copy-start(bf16[768,416]{1,0:T(8,128)(2,1)} %get-tuple-element.38) | copy-start | bytes 1916932
  86.6 2.2 %collective-permute-start.8 = (bf16[768,416]{0,1:T(8,128)(2,1)S(1)}, bf16[768,416]{0,1:T(8,128)(2,1)S(1)}, u32[]{:S(2)}, u32[]{:S(2)}) collective-permute-start(bf16[768,416]{0,1:T(8,128)(2,1)S(1)} %copy.327), channel_id=1, source_target_pairs={{0,64},{64,0},{1,65},{65,1},{2,66},{66,2},{3,67},{67,3},{4,68},{68... | collective-permute-start | bytes 1916936 | tf_op jit(solution)/shard_map/ppermute | solution.py:382
  133.9 16.7 %all-to-all-start.2 = ((bf16[16,48,416]{2,1,0:T(8,128)(2,1)}), bf16[16,48,416]{2,1,0:T(8,128)(2,1)S(1)}, u32[]{:S(2)}, u32[]{:S(2)}) async-start(bf16[16,48,416]{2,1,0:T(8,128)(2,1)} %broadcast_in_dim.31), calls=%async_computation.2 | async-start | bytes 1572864 | tf_op jit(solution)/shard_map/all_to_all | solution.py:388
  150.6 14.4 %copy-start = (bf16[16,48,416]{2,1,0:T(8,128)(2,1)}, bf16[16,48,416]{2,1,0:T(8,128)(2,1)S(1)}, u32[]{:S(2)}) copy-start(bf16[16,48,416]{2,1,0:T(8,128)(2,1)S(1)} %all-to-all-done.2) | copy-start | bytes 1916932
  150.8 14.2 %collective-permute-start.9 = (bf16[768,416]{0,1:T(8,128)(2,1)S(1)}, bf16[768,416]{0,1:T(8,128)(2,1)S(1)}, u32[]{:S(2)}, u32[]{:S(2)}) collective-permute-start(bf16[768,416]{0,1:T(8,128)(2,1)S(1)} %copy.329), channel_id=1, source_target_pairs={{0,64},{64,0},{1,65},{65,1},{2,66},{66,2},{3,67},{67,3},{4,68},{68... | collective-permute-start | bytes 1916936 | tf_op jit(solution)/shard_map/ppermute | solution.py:390

commit v2 on v1

--- a/solution.py
+++ b/solution.py
@@ -14,6 +14,7 @@
 F4 = jnp.float32
 LIMIT = 56 * 1024 * 1024
 RED, MIXC, MIXF, TAPC, TAPF, TOTAL = 0, 832, 1248, 1456, 1488, 1536
+LANES = 512
 SOURCE = ((2, 0, 1), (0, 1, 3))
 
 
@@ -83,7 +84,7 @@
                 keep[2 * p + 1, i] = got[32:64].astype(BF)
         return carry
 
-    lax.fori_loop(0, 16, step, 0)
+    lax.fori_loop(0, 16, step, 0, unroll=True)
 
 
 def fine_conv(i, shifted, taps_ref, flip, put):
@@ -111,7 +112,7 @@
         fine_conv(i, shifted, taps_ref, False, put)
         return carry
 
-    lax.fori_loop(0, 16, conv, 0)
+    lax.fori_loop(0, 16, conv, 0, unroll=2)
     chans = mix_ref.shape[0]
     wide = weight_ref.shape[1]
     for k in range(4):
@@ -139,17 +140,13 @@
         shifted[:, r] = got.reshape(5, 32, got.shape[1])
         return carry
 
-    lax.fori_loop(0, 24, step, 0)
-
-
-def backward(
-    cot_ref, tb_ref, lr_ref, mixc_ref, tapsc_ref, reduced_ref, pre_ref, depth_ref, weight_ref, mix_ref,
-    slide_ref, top_ref, bottom_ref, lrf_ref,
-    deltac_out, dfine_out, ddepth_out, gred_out, gmix_out, gtaps_out,
-    delta, delta_lr, shiftc, delta_red, shifted,
+    lax.fori_loop(0, 24, step, 0, unroll=True)
+
+
+def coarse_backward(
+    cot_ref, tb_ref, lr_ref, mixc_ref, tapsc_ref, reduced_ref, deltac_out, delta_red, delta, delta_lr, shiftc
 ):
     wide = mixc_ref.shape[0]
-    chans = mix_ref.shape[0]
     mixc = mixc_ref[...]
     inner = dot_nt(cot_ref[...].reshape(512, wide), mixc).astype(BF).reshape(16, 32, wide)
     delta[4:20] = inner
@@ -173,9 +170,16 @@
         delta_red[i] = (cot_ref[i].astype(F4) + back * slope).astype(BF)
         return carry
 
-    lax.fori_loop(0, 16, conv, 0)
+    lax.fori_loop(0, 16, conv, 0, unroll=2)
+
+
+def fine_terms(
+    red_ref, pre_ref, depth_ref, weight_ref, mix_ref, slide_ref, top_ref, bottom_ref, lrf_ref,
+    dfine_out, ddepth_out, gred_out, gmix_out, gtaps_out, shifted,
+):
+    chans = mix_ref.shape[0]
     fine_rows(slide_ref, top_ref, bottom_ref, lrf_ref, shifted)
-    red = delta_red[...].reshape(512, wide)
+    red = red_ref[...]
     for k in range(4):
         value = pre_ref[k].astype(F4)
         s = sigmoid(value)
@@ -203,7 +207,7 @@
                 sums = tuple(fresh)
         return sums
 
-    sums = lax.fori_loop(0, 16, taps, tuple(jnp.zeros((8, chans), F4) for _ in range(9)))
+    sums = lax.fori_loop(0, 16, taps, tuple(jnp.zeros((8, chans), F4) for _ in range(9)), unroll=2)
     gtaps_out[...] = jnp.zeros_like(gtaps_out)
     for at in range(9):
         gtaps_out[at : at + 1, :] = jnp.sum(sums[at], axis=0, keepdims=True)
@@ -234,16 +238,16 @@
         depth[i] = total.astype(BF)
         return carry
 
-    lax.fori_loop(0, 16, conv, 0)
+    lax.fori_loop(0, 16, conv, 0, unroll=2)
     flat = depth[...].reshape(512, wide)
     section_out[...] = (reduced_ref[...].reshape(512, wide).astype(F4) + dot(flat, mix_ref[...])).astype(BF).reshape(16, 32, wide)
     fine = gmixf_ref.shape[0]
-    packed[RED:MIXC, :] = gred_ref[...]
-    packed[MIXC:MIXF, :] = dot_tn(flat, cot_ref[...].reshape(512, wide)).astype(BF)
-    packed[MIXF:, :] = jnp.zeros((TOTAL - MIXF, wide), BF)
+    packed[...] = jnp.zeros_like(packed)
+    packed[RED:MIXC, 0:wide] = gred_ref[...]
+    packed[MIXC:MIXF, 0:wide] = dot_tn(flat, cot_ref[...].reshape(512, wide)).astype(BF)
     packed[MIXF:TAPC, 0:fine] = gmixf_ref[...].astype(BF)
     taps = jnp.concatenate([jnp.sum(sums[...], axis=1), jnp.zeros((7, wide), F4)], axis=0)
-    packed[TAPC:TAPF, :] = taps.astype(BF)
+    packed[TAPC:TAPF, 0:wide] = taps.astype(BF)
     packed[TAPF : TAPF + 16, 0:fine] = gtapsf_ref[...].astype(BF)
     core = core_ref[0]
     half = TOTAL // 2
@@ -259,10 +263,11 @@
     packed[pl.ds(pl.multiple_of(core * half, half), half), :] = near_ref[...]
     packed[pl.ds(pl.multiple_of((1 - core) * half, half), half), :] = far_ref[...]
     chans = mixf_out.shape[0]
-    red_out[...] = packed[RED:MIXC, :].astype(F4) * coarse
-    mixc_out[...] = packed[MIXC:MIXF, :].astype(F4) * coarse
+    wide = mixc_out.shape[0]
+    red_out[...] = (packed[RED:MIXC, 0:wide].astype(F4) * coarse).T
+    mixc_out[...] = packed[MIXC:MIXF, 0:wide].astype(F4) * coarse
     mixf_out[...] = packed[MIXF:TAPC, 0:chans].astype(F4) * fine
-    taps = packed[TAPC:TAPF, :].astype(F4) * coarse
+    taps = packed[TAPC:TAPF, 0:wide].astype(F4) * coarse
     for a in range(5):
         tapsc_out[a] = taps[5 * a : 5 * a + 5]
     taps = packed[TAPF : TAPF + 16, 0:chans].astype(F4) * fine
@@ -292,7 +297,7 @@
             put(2 * i + p + 1, ddepth_ref[2 * p, i], ddepth_ref[2 * p + 1, i])
         return carry
 
-    lax.fori_loop(0, 16, fill, 0)
+    lax.fori_loop(0, 16, fill, 0, unroll=True)
 
     def conv(i, carry):
         found = {}
@@ -308,7 +313,7 @@
             out_ref[2 * i + p] = dot(weave, both).astype(BF)
         return carry
 
-    lax.fori_loop(0, 16, conv, 0)
+    lax.fori_loop(0, 16, conv, 0, unroll=2)
 
 
 def call(body, outs, scratch, flops, *operands):
@@ -336,58 +341,93 @@
     return jnp.where(even, away, near), jnp.where(even, near, away)
 
 
-def halos(coarse, fine_top, fine_bottom, fine_left, fine_right):
+def coarse_edges(coarse):
     height, breadth, wide = coarse.shape
-    chans = fine_top.shape[-1]
-
-    def widen(rows):
-        return jnp.pad(rows, ((0, 0), (0, wide - chans)))
-
-    first = jnp.concatenate([coarse[:4].reshape(4 * breadth, wide), widen(fine_top)], axis=0)
-    last = jnp.concatenate([coarse[-4:].reshape(4 * breadth, wide), widen(fine_bottom)], axis=0)
-    low, high = swap(first, last, ROWS)
-    split = 4 * breadth
-    top, bottom = low[:split].reshape(4, breadth, wide), high[:split].reshape(4, breadth, wide)
-    fine_low, fine_high = low[split:, :chans], high[split:, :chans]
-
-    def column(at, edge, pixels):
+    return coarse[:4].reshape(4 * breadth, wide), coarse[-4:].reshape(4 * breadth, wide)
+
+
+def coarse_columns(top, coarse, bottom):
+    breadth = coarse.shape[1]
+
+    def pick(at):
         parts = [
             jnp.concatenate([top[:, at + s], coarse[:, at + s], bottom[:, at + s]], axis=0)
             for s in range(4)
         ]
-        ends = [fine_low[edge : edge + 1], pixels, fine_high[edge : edge + 1]]
-        return jnp.concatenate(parts + [widen(jnp.concatenate(ends, axis=0))], axis=0)
-
+        return jnp.concatenate(parts, axis=0)
+
+    return pick(0), pick(breadth - 4)
+
+
+def coarse_sides(left, right):
+    wide = left.shape[1]
+
+    def spread(block):
+        return block.reshape(4, -1, wide).transpose(1, 0, 2)
+
+    return sides(spread(left), spread(right))
+
+
+def fine_columns(low, pixels_left, pixels_right, high):
+    end = low.shape[0] - 1
+    left = jnp.concatenate([low[:1], pixels_left, high[:1]], axis=0)
+    right = jnp.concatenate([low[end:], pixels_right, high[end:]], axis=0)
+    return left, right
+
+
+def fine_sides(left, right):
+    return sides(left[:, None], right[:, None])
+
+
+def stack_rows(coarse, fine):
+    widened = jnp.pad(fine, ((0, 0), (0, coarse.shape[1] - fine.shape[1])))
+    return jnp.concatenate([coarse, widened], axis=0)
+
+
+def input_halos(coarse, fine):
+    height, breadth, wide = coarse.shape
+    chans = fine.shape[-1]
+    first, last = coarse_edges(coarse)
+    split = 4 * breadth
+    low, high = swap(stack_rows(first, fine[0]), stack_rows(last, fine[-1]), ROWS)
+    top, bottom = low[:split].reshape(4, breadth, wide), high[:split].reshape(4, breadth, wide)
+    fine_low, fine_high = low[split:, :chans], high[split:, :chans]
+    coarse_first, coarse_last = coarse_columns(top, coarse, bottom)
+    fine_first, fine_last = fine_columns(fine_low, fine[:, 0], fine[:, -1], fine_high)
     left, right = swap(
-        column(0, 0, fine_left),
-        column(breadth - 4, fine_low.shape[0] - 1, fine_right),
-        COLS,
-    )
-    tall = height + 8
-
-    def spread(block):
-        return block[: 4 * tall].reshape(4, tall, wide).transpose(1, 0, 2)
-
-    sides_coarse = sides(spread(left), spread(right))
-    sides_fine = sides(left[4 * tall :, None, :chans], right[4 * tall :, None, :chans])
-    return top, bottom, sides_coarse, fine_low, fine_high, sides_fine
-
-
-def reduce_terms(mine, other):
-    total, wide = mine.shape
+        stack_rows(coarse_first, fine_first), stack_rows(coarse_last, fine_last), COLS
+    )
+    split = 4 * (height + 8)
+    side_coarse = coarse_sides(left[:split], right[:split])
+    side_fine = fine_sides(left[split:, :chans], right[split:, :chans])
+    return top, bottom, side_coarse, fine_low, fine_high, side_fine
+
+
+def hold(value, *others):
+    return lax.optimization_barrier((value, *others))[0]
+
+
+def reduce_terms(mine, other, rows_step, columns_step, last_step):
+    total, lanes = mine.shape
     core = lax.axis_index("core")
     plane = lax.axis_size(PLANE)
     depth = lax.axis_size("z")
     trade = [(0, 1), (1, 0)]
-    mine = mine.astype(F4) + lax.ppermute(other, "core", trade).astype(F4)
+    mine = mine + lax.ppermute(other, "core", trade)
     chunk = total // plane
-    got = lax.all_to_all(mine.astype(BF).reshape(plane, chunk, wide), PLANE, 0, 0, tiled=True)
+    mine = mine.reshape(plane, chunk, lanes)
+    edges = rows_step(mine)
+    got = lax.all_to_all(mine, PLANE, 0, 0, tiled=True)
     mine = jnp.sum(got.astype(F4), axis=0).astype(BF)
-    got = lax.all_to_all(jnp.broadcast_to(mine, (depth, chunk, wide)), "z", 0, 0, tiled=True)
+    mine, edges = lax.optimization_barrier((mine, edges))
+    edges = columns_step(edges)
+    got = lax.all_to_all(jnp.broadcast_to(mine, (depth, chunk, lanes)), "z", 0, 0, tiled=True)
     mine = jnp.sum(got.astype(F4), axis=0).astype(BF)
-    got = lax.all_to_all(jnp.broadcast_to(mine, (plane, chunk, wide)), PLANE, 0, 0, tiled=True)
-    got = got.reshape(total, wide)
-    return got, lax.ppermute(got, "core", trade)
+    mine, edges = lax.optimization_barrier((mine, edges))
+    extra = last_step(edges)
+    got = lax.all_to_all(jnp.broadcast_to(mine, (plane, chunk, lanes)), PLANE, 0, 0, tiled=True)
+    got, extra = lax.optimization_barrier((got.reshape(total, lanes), extra))
+    return got, lax.ppermute(got, "core", trade), extra
 
 
 def sides(left, right):
@@ -402,9 +442,7 @@
     scale_fine = float(height * breadth * devices_all) ** (-0.5)
     scale_coarse = float(height * breadth // 4 * devices_all) ** (-0.5)
     core = lax.axis_index("core").astype(jnp.int32).reshape(1)
-    ctop, cbottom, clr, top, bottom, lr = halos(
-        cotangent, slide_pixels[0], slide_pixels[-1], slide_pixels[:, 0], slide_pixels[:, -1]
-    )
+    ctop, cbottom, clr, top, bottom, lr = input_halos(cotangent, slide_pixels)
     top, bottom = top[None], bottom[None]
 
     slide, depth, pre, reduced, act = call(
@@ -422,72 +460,85 @@
     )
     reduced = reduced.reshape(16, 32, wide)
 
-    delta_coarse, dfine, ddepth, term_reduce, term_mix_fine, term_taps_fine = call(
-        backward,
+    delta_coarse, delta_reduced = call(
+        coarse_backward,
+        [((16, 32, wide), BF), ((16, 32, wide), BF)],
+        [((24, 32, wide), BF), ((24, 16, wide), BF), ((5, 24, 32, wide), F4)],
+        8_000_000_000,
+        cotangent, jnp.concatenate([ctop, cbottom], axis=0), clr, mix_coarse, taps_coarse, reduced,
+    )
+    arows = swap(*coarse_edges(act), ROWS)
+    arows, delta_reduced = lax.optimization_barrier((arows, delta_reduced))
+    atop, abottom = (block.reshape(4, 32, wide) for block in arows)
+    acolumns = swap(*coarse_columns(atop, act, abottom), COLS)
+    dfine, ddepth, term_reduce, term_mix_fine, term_taps_fine = call(
+        fine_terms,
         [
-            ((16, 32, wide), BF),
             ((4, 16, 32, chans), BF),
             ((4, 16, 32, chans), BF),
             ((4 * chans, wide), BF),
             ((chans, chans), F4),
             ((16, chans), F4),
         ],
-        [
-            ((24, 32, wide), BF),
-            ((24, 16, wide), BF),
-            ((5, 24, 32, wide), F4),
-            ((16, 32, wide), BF),
-            ((4, 34, 32, chans), F4),
-        ],
+        [((4, 34, 32, chans), F4)],
         8_000_000_000,
-        cotangent, jnp.concatenate([ctop, cbottom], axis=0), clr, mix_coarse, taps_coarse, reduced, pre,
-        depth.reshape(4, 512, chans), reduce_weight, mix_fine, slide_pixels, top, bottom, lr,
-    )
-
-    inner = ddepth.reshape(2, 2, 16, 32, chans)
-    atop, abottom, alr, dtop, dbottom, dlr = halos(
-        act,
-        ddepth[:2, 0].reshape(breadth, chans),
-        ddepth[2:, 15].reshape(breadth, chans),
-        inner[:, 0, :, 0].transpose(1, 0, 2).reshape(height, chans),
-        inner[:, 1, :, 31].transpose(1, 0, 2).reshape(height, chans),
-    )
+        delta_reduced.reshape(512, wide), pre, depth.reshape(4, 512, chans), reduce_weight, mix_fine,
+        slide_pixels, top, bottom, lr,
+    )
+    acolumns, ddepth = lax.optimization_barrier((acolumns, ddepth))
+    alr = coarse_sides(*acolumns)
     section_out, mine, other = call(
         coarse_forward,
-        [((16, 32, wide), BF), ((TOTAL // 2, wide), BF), ((TOTAL // 2, wide), BF)],
+        [((16, 32, wide), BF), ((TOTAL // 2, LANES), BF), ((TOTAL // 2, LANES), BF)],
         [
             ((5, 24, 32, wide), F4),
             ((25, 8, wide), F4),
             ((16, 32, wide), BF),
             ((24, 32, wide), BF),
-            ((TOTAL, wide), BF),
+            ((TOTAL, LANES), BF),
         ],
         4_000_000_000,
         act, atop, abottom, alr, taps_coarse, mix_coarse, reduced, cotangent, delta_coarse,
         term_reduce, term_mix_fine, term_taps_fine, core,
     )
-    (pixel_grad,) = call(
-        fine_backward,
-        [((height, breadth, chans), BF)],
-        [((4, 34, 32, chans), F4)],
-        2_000_000_000,
-        ddepth, dtop.reshape(2, 32, chans), dbottom.reshape(2, 32, chans), dlr, taps_fine, dfine, slide,
-    )
-    near, far = reduce_terms(mine, other)
+    def rows_step(after):
+        edges = ddepth[:2, 0].reshape(breadth, chans), ddepth[2:, 15].reshape(breadth, chans)
+        return swap(*hold(edges, after), ROWS)
+
+    def columns_step(edges):
+        inner = ddepth.reshape(2, 2, 16, 32, chans)
+        left = inner[:, 0, :, 0].transpose(1, 0, 2).reshape(height, chans)
+        right = inner[:, 1, :, 31].transpose(1, 0, 2).reshape(height, chans)
+        low, high = edges
+        return low, high, *swap(*fine_columns(low, left, right, high), COLS)
+
+    def last_step(edges):
+        low, high, left, right = edges
+        return call(
+            fine_backward,
+            [((height, breadth, chans), BF)],
+            [((4, 34, 32, chans), F4)],
+            2_000_000_000,
+            ddepth, low.reshape(2, 32, chans), high.reshape(2, 32, chans), fine_sides(left, right),
+            taps_fine, dfine, slide,
+        )[0]
+
+    near, far, pixel_grad = reduce_terms(mine, other, rows_step, columns_step, last_step)
     grads = call(
         functools.partial(unpack, fine=scale_fine, coarse=scale_coarse),
         [
             ((3, 3, chans), F4),
             ((chans, chans), F4),
-            ((4 * chans, wide), F4),
+            ((wide, 4 * chans), F4),
             ((5, 5, wide), F4),
             ((wide, wide), F4),
         ],
-        [((TOTAL, wide), BF)],
+        [((TOTAL, LANES), BF)],
         1_000_000,
         near, far, core,
     )
-    return (section_out, pixel_grad, *grads)
+    tapsf, mixf, red, tapsc, mixc = grads
+    return (section_out, pixel_grad, tapsf, mixf, red.T, tapsc, mixc)
 
 
 def solution(mesh):

time: 173 us -> 147 us (0.85)
  blocking collectives: 43.4 us -> 0 us
  starting transfers between devices: 29 us -> 55.9 us
  Pallas kernels: 53 us -> 40.9 us
  waiting for transfers between devices: 21.6 us -> 27.3 us
  local copies, waits for them, and re-layouts: 18.6 us -> 13.3 us
  other arithmetic: 4.87 us -> 7.77 us
    all_to_all x2 -> x0, blocking collectives: 43.4 us -> none  [the longest x1 27.1 us: reduce_terms(): lax.all_to_all(mine.astype(BF).reshape(plane, chunk, wide), PLANE, 0, 0,...]
    all_to_all x1 -> x3, starting transfers between devices: 5.21 us -> 23 us  [the longest x1 9.88 us: reduce_terms(): got = lax.all_to_all(mine, PLANE, 0, 0, tiled=True)]
    pallas_call x5 -> x6, Pallas kernels: 53 us -> 40.9 us  [call(): pl.pallas_call(body, out_shape=[jax.ShapeDtypeStruct(shape, kind) for sha...]
    ppermute x4 -> x6, starting transfers between devices: 7.52 us -> 13.6 us  [swap(): away = lax.ppermute(jnp.where(even, first, last), axes, far)]
    all_to_all x1 -> x3, waiting for transfers between devices: 10.2 us -> 15.6 us  [the longest x1 5.91 us: reduce_terms(): got = lax.all_to_all(mine, PLANE, 0, 0, tiled=True)]
    ppermute x4 -> x6, waiting for transfers between devices: 5.14 us -> 1.71 us  [swap(): away = lax.ppermute(jnp.where(even, first, last), axes, far)]
    ppermute x4 -> x6, starting transfers between devices: 12.3 us -> 15.5 us  [swap(): lax.ppermute(jnp.where(even, last, first), axes, [(i, i ^ 1) for i in ran...]
    add x0 -> x1, other arithmetic: none -> 2.22 us  [reduce_terms(): mine = mine + lax.ppermute(other, 'core', trade)]
  transfers between devices with their start and end apart: 11 -> 17, of which waited for: 6 -> 9; matrix products, arithmetic and copies ran while one was open for 3% -> 5% of each run, Pallas kernels for 5% -> 15%
where the time goes in v2:
time: 147 us
  starting transfers between devices  55.9 us (38%)
  Pallas kernels  40.9 us (28%)
  waiting for transfers between devices  27.3 us (19%)
  local copies, waits for them, and re-layouts  13.3 us (9%)
  other arithmetic  7.77 us (5%)
    pallas_call x6, Pallas kernels, call(): pl.pallas_call(body, out_shape=[jax.ShapeDtypeStruct(shape, kind) for sha...  40.9 us
    ppermute x6, starting transfers between devices, swap(): lax.ppermute(jnp.where(even, last, first), axes, [(i, i ^ 1) for i in ran...  15.5 us
    ppermute x6, starting transfers between devices, swap(): away = lax.ppermute(jnp.where(even, first, last), axes, far)  13.6 us
    all_to_all x1, starting transfers between devices, reduce_terms(): got = lax.all_to_all(mine, PLANE, 0, 0, tiled=True)  9.88 us
    all_to_all x1, starting transfers between devices, reduce_terms(): lax.all_to_all(jnp.broadcast_to(mine, (plane, chunk, lanes)), PLANE, 0, 0...  9.13 us
    all_to_all x1, waiting for transfers between devices, reduce_terms(): got = lax.all_to_all(mine, PLANE, 0, 0, tiled=True)  5.91 us
    ppermute x6, waiting for transfers between devices, swap(): lax.ppermute(jnp.where(even, last, first), axes, [(i, i ^ 1) for i in ran...  5.87 us
    all_to_all x1, waiting for transfers between devices, reduce_terms(): lax.all_to_all(jnp.broadcast_to(mine, (plane, chunk, lanes)), PLANE, 0, 0...  5.69 us
  transfers between devices with their start and end apart: 17, of which 9 were waited for; matrix products, arithmetic and copies ran while one was open for 5% of the time, Pallas kernels for 15%

profile of v2, /device:TPU:1, one launch (start us, length us, event | category | flops | bytes accessed | tf_op | source)
XLA Modules:
  0.0 146.6 jit_solution(9676105588522593029)
XLA Ops:
  0.7 1.1 fusion.31
  1.8 0.8 slice_bitcast_fusion.3
  2.5 0.1 broadcast_select_fusion.2
  2.6 4.6 %collective-permute-start = (bf16[192,416]{1,0:T(8,128)(2,1)S(1)}, bf16[192,416]{1,0:T(8,128)(2,1)S(1)}, u32[]{:S(2)}, u32[]{:S(2)}) collective-permute-start(bf16[192,416]{1,0:T(8,128)(2,1)S(1)} %get-tuple-element.114), channel_id=1, source_target_pairs={{64,128},{128,64},{65,129},{129,65},{66,130},{130,66},{67,131},{13... | collective-permute-start | bytes 479240 | tf_op jit(solution)/shard_map/ppermute | solution.py:340
  7.2 0.1 collective-permute-start.1
  7.3 1.0 fusion.28
  8.3 0.2 fusion.30
  8.6 1.5 %copy.286.weight_ref = bf16[832,416]{1,0:T(8,128)(2,1)} copy(bf16[832,416]{0,1:T(8,128)(2,1)S(1)} %copy-done.2) | data formatting | bytes 1384448 | tf_op args[3]
  10.2 0.3 collective-permute-done
  10.6 0.6 slice_bitcast_fusion
  11.3 0.1 fusion.36
  11.3 0.1 fusion.37
  11.5 0.6 concatenate.50
  12.1 0.6 concatenate.48
  12.8 0.7 collective-permute-start.2
  13.5 4.6 %collective-permute-start.3 = (bf16[130,416]{1,0:T(8,128)(2,1)S(1)}, bf16[130,416]{1,0:T(8,128)(2,1)S(1)}, u32[]{:S(2)}, u32[]{:S(2)}) collective-permute-start(bf16[130,416]{1,0:T(8,128)(2,1)S(1)} %get-tuple-element.118), channel_id=1, source_target_pairs={{0,1},{1,0},{2,3},{3,2},{4,5},{5,4},{6,7},{7,6},{8,9},{9,8},{10,11... | collective-permute-start | bytes 324488 | tf_op jit(solution)/shard_map/ppermute | solution.py:337
  18.1 0.7 pad_maximum_fusion.tb_ref
  18.8 2.9 %collective-permute-done.3 = bf16[130,416]{1,0:T(8,128)(2,1)S(1)} collective-permute-done((bf16[130,416]{1,0:T(8,128)(2,1)S(1)}, bf16[130,416]{1,0:T(8,128)(2,1)S(1)}, u32[]{:S(2)}, u32[]{:S(2)}) %collective-permute-start.3) | collective-permute-done | bytes 108192 | tf_op jit(solution)/shard_map/ppermute | solution.py:337
  21.9 0.1 copy.408
  21.9 0.1 copy.409
  22.0 0.8 fusion.12.lr_ref.lrf_ref
  22.8 6.4 %shard_map.126 = (bf16[4,16,32,208]{3,2,1,0:T(8,128)(2,1)}, bf16[4,16,32,208]{3,2,1,0:T(8,128)(2,1)}, bf16[4,512,208]{2,1,0:T(8,128)(2,1)}, bf16[512,416]{1,0:T(8,128)(2,1)}, bf16[16,32,416]{2,1,0:T(8,128)(2,1)}) custom-call(bf16[32,64,208]{2,1,0:T(8,128)(2,1)} %slide_ref.3, bf16[1,64,208]{2,1,0:T(8,128)(2,1)} %get-tuple-element.174.top_ref, ...), custom_call_target="tpu_custom_call" | custom-call | flops 4000000000 | bytes 8000000 | tf_op jit(solution)/shard_map/pallas_call | solution.py:323
  29.2 1.0 broadcast_select_fusion.8
  30.2 3.6 %collective-permute-start.4 = (bf16[128,416]{1,0:T(8,128)(2,1)S(1)}, bf16[128,416]{1,0:T(8,128)(2,1)S(1)}, u32[]{:S(2)}, u32[]{:S(2)}) collective-permute-start(bf16[128,416]{1,0:T(8,128)(2,1)S(1)} %bitcast.205), channel_id=1, source_target_pairs={{64,128},{128,64},{65,129},{129,65},{66,130},{130,66},{67,131},{13... | collective-permute-start | bytes 319496 | tf_op jit(solution)/shard_map/ppermute | solution.py:340
  33.8 0.1 collective-permute-start.5
  33.9 0.9 fusion.8.lr_ref
  34.7 6.6 %shard_map.127 = (bf16[16,32,416]{2,1,0:T(8,128)(2,1)}, bf16[16,32,416]{2,1,0:T(8,128)(2,1)}) custom-call(bf16[16,32,416]{2,1,0:T(8,128)(2,1)} %cot_ref.3, bf16[8,32,416]{2,1,0:T(8,128)(2,1)} %pad_maximum_fusion.tb_ref, bf16[24,16,416]{2,1,0:T(8,128)(2,1)} %fusion.8.lr_ref, bf16[416,416]{1,0:T(8,128)(2,1)} %mix_ref.5, f32[5,5,416]{2,1,0:T(8,128)} %taps_ref.4, ...), custom_call_target="tpu_custom_call" | custom-call | flops 8000000000 | bytes 8000000 | tf_op jit(solution)/shard_map/pallas_call | solution.py:323
  41.4 0.2 fusion.29
  41.8 0.1 fusion.34
  41.8 0.1 fusion.35
  42.1 0.6 concatenate.54
  42.7 0.6 concatenate.55
  43.4 0.7 collective-permute-start.6
  44.0 6.0 %collective-permute-start.7 = (bf16[96,416]{1,0:T(8,128)(2,1)S(1)}, bf16[96,416]{1,0:T(8,128)(2,1)S(1)}, u32[]{:S(2)}, u32[]{:S(2)}) collective-permute-start(bf16[96,416]{1,0:T(8,128)(2,1)S(1)} %get-tuple-element.123), channel_id=1, source_target_pairs={{0,1},{1,0},{2,3},{3,2},{4,5},{5,4},{6,7},{7,6},{8,9},{9,8},{10,11... | collective-permute-start | bytes 239624 | tf_op jit(solution)/shard_map/ppermute | solution.py:337
  50.0 9.1 %shard_map.128 = (bf16[4,16,32,208]{3,2,1,0:T(8,128)(2,1)}, bf16[4,16,32,208]{3,2,1,0:T(8,128)(2,1)}, bf16[832,416]{1,0:T(8,128)(2,1)}, f32[208,208]{1,0:T(8,128)}, f32[16,208]{1,0:T(8,128)}) custom-call(bf16[512,416]{1,0:T(8,128)(2,1)} %bitcast.243, bf16[4,512,208]{2,1,0:T(8,128)(2,1)} %get-tuple-element.51.pre_ref, bf16[4,512,208]{2,1,0:T(8,128)(2,1)} %bitcast.240, ...), custom_call_target="tpu_custom_call" | custom-call | flops 8000000000 | bytes 8000000 | tf_op jit(solution)/shard_map/pallas_call | solution.py:323
  59.3 0.9 fusion.9.lr_ref
  60.2 9.0 %shard_map.129 = (bf16[16,32,416]{2,1,0:T(8,128)(2,1)}, bf16[768,512]{1,0:T(8,128)(2,1)}, bf16[768,512]{1,0:T(8,128)(2,1)}) custom-call(bf16[16,32,416]{2,1,0:T(8,128)(2,1)} %get-tuple-element.45.act_ref, bf16[4,32,416]{2,1,0:T(8,128)(2,1)} %bitcast.203, bf16[4,32,416]{2,1,0:T(8,128)(2,1)} %bitcast.201, bf16[24,16,416]{2,1,0:T(8,128)(2,1)} %fusion.9.lr_ref, ...), custom_call_target="tpu_custom_call" | custom-call | flops 4000000000 | bytes 8000000 | tf_op jit(solution)/shard_map/pallas_call | solution.py:323
  69.2 1.0 collective-permute-start.8
  70.3 2.1 %collective-permute-done.8 = bf16[768,512]{1,0:T(8,128)(2,1)S(1)} collective-permute-done((bf16[768,512]{1,0:T(8,128)(2,1)}, bf16[768,512]{1,0:T(8,128)(2,1)S(1)}, u32[]{:S(2)}, u32[]{:S(2)}) %collective-permute-start.8) | collective-permute-done | bytes 786464 | tf_op jit(solution)/shard_map/ppermute | solution.py:416
  72.4 2.2 %add.50 = bf16[768,512]{1,0:T(8,128)(2,1)} add(bf16[768,512]{1,0:T(8,128)(2,1)} %get-tuple-element.61, bf16[768,512]{1,0:T(8,128)(2,1)S(1)} %collective-permute-done.8) | non-fusion elementwise | flops 393216 | bytes 2359296 | tf_op jit(solution)/shard_map/add | solution.py:416
  74.6 9.9 %all-to-all-start = ((bf16[16,48,512]{2,1,0:T(8,128)(2,1)}), bf16[16,48,512]{2,1,0:T(8,128)(2,1)S(1)}, u32[]{:S(2)}, u32[]{:S(2)}) async-start(bf16[16,48,512]{2,1,0:T(8,128)(2,1)} %bitcast.36), calls=%async_computation | async-start | bytes 1572864 | tf_op jit(solution)/shard_map/all_to_all | solution.py:420
  84.5 0.8 fusion.27
  85.3 0.7 collective-permute-start.10
  86.0 3.5 %collective-permute-start.9 = (bf16[64,208]{1,0:T(8,128)(2,1)S(1)}, bf16[64,208]{1,0:T(8,128)(2,1)S(1)}, u32[]{:S(2)}, u32[]{:S(2)}) collective-permute-start(bf16[64,208]{1,0:T(8,128)(2,1)S(1)} %get-tuple-element.164), channel_id=1, source_target_pairs={{64,128},{128,64},{65,129},{129,65},{66,130},{130,66},{67,131},{13... | collective-permute-start | bytes 79880 | tf_op jit(solution)/shard_map/ppermute | solution.py:340
  89.5 1.0 fusion.26
  90.7 1.4 collective-permute-done.9
  92.1 5.9 %all-to-all-done = bf16[16,48,512]{2,1,0:T(8,128)(2,1)S(1)} async-done(((bf16[16,48,512]{2,1,0:T(8,128)(2,1)}), bf16[16,48,512]{2,1,0:T(8,128)(2,1)S(1)}, u32[]{:S(2)}, u32[]{:S(2)}) %all-to-all-start) | async-done | bytes 786464 | tf_op jit(solution)/shard_map/all_to_all | solution.py:420
  98.0 0.1 reduce_sum.24
  98.1 0.8 broadcast_in_dim.28
  98.9 4.0 %all-to-all-start.1 = ((bf16[8,48,512]{2,1,0:T(8,128)(2,1)}), bf16[8,48,512]{2,1,0:T(8,128)(2,1)S(1)}, u32[]{:S(2)}, u32[]{:S(2)}) async-start(bf16[8,48,512]{2,1,0:T(8,128)(2,1)} %broadcast_in_dim.28), calls=%async_computation.1 | async-start | bytes 786432 | tf_op jit(solution)/shard_map/all_to_all | solution.py:424
  102.9 0.7 collective-permute-start.11
  103.6 4.0 %collective-permute-start.12 = (bf16[34,208]{1,0:T(8,128)(2,1)S(1)}, bf16[34,208]{1,0:T(8,128)(2,1)S(1)}, u32[]{:S(2)}, u32[]{:S(2)}) collective-permute-start(bf16[34,208]{1,0:T(8,128)(2,1)S(1)} %get-tuple-element.167), channel_id=1, source_target_pairs={{0,1},{1,0},{2,3},{3,2},{4,5},{5,4},{6,7},{7,6},{8,9},{9,8},{10,11... | collective-permute-start | bytes 42440 | tf_op jit(solution)/shard_map/ppermute | solution.py:337
  107.5 2.9 %collective-permute-done.12 = bf16[34,208]{1,0:T(8,128)(2,1)S(1)} collective-permute-done((bf16[34,208]{1,0:T(8,128)(2,1)S(1)}, bf16[34,208]{1,0:T(8,128)(2,1)S(1)}, u32[]{:S(2)}, u32[]{:S(2)}) %collective-permute-start.12) | collective-permute-done | bytes 14176 | tf_op jit(solution)/shard_map/ppermute | solution.py:337
  110.5 4.0 %all-to-all-done.1 = bf16[8,48,512]{2,1,0:T(8,128)(2,1)S(1)} async-done(((bf16[8,48,512]{2,1,0:T(8,128)(2,1)}), bf16[8,48,512]{2,1,0:T(8,128)(2,1)S(1)}, u32[]{:S(2)}, u32[]{:S(2)}) %all-to-all-start.1) | async-done | bytes 393248 | tf_op jit(solution)/shard_map/all_to_all | solution.py:424
  114.5 0.1 reduce_sum.25
  114.6 1.0 broadcast_in_dim.29
  115.6 9.1 %all-to-all-start.2 = ((bf16[16,48,512]{2,1,0:T(8,128)(2,1)}), bf16[16,48,512]{2,1,0:T(8,128)(2,1)S(1)}, u32[]{:S(2)}, u32[]{:S(2)}) async-start(bf16[16,48,512]{2,1,0:T(8,128)(2,1)} %broadcast_in_dim.29), calls=%async_computation.2 | async-start | bytes 1572864 | tf_op jit(solution)/shard_map/all_to_all | solution.py:428
  124.8 0.8 fusion.13.lr_ref
  125.6 6.3 %shard_map.130 = bf16[32,64,208]{2,1,0:T(8,128)(2,1)} custom-call(bf16[4,16,32,208]{3,2,1,0:T(8,128)(2,1)} %get-tuple-element.63.ddepth_ref, bf16[2,32,208]{2,1,0:T(8,128)(2,1)} %bitcast.221, bf16[2,32,208]{2,1,0:T(8,128)(2,1)} %bitcast.220, bf16[34,16,208]{2,1,0:T(8,128)(2,1)} %fusion.13.lr_ref, f32[3,3,208]{2,1,0:T(4,128)} %taps_ref.5, ...), custom_call_target="tpu_custom_call" | custom-call | flops 2000000000 | bytes 8000000 | tf_op jit(solution)/shard_map/pallas_call | solution.py:323
  131.9 5.7 %all-to-all-done.2 = bf16[16,48,512]{2,1,0:T(8,128)(2,1)S(1)} async-done(((bf16[16,48,512]{2,1,0:T(8,128)(2,1)}), bf16[16,48,512]{2,1,0:T(8,128)(2,1)S(1)}, u32[]{:S(2)}, u32[]{:S(2)}) %all-to-all-start.2) | async-done | bytes 786464 | tf_op jit(solution)/shard_map/all_to_all | solution.py:428
  137.6 2.8 %collective-permute-start.13 = (bf16[768,512]{1,0:T(8,128)(2,1)S(1)}, bf16[768,512]{1,0:T(8,128)(2,1)S(1)}, u32[]{:S(2)}, u32[]{:S(2)}) collective-permute-start(bf16[768,512]{1,0:T(8,128)(2,1)S(1)} %bitcast.184), channel_id=1, source_target_pairs={{0,64},{64,0},{1,65},{65,1},{2,66},{66,2},{3,67},{67,3},{4,68},{68... | collective-permute-start | bytes 2359304 | tf_op jit(solution)/shard_map/ppermute | solution.py:430
  140.3 1.9 %collective-permute-done.13.far_ref = bf16[768,512]{1,0:T(8,128)(2,1)S(1)} collective-permute-done((bf16[768,512]{1,0:T(8,128)(2,1)S(1)}, bf16[768,512]{1,0:T(8,128)(2,1)S(1)}, u32[]{:S(2)}, u32[]{:S(2)}) %collective-permute-start.13) | collective-permute-done | bytes 786464 | tf_op jit(solution)/shard_map/ppermute | solution.py:430
  142.3 0.9 copy-done.1
  143.1 3.5 %shard_map.131 = (f32[3,3,208]{2,1,0:T(4,128)}, f32[208,208]{1,0:T(8,128)}, f32[416,832]{1,0:T(8,128)}, f32[5,5,416]{2,1,0:T(8,128)}, f32[416,416]{1,0:T(8,128)}) custom-call(bf16[768,512]{1,0:T(8,128)(2,1)} %bitcast.185, bf16[768,512]{1,0:T(8,128)(2,1)} %copy-done.1, s32[1]{0:T(128)} %bitcast.35.core_ref), custom_call_target="tpu_custom_call" | custom-call | flops 1000000 | bytes 8000000 | tf_op jit(solution)/shard_map/pallas_call | solution.py:323
  (95 shorter events, 0.9 us)
Async XLA Ops:
  0.6 7.7 %copy-start.4 = (bf16[16,32,416]{2,1,0:T(8,128)(2,1)S(1)}, bf16[16,32,416]{2,1,0:T(8,128)(2,1)}, u32[]{:S(2)}) copy-start(bf16[16,32,416]{2,1,0:T(8,128)(2,1)} %cot_ref.3) | copy-start | bytes 1277956
  0.6 8.0 %copy-start.2 = (bf16[832,416]{0,1:T(8,128)(2,1)S(1)}, bf16[832,416]{0,1:T(8,128)(2,1)}, u32[]{:S(2)}) copy-start(bf16[832,416]{0,1:T(8,128)(2,1)} %param.10) | copy-start | bytes 2076676
  2.6 7.9 %collective-permute-start = (bf16[192,416]{1,0:T(8,128)(2,1)S(1)}, bf16[192,416]{1,0:T(8,128)(2,1)S(1)}, u32[]{:S(2)}, u32[]{:S(2)}) collective-permute-start(bf16[192,416]{1,0:T(8,128)(2,1)S(1)} %get-tuple-element.114), channel_id=1, source_target_pairs={{64,128},{128,64},{65,129},{129,65},{66,130},{130,66},{67,131},{13... | collective-permute-start | bytes 479240 | tf_op jit(solution)/shard_map/ppermute | solution.py:340
  7.2 3.3 %collective-permute-start.1 = (bf16[192,416]{1,0:T(8,128)(2,1)S(1)}, bf16[192,416]{1,0:T(8,128)(2,1)S(1)}, u32[]{:S(2)}, u32[]{:S(2)}) collective-permute-start(bf16[192,416]{1,0:T(8,128)(2,1)S(1)} %get-tuple-element.113), channel_id=1, source_target_pairs={{0,64},{64,0},{128,192},{192,128},{1,65},{65,1},{129,193},{193,129... | collective-permute-start | bytes 479240 | tf_op jit(solution)/shard_map/ppermute | solution.py:337
  12.8 6.0 %collective-permute-start.2 = (bf16[130,416]{1,0:T(8,128)(2,1)S(1)}, bf16[130,416]{1,0:T(8,128)(2,1)S(1)}, u32[]{:S(2)}, u32[]{:S(2)}) collective-permute-start(bf16[130,416]{1,0:T(8,128)(2,1)S(1)} %get-tuple-element.117), channel_id=1, source_target_pairs={{1,2},{3,4},{5,6},{7,8},{9,10},{11,12},{13,14},{15,16},{17,18},{19... | collective-permute-start | bytes 324488 | tf_op jit(solution)/shard_map/ppermute | solution.py:340
  13.5 8.3 %collective-permute-start.3 = (bf16[130,416]{1,0:T(8,128)(2,1)S(1)}, bf16[130,416]{1,0:T(8,128)(2,1)S(1)}, u32[]{:S(2)}, u32[]{:S(2)}) collective-permute-start(bf16[130,416]{1,0:T(8,128)(2,1)S(1)} %get-tuple-element.118), channel_id=1, source_target_pairs={{0,1},{1,0},{2,3},{3,2},{4,5},{5,4},{6,7},{7,6},{8,9},{9,8},{10,11... | collective-permute-start | bytes 324488 | tf_op jit(solution)/shard_map/ppermute | solution.py:337
  30.2 11.5 %collective-permute-start.4 = (bf16[128,416]{1,0:T(8,128)(2,1)S(1)}, bf16[128,416]{1,0:T(8,128)(2,1)S(1)}, u32[]{:S(2)}, u32[]{:S(2)}) collective-permute-start(bf16[128,416]{1,0:T(8,128)(2,1)S(1)} %bitcast.205), channel_id=1, source_target_pairs={{64,128},{128,64},{65,129},{129,65},{66,130},{130,66},{67,131},{13... | collective-permute-start | bytes 319496 | tf_op jit(solution)/shard_map/ppermute | solution.py:340
  33.8 7.9 %collective-permute-start.5 = (bf16[128,416]{1,0:T(8,128)(2,1)S(1)}, bf16[128,416]{1,0:T(8,128)(2,1)S(1)}, u32[]{:S(2)}, u32[]{:S(2)}) collective-permute-start(bf16[128,416]{1,0:T(8,128)(2,1)S(1)} %bitcast.204), channel_id=1, source_target_pairs={{0,64},{64,0},{128,192},{192,128},{1,65},{65,1},{129,193},{193,129... | collective-permute-start | bytes 319496 | tf_op jit(solution)/shard_map/ppermute | solution.py:337
  34.7 6.6 %copy-start.3 = (bf16[16,32,416]{2,1,0:T(8,128)(2,1)S(1)}, bf16[16,32,416]{2,1,0:T(8,128)(2,1)}, u32[]{:S(2)}) copy-start(bf16[16,32,416]{2,1,0:T(8,128)(2,1)} %get-tuple-element.45.act_ref) | copy-start | bytes 1277956
  41.8 17.4 %copy-start.5 = (bf16[128,416]{1,0:T(8,128)(2,1)}, bf16[128,416]{1,0:T(8,128)(2,1)S(1)}, u32[]{:S(2)}) copy-start(bf16[128,416]{1,0:T(8,128)(2,1)S(1)} %get-tuple-element.49) | copy-start | bytes 319492
  41.8 17.4 %copy-start.6 = (bf16[128,416]{1,0:T(8,128)(2,1)}, bf16[128,416]{1,0:T(8,128)(2,1)S(1)}, u32[]{:S(2)}) copy-start(bf16[128,416]{1,0:T(8,128)(2,1)S(1)} %get-tuple-element.48) | copy-start | bytes 319492
  43.4 15.8 %collective-permute-start.6 = (bf16[96,416]{1,0:T(8,128)(2,1)S(1)}, bf16[96,416]{1,0:T(8,128)(2,1)S(1)}, u32[]{:S(2)}, u32[]{:S(2)}) collective-permute-start(bf16[96,416]{1,0:T(8,128)(2,1)S(1)} %get-tuple-element.124), channel_id=1, source_target_pairs={{1,2},{3,4},{5,6},{7,8},{9,10},{11,12},{13,14},{15,16},{17,18},{19... | collective-permute-start | bytes 239624 | tf_op jit(solution)/shard_map/ppermute | solution.py:340
  44.0 15.1 %collective-permute-start.7 = (bf16[96,416]{1,0:T(8,128)(2,1)S(1)}, bf16[96,416]{1,0:T(8,128)(2,1)S(1)}, u32[]{:S(2)}, u32[]{:S(2)}) collective-permute-start(bf16[96,416]{1,0:T(8,128)(2,1)S(1)} %get-tuple-element.123), channel_id=1, source_target_pairs={{0,1},{1,0},{2,3},{3,2},{4,5},{5,4},{6,7},{7,6},{8,9},{9,8},{10,11... | collective-permute-start | bytes 239624 | tf_op jit(solution)/shard_map/ppermute | solution.py:337
  69.2 3.2 %collective-permute-start.8 = (bf16[768,512]{1,0:T(8,128)(2,1)}, bf16[768,512]{1,0:T(8,128)(2,1)S(1)}, u32[]{:S(2)}, u32[]{:S(2)}) collective-permute-start(bf16[768,512]{1,0:T(8,128)(2,1)} %get-tuple-element.62), channel_id=1, source_target_pairs={{0,64},{64,0},{1,65},{65,1},{2,66},{66,2},{3,67},{67,3},{4,68},{68... | collective-permute-start | bytes 2359304 | tf_op jit(solution)/shard_map/ppermute | solution.py:416
  74.6 23.4 %all-to-all-start = ((bf16[16,48,512]{2,1,0:T(8,128)(2,1)}), bf16[16,48,512]{2,1,0:T(8,128)(2,1)S(1)}, u32[]{:S(2)}, u32[]{:S(2)}) async-start(bf16[16,48,512]{2,1,0:T(8,128)(2,1)} %bitcast.36), calls=%async_computation | async-start | bytes 1572864 | tf_op jit(solution)/shard_map/all_to_all | solution.py:420
  85.3 5.4 %collective-permute-start.10 = (bf16[64,208]{1,0:T(8,128)(2,1)S(1)}, bf16[64,208]{1,0:T(8,128)(2,1)S(1)}, u32[]{:S(2)}, u32[]{:S(2)}) collective-permute-start(bf16[64,208]{1,0:T(8,128)(2,1)S(1)} %get-tuple-element.163), channel_id=1, source_target_pairs={{0,64},{64,0},{128,192},{192,128},{1,65},{65,1},{129,193},{193,129... | collective-permute-start | bytes 79880 | tf_op jit(solution)/shard_map/ppermute | solution.py:337
  86.0 6.0 %collective-permute-start.9 = (bf16[64,208]{1,0:T(8,128)(2,1)S(1)}, bf16[64,208]{1,0:T(8,128)(2,1)S(1)}, u32[]{:S(2)}, u32[]{:S(2)}) collective-permute-start(bf16[64,208]{1,0:T(8,128)(2,1)S(1)} %get-tuple-element.164), channel_id=1, source_target_pairs={{64,128},{128,64},{65,129},{129,65},{66,130},{130,66},{67,131},{13... | collective-permute-start | bytes 79880 | tf_op jit(solution)/shard_map/ppermute | solution.py:340
  92.0 23.5 %copy-start.7 = (bf16[64,208]{1,0:T(8,128)(2,1)}, bf16[64,208]{1,0:T(8,128)(2,1)S(1)}, u32[]{:S(2)}) copy-start(bf16[64,208]{1,0:T(8,128)(2,1)S(1)} %get-tuple-element.71) | copy-start | bytes 79876
  92.1 23.5 %copy-start.8 = (bf16[64,208]{1,0:T(8,128)(2,1)}, bf16[64,208]{1,0:T(8,128)(2,1)S(1)}, u32[]{:S(2)}) copy-start(bf16[64,208]{1,0:T(8,128)(2,1)S(1)} %get-tuple-element.70) | copy-start | bytes 79876
  98.9 15.7 %all-to-all-start.1 = ((bf16[8,48,512]{2,1,0:T(8,128)(2,1)}), bf16[8,48,512]{2,1,0:T(8,128)(2,1)S(1)}, u32[]{:S(2)}, u32[]{:S(2)}) async-start(bf16[8,48,512]{2,1,0:T(8,128)(2,1)} %broadcast_in_dim.28), calls=%async_computation.1 | async-start | bytes 786432 | tf_op jit(solution)/shard_map/all_to_all | solution.py:424
  102.9 4.7 %collective-permute-start.11 = (bf16[34,208]{1,0:T(8,128)(2,1)S(1)}, bf16[34,208]{1,0:T(8,128)(2,1)S(1)}, u32[]{:S(2)}, u32[]{:S(2)}) collective-permute-start(bf16[34,208]{1,0:T(8,128)(2,1)S(1)} %get-tuple-element.168), channel_id=1, source_target_pairs={{1,2},{3,4},{5,6},{7,8},{9,10},{11,12},{13,14},{15,16},{17,18},{19... | collective-permute-start | bytes 42440 | tf_op jit(solution)/shard_map/ppermute | solution.py:340
  103.6 6.9 %collective-permute-start.12 = (bf16[34,208]{1,0:T(8,128)(2,1)S(1)}, bf16[34,208]{1,0:T(8,128)(2,1)S(1)}, u32[]{:S(2)}, u32[]{:S(2)}) collective-permute-start(bf16[34,208]{1,0:T(8,128)(2,1)S(1)} %get-tuple-element.167), channel_id=1, source_target_pairs={{0,1},{1,0},{2,3},{3,2},{4,5},{5,4},{6,7},{7,6},{8,9},{9,8},{10,11... | collective-permute-start | bytes 42440 | tf_op jit(solution)/shard_map/ppermute | solution.py:337
  115.6 22.0 %all-to-all-start.2 = ((bf16[16,48,512]{2,1,0:T(8,128)(2,1)}), bf16[16,48,512]{2,1,0:T(8,128)(2,1)S(1)}, u32[]{:S(2)}, u32[]{:S(2)}) async-start(bf16[16,48,512]{2,1,0:T(8,128)(2,1)} %broadcast_in_dim.29), calls=%async_computation.2 | async-start | bytes 1572864 | tf_op jit(solution)/shard_map/all_to_all | solution.py:428
  137.6 4.7 %copy-start = (bf16[16,48,512]{2,1,0:T(8,128)(2,1)}, bf16[16,48,512]{2,1,0:T(8,128)(2,1)S(1)}, u32[]{:S(2)}) copy-start(bf16[16,48,512]{2,1,0:T(8,128)(2,1)S(1)} %all-to-all-done.2) | copy-start | bytes 2359300
  137.6 4.7 %collective-permute-start.13 = (bf16[768,512]{1,0:T(8,128)(2,1)S(1)}, bf16[768,512]{1,0:T(8,128)(2,1)S(1)}, u32[]{:S(2)}, u32[]{:S(2)}) collective-permute-start(bf16[768,512]{1,0:T(8,128)(2,1)S(1)} %bitcast.184), channel_id=1, source_target_pairs={{0,64},{64,0},{1,65},{65,1},{2,66},{66,2},{3,67},{67,3},{4,68},{68... | collective-permute-start | bytes 2359304 | tf_op jit(solution)/shard_map/ppermute | solution.py:430
  142.3 0.9 copy-start.1

commit v3 on v2

--- a/solution.py
+++ b/solution.py
@@ -12,7 +12,7 @@
 PLANE = ("yl", "x", "yh")
 BF = jnp.bfloat16
 F4 = jnp.float32
-LIMIT = 56 * 1024 * 1024
+LIMIT = 28 * 1024 * 1024
 RED, MIXC, MIXF, TAPC, TAPF, TOTAL = 0, 832, 1248, 1456, 1488, 1536
 LANES = 512
 SOURCE = ((2, 0, 1), (0, 1, 3))
@@ -62,7 +62,7 @@
 
 
 def sigmoid(value):
-    return 1.0 / (1.0 + jnp.exp(-value))
+    return 0.5 * jnp.tanh(0.5 * value) + 0.5
 
 
 def fine_rows(slide_ref, top_ref, bottom_ref, lr_ref, shifted, keep=None):
@@ -213,16 +213,75 @@
         gtaps_out[at : at + 1, :] = jnp.sum(sums[at], axis=0, keepdims=True)
 
 
+def edge_message(outs, source, bases, ats, near_ref, away_ref, middle):
+    for out, at in zip(outs, ats):
+        total = 0.0
+        for block, base in ((near_ref[...], bases[0]), (away_ref[...], bases[1]), (middle, None)):
+            pick = picker(out.shape[0], block.shape[0], functools.partial(source, at, base))
+            total = total + dot(pick, block)
+        out[...] = total.astype(BF)
+
+
+def coarse_message(flags_ref, near_ref, away_ref, act_ref, near_out, away_out):
+    def source(at, base, row):
+        column, r = row // 24, row % 24
+        if base is None:
+            inside = jnp.logical_and(r >= 4, r < 20)
+            return jnp.where(inside, (r - 4) * 32 + at + column, -1)
+        inside = jnp.logical_and(r >= base, r < base + 4)
+        return jnp.where(inside, (r - base) * 32 + at + column, -1)
+
+    base = jnp.where(flags_ref[0] == 0, 20, 0)
+    at = jnp.where(flags_ref[1] == 0, 28, 0)
+    middle = act_ref[...].reshape(512, act_ref.shape[2])
+    edge_message((near_out, away_out), source, (base, 20 - base), (at, 28 - at), near_ref, away_ref, middle)
+
+
+def fine_message(flags_ref, near_ref, away_ref, ddepth_ref, near_out, away_out):
+    def source(at, base, row):
+        if base is None:
+            r = row - 1
+            inside = jnp.logical_and(r >= 0, r < 32)
+            return jnp.where(inside, ((r % 2) * 32 + r // 2) * 32 + at * 543, -1)
+        return jnp.where(row == base, at * 63, -1)
+
+    base = jnp.where(flags_ref[0] == 0, 33, 0)
+    at = jnp.where(flags_ref[1] == 0, 1, 0)
+    middle = ddepth_ref[...].reshape(2048, ddepth_ref.shape[3])
+    edge_message((near_out, away_out), source, (base, 33 - base), (at, 1 - at), near_ref, away_ref, middle)
+
+
+def side_rows(flags_ref, near_ref, away_ref, rows, width):
+    def source(base, row):
+        r, place = row // 16, row % 16 - base
+        inside = jnp.logical_and(place >= 0, place < width)
+        return jnp.where(inside, place * rows + r, -1)
+
+    base = jnp.where(flags_ref[1] == 0, width, 0)
+    total = 0.0
+    for block, at in ((near_ref[...], base), (away_ref[...], width - base)):
+        pick = picker(16 * rows, block.shape[0], functools.partial(source, at))
+        total = total + dot(pick, block)
+    return total.astype(BF).reshape(rows, 16, near_ref.shape[1])
+
+
 def coarse_forward(
-    act_ref, top_ref, bottom_ref, lr_ref, taps_ref, mix_ref, reduced_ref, cot_ref, deltac_ref,
-    gred_ref, gmixf_ref, gtapsf_ref, core_ref,
-    section_out, mine_out, other_out, shifted, sums, depth, rows, packed,
+    flags_ref, act_ref, near_ref, away_ref, nside_ref, aside_ref, taps_ref, mix_ref, reduced_ref, cot_ref, deltac_ref,
+    gred_ref, gmixf_ref, gtapsf_ref,
+    section_out, mine_out, other_out, shifted, sums, depth, rows, sides_of, packed,
 ):
     wide = mix_ref.shape[0]
-    rows[0:4] = top_ref[...]
+    for parity in range(2):
+
+        @pl.when(flags_ref[0] == parity)
+        def _():
+            low, high = (near_ref, away_ref) if parity else (away_ref, near_ref)
+            rows[0:4] = low[...].reshape(4, 32, wide)
+            rows[20:24] = high[...].reshape(4, 32, wide)
+
     rows[4:20] = act_ref[...]
-    rows[20:24] = bottom_ref[...]
-    coarse_rows(lambda r: rows[r], lambda r: lr_ref[r], shifted)
+    sides_of[...] = side_rows(flags_ref, nside_ref, aside_ref, 24, 4)
+    coarse_rows(lambda r: rows[r], lambda r: sides_of[r], shifted)
     sums[...] = jnp.zeros_like(sums)
 
     def conv(i, carry):
@@ -249,16 +308,16 @@
     taps = jnp.concatenate([jnp.sum(sums[...], axis=1), jnp.zeros((7, wide), F4)], axis=0)
     packed[TAPC:TAPF, 0:wide] = taps.astype(BF)
     packed[TAPF : TAPF + 16, 0:fine] = gtapsf_ref[...].astype(BF)
-    core = core_ref[0]
+    core = flags_ref[2]
     half = TOTAL // 2
     mine_out[...] = packed[pl.ds(pl.multiple_of(core * half, half), half), :]
     other_out[...] = packed[pl.ds(pl.multiple_of((1 - core) * half, half), half), :]
 
 
 def unpack(
-    near_ref, far_ref, core_ref, tapsf_out, mixf_out, red_out, tapsc_out, mixc_out, packed, *, fine, coarse
+    flags_ref, near_ref, far_ref, tapsf_out, mixf_out, red_out, tapsc_out, mixc_out, packed, *, fine, coarse
 ):
-    core = core_ref[0]
+    core = flags_ref[2]
     half = TOTAL // 2
     packed[pl.ds(pl.multiple_of(core * half, half), half), :] = near_ref[...]
     packed[pl.ds(pl.multiple_of((1 - core) * half, half), half), :] = far_ref[...]
@@ -276,7 +335,8 @@
 
 
 def fine_backward(
-    ddepth_ref, top_ref, bottom_ref, lr_ref, taps_ref, dfine_ref, slide_ref, out_ref, shifted
+    flags_ref, ddepth_ref, near_ref, away_ref, nside_ref, aside_ref, taps_ref, dfine_ref, slide_ref, out_ref,
+    shifted, lr_ref, ends,
 ):
     chans = taps_ref.shape[2]
     pick = picker(64, 80, phase_source)
@@ -289,8 +349,17 @@
         shifted[2, r] = got[:32]
         shifted[3, r] = got[32:]
 
-    put(0, top_ref[0], top_ref[1])
-    put(33, bottom_ref[0], bottom_ref[1])
+    lr_ref[...] = side_rows(flags_ref, nside_ref, aside_ref, 48, 1)
+    for parity in range(2):
+
+        @pl.when(flags_ref[0] == parity)
+        def _():
+            low, high = (near_ref, away_ref) if parity else (away_ref, near_ref)
+            ends[0] = low[...]
+            ends[1] = high[...]
+
+    put(0, ends[0, :32], ends[0, 32:])
+    put(33, ends[1, :32], ends[1, 32:])
 
     def fill(i, carry):
         for p in range(2):
@@ -331,13 +400,24 @@
     )(*operands)
 
 
-def swap(first, last, axes):
+def trade(first, last, axes):
+    even = lax.axis_index(axes) % 2 == 0
+    return send(jnp.where(even, last, first), jnp.where(even, first, last), axes)
+
+
+def send(near, away, axes):
     count = lax.axis_size(axes)
-    even = lax.axis_index(axes) % 2 == 0
-    near = lax.ppermute(jnp.where(even, last, first), axes, [(i, i ^ 1) for i in range(count)])
     far = [(i, i + 1) for i in range(1, count - 1, 2)]
     far = far + [(j, i) for i, j in far]
-    away = lax.ppermute(jnp.where(even, first, last), axes, far)
+    return (
+        lax.ppermute(near, axes, [(i, i ^ 1) for i in range(count)]),
+        lax.ppermute(away, axes, far),
+    )
+
+
+def swap(first, last, axes):
+    even = lax.axis_index(axes) % 2 == 0
+    near, away = trade(first, last, axes)
     return jnp.where(even, away, near), jnp.where(even, near, away)
 
 
@@ -412,8 +492,8 @@
     core = lax.axis_index("core")
     plane = lax.axis_size(PLANE)
     depth = lax.axis_size("z")
-    trade = [(0, 1), (1, 0)]
-    mine = mine + lax.ppermute(other, "core", trade)
+    across = [(0, 1), (1, 0)]
+    mine = mine + lax.ppermute(other, "core", across)
     chunk = total // plane
     mine = mine.reshape(plane, chunk, lanes)
     edges = rows_step(mine)
@@ -427,7 +507,7 @@
     extra = last_step(edges)
     got = lax.all_to_all(jnp.broadcast_to(mine, (plane, chunk, lanes)), PLANE, 0, 0, tiled=True)
     got, extra = lax.optimization_barrier((got.reshape(total, lanes), extra))
-    return got, lax.ppermute(got, "core", trade), extra
+    return got, lax.ppermute(got, "core", across), extra
 
 
 def sides(left, right):
@@ -441,7 +521,9 @@
     devices_all = lax.axis_size(ROWS) * lax.axis_size(COLS)
     scale_fine = float(height * breadth * devices_all) ** (-0.5)
     scale_coarse = float(height * breadth // 4 * devices_all) ** (-0.5)
-    core = lax.axis_index("core").astype(jnp.int32).reshape(1)
+    flags = jnp.stack(
+        [lax.axis_index(ROWS) % 2, lax.axis_index(COLS) % 2, lax.axis_index("core")]
+    ).astype(jnp.int32)
     ctop, cbottom, clr, top, bottom, lr = input_halos(cotangent, slide_pixels)
     top, bottom = top[None], bottom[None]
 
@@ -467,10 +549,13 @@
         8_000_000_000,
         cotangent, jnp.concatenate([ctop, cbottom], axis=0), clr, mix_coarse, taps_coarse, reduced,
     )
-    arows = swap(*coarse_edges(act), ROWS)
+    arows = trade(*coarse_edges(act), ROWS)
     arows, delta_reduced = lax.optimization_barrier((arows, delta_reduced))
-    atop, abottom = (block.reshape(4, 32, wide) for block in arows)
-    acolumns = swap(*coarse_columns(atop, act, abottom), COLS)
+    tall = 4 * (height // 2 + 8)
+    message = call(
+        coarse_message, [((tall, wide), BF), ((tall, wide), BF)], [], 10_000_000, flags, *arows, act
+    )
+    acolumns = send(*message, COLS)
     dfine, ddepth, term_reduce, term_mix_fine, term_taps_fine = call(
         fine_terms,
         [
@@ -486,7 +571,6 @@
         slide_pixels, top, bottom, lr,
     )
     acolumns, ddepth = lax.optimization_barrier((acolumns, ddepth))
-    alr = coarse_sides(*acolumns)
     section_out, mine, other = call(
         coarse_forward,
         [((16, 32, wide), BF), ((TOTAL // 2, LANES), BF), ((TOTAL // 2, LANES), BF)],
@@ -495,32 +579,30 @@
             ((25, 8, wide), F4),
             ((16, 32, wide), BF),
             ((24, 32, wide), BF),
+            ((24, 16, wide), BF),
             ((TOTAL, LANES), BF),
         ],
         4_000_000_000,
-        act, atop, abottom, alr, taps_coarse, mix_coarse, reduced, cotangent, delta_coarse,
-        term_reduce, term_mix_fine, term_taps_fine, core,
+        flags, act, *arows, *acolumns, taps_coarse, mix_coarse, reduced, cotangent, delta_coarse,
+        term_reduce, term_mix_fine, term_taps_fine,
     )
     def rows_step(after):
         edges = ddepth[:2, 0].reshape(breadth, chans), ddepth[2:, 15].reshape(breadth, chans)
-        return swap(*hold(edges, after), ROWS)
-
-    def columns_step(edges):
-        inner = ddepth.reshape(2, 2, 16, 32, chans)
-        left = inner[:, 0, :, 0].transpose(1, 0, 2).reshape(height, chans)
-        right = inner[:, 1, :, 31].transpose(1, 0, 2).reshape(height, chans)
-        low, high = edges
-        return low, high, *swap(*fine_columns(low, left, right, high), COLS)
+        return trade(*hold(edges, after), ROWS)
+
+    def columns_step(rows):
+        message = call(
+            fine_message, [((48, chans), BF), ((48, chans), BF)], [], 10_000_000, flags, *rows, ddepth
+        )
+        return *rows, *send(*message, COLS)
 
     def last_step(edges):
-        low, high, left, right = edges
         return call(
             fine_backward,
             [((height, breadth, chans), BF)],
-            [((4, 34, 32, chans), F4)],
+            [((4, 34, 32, chans), F4), ((48, 16, chans), BF), ((2, 64, chans), BF)],
             2_000_000_000,
-            ddepth, low.reshape(2, 32, chans), high.reshape(2, 32, chans), fine_sides(left, right),
-            taps_fine, dfine, slide,
+            flags, ddepth, *edges, taps_fine, dfine, slide,
         )[0]
 
     near, far, pixel_grad = reduce_terms(mine, other, rows_step, columns_step, last_step)
@@ -535,7 +617,7 @@
         ],
         [((TOTAL, LANES), BF)],
         1_000_000,
-        near, far, core,
+        flags, near, far,
     )
     tapsf, mixf, red, tapsc, mixc = grads
     return (section_out, pixel_grad, tapsf, mixf, red.T, tapsc, mixc)

time: 147 us -> 129 us (0.88)
  Pallas kernels: 40.9 us -> 30.5 us
  other arithmetic: 7.77 us -> 1.81 us
  waiting for transfers between devices: 27.3 us -> 32.3 us
  starting transfers between devices: 55.9 us -> 51.4 us
  local copies, waits for them, and re-layouts: 13.3 us -> 10.7 us
    pallas_call x6 -> x8, Pallas kernels: 40.9 us -> 30.5 us  [call(): pl.pallas_call(body, out_shape=[jax.ShapeDtypeStruct(shape, kind) for sha...]
    ppermute x14, starting transfers between devices: 32.9 us -> 24.9 us  [the longest x6 12.3 us: send(): lax.ppermute(away, axes, far)]
    all_to_all x1, waiting for transfers between devices: 4.03 us -> 8.5 us  [reduce_terms(): lax.all_to_all(jnp.broadcast_to(mine, (depth, chunk, lanes)), 'z', 0, 0,...]
    all_to_all x1, starting transfers between devices: 9.88 us -> 14.2 us  [reduce_terms(): got = lax.all_to_all(mine, PLANE, 0, 0, tiled=True)]
    all_to_all x1, waiting for transfers between devices: 5.91 us -> 9.76 us  [reduce_terms(): got = lax.all_to_all(mine, PLANE, 0, 0, tiled=True)]
    concatenate x4 -> x2, other arithmetic: 3.38 us -> 0.22 us  [sides(): both = jnp.concatenate([left, right], axis=1)]
    ppermute x14, waiting for transfers between devices: 11.6 us -> 9.43 us  [the longest x6 2.82 us: send(): lax.ppermute(away, axes, far)]
    unnamed x53 -> x31, local copies, waits for them, and re-layouts: 2.62 us -> 4.28 us
  transfers between devices with their start and end apart: 17 -> 17, of which waited for: 9 -> 7; matrix products, arithmetic and copies ran while one was open for 5% -> 2% of each run, Pallas kernels for 15% -> 13%
where the time goes in v3:
time: 129 us; the launch traced here: 128 us
  starting transfers between devices  51.4 us (40%)
  waiting for transfers between devices  32.3 us (25%)
  Pallas kernels  30.5 us (24%)
  local copies, waits for them, and re-layouts  10.7 us (8%)
  other arithmetic  1.81 us (1%)
  between operations  1.31 us (1%)
    pallas_call x8, Pallas kernels, call(): pl.pallas_call(body, out_shape=[jax.ShapeDtypeStruct(shape, kind) for sha...  30.5 us
    all_to_all x1, starting transfers between devices, reduce_terms(): got = lax.all_to_all(mine, PLANE, 0, 0, tiled=True)  14.2 us
    ppermute x6, starting transfers between devices, send(): lax.ppermute(away, axes, far)  12.3 us
    ppermute x6, starting transfers between devices, send(): lax.ppermute(near, axes, [(i, i ^ 1) for i in range(count)])  9.76 us
    all_to_all x1, waiting for transfers between devices, reduce_terms(): got = lax.all_to_all(mine, PLANE, 0, 0, tiled=True)  9.76 us
    all_to_all x1, starting transfers between devices, reduce_terms(): lax.all_to_all(jnp.broadcast_to(mine, (plane, chunk, lanes)), PLANE, 0, 0...  8.7 us
    all_to_all x1, waiting for transfers between devices, reduce_terms(): lax.all_to_all(jnp.broadcast_to(mine, (depth, chunk, lanes)), 'z', 0, 0,...  8.5 us
    all_to_all x1, waiting for transfers between devices, reduce_terms(): lax.all_to_all(jnp.broadcast_to(mine, (plane, chunk, lanes)), PLANE, 0, 0...  4.63 us
  transfers between devices with their start and end apart: 17, of which 7 were waited for; matrix products, arithmetic and copies ran while one was open for 2% of the time, Pallas kernels for 13%

profile of v3, /device:TPU:1, one launch (start us, length us, event | category | flops | bytes accessed | tf_op | source)
XLA Modules:
  0.0 128.1 jit_solution(14780572150346741367)
XLA Ops:
  0.6 0.0 copy-start
  0.7 0.9 slice_bitcast_fusion.3
  1.5 1.0 fusion.23
  2.5 0.1 broadcast_select_fusion.2
  2.6 3.3 %collective-permute-start.1 = (bf16[192,416]{1,0:T(8,128)(2,1)S(1)}, bf16[192,416]{1,0:T(8,128)(2,1)S(1)}, u32[]{:S(2)}, u32[]{:S(2)}) collective-permute-start(bf16[192,416]{1,0:T(8,128)(2,1)S(1)} %get-tuple-element.111), channel_id=1, source_target_pairs={{0,64},{64,0},{128,192},{192,128},{1,65},{65,1},{129,193},{193,129... | collective-permute-start | bytes 479240 | tf_op jit(solution)/shard_map/ppermute | solution.py:413
  5.9 1.9 %collective-permute-start = (bf16[192,416]{1,0:T(8,128)(2,1)S(1)}, bf16[192,416]{1,0:T(8,128)(2,1)S(1)}, u32[]{:S(2)}, u32[]{:S(2)}) collective-permute-start(bf16[192,416]{1,0:T(8,128)(2,1)S(1)} %get-tuple-element.112), channel_id=1, source_target_pairs={{64,128},{128,64},{65,129},{129,65},{66,130},{130,66},{67,131},{13... | collective-permute-start | bytes 479240 | tf_op jit(solution)/shard_map/ppermute | solution.py:414
  7.9 1.0 fusion.21
  8.9 0.2 fusion.22
  9.2 0.8 copy.118.weight_ref
  10.0 0.1 pad_add_fusion.flags_ref
  10.1 0.0 collective-permute-done.1
  10.1 2.8 %collective-permute-done = bf16[192,416]{1,0:T(8,128)(2,1)S(1)} collective-permute-done((bf16[192,416]{1,0:T(8,128)(2,1)S(1)}, bf16[192,416]{1,0:T(8,128)(2,1)S(1)}, u32[]{:S(2)}, u32[]{:S(2)}) %collective-permute-start) | collective-permute-done | bytes 159776 | tf_op jit(solution)/shard_map/ppermute | solution.py:414
  13.0 0.1 fusion.27
  13.1 0.1 fusion.26
  13.3 0.6 concatenate.32
  13.9 0.6 concatenate.30
  14.5 0.0 copy-start.3
  14.5 0.0 copy-start.5
  14.6 0.8 collective-permute-start.2
  15.4 2.9 %collective-permute-start.3 = (bf16[130,416]{1,0:T(8,128)(2,1)S(1)}, bf16[130,416]{1,0:T(8,128)(2,1)S(1)}, u32[]{:S(2)}, u32[]{:S(2)}) collective-permute-start(bf16[130,416]{1,0:T(8,128)(2,1)S(1)} %get-tuple-element.116), channel_id=1, source_target_pairs={{0,1},{1,0},{2,3},{3,2},{4,5},{5,4},{6,7},{7,6},{8,9},{9,8},{10,11... | collective-permute-start | bytes 324488 | tf_op jit(solution)/shard_map/ppermute | solution.py:413
  18.3 0.0 collective-permute-done.2
  18.3 2.4 %collective-permute-done.3 = bf16[130,416]{1,0:T(8,128)(2,1)S(1)} collective-permute-done((bf16[130,416]{1,0:T(8,128)(2,1)S(1)}, bf16[130,416]{1,0:T(8,128)(2,1)S(1)}, u32[]{:S(2)}, u32[]{:S(2)}) %collective-permute-start.3) | collective-permute-done | bytes 108192 | tf_op jit(solution)/shard_map/ppermute | solution.py:413
  20.8 0.1 copy.177
  20.9 0.1 copy.176
  21.0 0.1 fusion.7.lr_ref.lrf_ref
  21.1 0.0 copy-start.2
  21.1 0.0 copy-start.4
  21.1 3.7 %shard_map.126 = (bf16[4,16,32,208]{3,2,1,0:T(8,128)(2,1)S(1)}, bf16[4,16,32,208]{3,2,1,0:T(8,128)(2,1)S(1)}, bf16[4,512,208]{2,1,0:T(8,128)(2,1)S(1)}, bf16[512...) custom-call(bf16[32,64,208]{2,1,0:T(8,128)(2,1)S(1)} %copy-done.1, bf16[1,64,208]{2,1,0:T(8,128)(2,1)S(1)} %get-tuple-element.140.top_ref, ...), custom_call_target="tpu_custom_call" | custom-call | flops 4000000000 | bytes 8000000 | tf_op jit(solution)/shard_map/pallas_call | solution.py:392
  24.8 0.0 copy-start.6
  24.9 0.1 collective-permute-start.4
  25.0 4.3 %collective-permute-start.5 = (bf16[128,416]{1,0:T(8,128)(2,1)S(1)}, bf16[128,416]{1,0:T(8,128)(2,1)S(1)}, u32[]{:S(2)}, u32[]{:S(2)}) collective-permute-start(bf16[128,416]{1,0:T(8,128)(2,1)S(1)} %bitcast.105), channel_id=1, source_target_pairs={{64,128},{128,64},{65,129},{129,65},{66,130},{130,66},{67,131},{13... | collective-permute-start | bytes 319496 | tf_op jit(solution)/shard_map/ppermute | solution.py:414
  29.2 0.1 fusion.4.lr_ref
  29.4 4.2 %shard_map.127 = (bf16[16,32,416]{2,1,0:T(8,128)(2,1)S(1)}, bf16[16,32,416]{2,1,0:T(8,128)(2,1)S(1)}) custom-call(bf16[16,32,416]{2,1,0:T(8,128)(2,1)S(1)} %copy-done, bf16[8,32,416]{2,1,0:T(8,128)(2,1)S(1)} %pad_maximum_fusion.tb_ref, bf16[24,16,416]{2,1,0:T(8,128)(2,1)S(1)} %fusion.4.lr_ref, bf16[416,416]{1,0:T(8,128)(2,1)S(1)} %copy-done.2, ...), custom_call_target="tpu_custom_call" | custom-call | flops 8000000000 | bytes 8000000 | tf_op jit(solution)/shard_map/pallas_call | solution.py:392
  33.6 1.0 shard_map.128
  34.6 1.8 %collective-permute-start.6 = (bf16[96,416]{1,0:T(8,128)(2,1)S(1)}, bf16[96,416]{1,0:T(8,128)(2,1)S(1)}, u32[]{:S(2)}, u32[]{:S(2)}) collective-permute-start(bf16[96,416]{1,0:T(8,128)(2,1)S(1)} %get-tuple-element.54), channel_id=1, source_target_pairs={{0,1},{1,0},{2,3},{3,2},{4,5},{5,4},{6,7},{7,6},{8,9},{9,8},{10,11... | collective-permute-start | bytes 239624 | tf_op jit(solution)/shard_map/ppermute | solution.py:413
  36.4 0.8 collective-permute-start.7
  37.3 5.3 %shard_map.129 = (bf16[4,16,32,208]{3,2,1,0:T(8,128)(2,1)S(1)}, bf16[4,16,32,208]{3,2,1,0:T(8,128)(2,1)S(1)}, bf16[832,416]{1,0:T(8,128)(2,1)S(1)}, f32[208,208]{1,0:T(8,128)S(1)}, f32[16,208]{1,0:T(8,128)S(1)}) custom-call(bf16[512,416]{1,0:T(8,128)(2,1)S(1)} %bitcast.94, bf16[4,512,208]{2,1,0:T(8,128)(2,1)S(1)} %get-tuple-element.57.pre_ref, ...), custom_call_target="tpu_custom_call" | custom-call | flops 8000000000 | bytes 8000000 | tf_op jit(solution)/shard_map/pallas_call | solution.py:392
  42.5 0.0 copy-start.8
  42.6 1.0 copy-done.8
  43.5 7.2 %shard_map.130 = (bf16[16,32,416]{2,1,0:T(8,128)(2,1)}, bf16[768,512]{1,0:T(8,128)(2,1)S(1)}, bf16[768,512]{1,0:T(8,128)(2,1)S(1)}) custom-call(s32[3]{0:T(128)S(1)} %pad_add_fusion.flags_ref, bf16[16,32,416]{2,1,0:T(8,128)(2,1)S(1)} %get-tuple-element.49.act_ref, bf16[128,416]{1,0:T(8,128)(2,1)S(1)} %collective-permute-done.4.near_ref, ...), custom_call_target="tpu_custom_call" | custom-call | flops 4000000000 | bytes 8000000 | tf_op jit(solution)/shard_map/pallas_call | solution.py:392
  50.7 2.3 %collective-permute-done.8 = bf16[768,512]{1,0:T(8,128)(2,1)S(1)} collective-permute-done((bf16[768,512]{1,0:T(8,128)(2,1)S(1)}, bf16[768,512]{1,0:T(8,128)(2,1)S(1)}, u32[]{:S(2)}, u32[]{:S(2)}) %collective-permute-start.8) | collective-permute-done | bytes 786464 | tf_op jit(solution)/shard_map/ppermute | solution.py:496
  53.0 1.1 add.50
  54.1 14.2 %all-to-all-start = ((bf16[16,48,512]{2,1,0:T(8,128)(2,1)}), bf16[16,48,512]{2,1,0:T(8,128)(2,1)S(1)}, u32[]{:S(2)}, u32[]{:S(2)}) async-start(bf16[16,48,512]{2,1,0:T(8,128)(2,1)} %bitcast.32), calls=%async_computation | async-start | bytes 1572864 | tf_op jit(solution)/shard_map/all_to_all | solution.py:500
  68.3 3.9 %collective-permute-start.10 = (bf16[64,208]{1,0:T(8,128)(2,1)S(1)}, bf16[64,208]{1,0:T(8,128)(2,1)S(1)}, u32[]{:S(2)}, u32[]{:S(2)}) collective-permute-start(bf16[64,208]{1,0:T(8,128)(2,1)S(1)} %get-tuple-element.137), channel_id=1, source_target_pairs={{64,128},{128,64},{65,129},{129,65},{66,130},{130,66},{67,131},{13... | collective-permute-start | bytes 79880 | tf_op jit(solution)/shard_map/ppermute | solution.py:414
  72.2 0.1 collective-permute-start.9
  72.3 9.8 %all-to-all-done = bf16[16,48,512]{2,1,0:T(8,128)(2,1)S(1)} async-done(((bf16[16,48,512]{2,1,0:T(8,128)(2,1)}), bf16[16,48,512]{2,1,0:T(8,128)(2,1)S(1)}, u32[]{:S(2)}, u32[]{:S(2)}) %all-to-all-start) | async-done | bytes 786464 | tf_op jit(solution)/shard_map/all_to_all | solution.py:500
  82.0 0.1 reduce_sum.24
  82.2 0.8 broadcast_in_dim.22
  82.9 3.6 %all-to-all-start.1 = ((bf16[8,48,512]{2,1,0:T(8,128)(2,1)}), bf16[8,48,512]{2,1,0:T(8,128)(2,1)S(1)}, u32[]{:S(2)}, u32[]{:S(2)}) async-start(bf16[8,48,512]{2,1,0:T(8,128)(2,1)} %broadcast_in_dim.22), calls=%async_computation.1 | async-start | bytes 786432 | tf_op jit(solution)/shard_map/all_to_all | solution.py:504
  86.6 1.0 shard_map.131
  87.6 1.5 %collective-permute-start.11 = (bf16[48,208]{1,0:T(8,128)(2,1)S(1)}, bf16[48,208]{1,0:T(8,128)(2,1)S(1)}, u32[]{:S(2)}, u32[]{:S(2)}) collective-permute-start(bf16[48,208]{1,0:T(8,128)(2,1)S(1)} %get-tuple-element.75), channel_id=1, source_target_pairs={{0,1},{1,0},{2,3},{3,2},{4,5},{5,4},{6,7},{7,6},{8,9},{9,8},{10,11... | collective-permute-start | bytes 59912 | tf_op jit(solution)/shard_map/ppermute | solution.py:413
  89.2 0.7 collective-permute-start.12
  89.8 8.5 %all-to-all-done.1 = bf16[8,48,512]{2,1,0:T(8,128)(2,1)S(1)} async-done(((bf16[8,48,512]{2,1,0:T(8,128)(2,1)}), bf16[8,48,512]{2,1,0:T(8,128)(2,1)S(1)}, u32[]{:S(2)}, u32[]{:S(2)}) %all-to-all-start.1) | async-done | bytes 393248 | tf_op jit(solution)/shard_map/all_to_all | solution.py:504
  98.3 0.1 reduce_sum.25
  98.4 1.0 broadcast_in_dim.23
  99.4 8.7 %all-to-all-start.2 = ((bf16[16,48,512]{2,1,0:T(8,128)(2,1)}), bf16[16,48,512]{2,1,0:T(8,128)(2,1)S(1)}, u32[]{:S(2)}, u32[]{:S(2)}) async-start(bf16[16,48,512]{2,1,0:T(8,128)(2,1)} %broadcast_in_dim.23), calls=%async_computation.2 | async-start | bytes 1572864 | tf_op jit(solution)/shard_map/all_to_all | solution.py:508
  108.1 0.0 copy-start.7
  108.1 1.2 copy-done.7
  109.3 1.2 copy-done.9
  110.5 5.6 %shard_map.132 = bf16[32,64,208]{2,1,0:T(8,128)(2,1)} custom-call(s32[3]{0:T(128)S(1)} %pad_add_fusion.flags_ref, bf16[4,16,32,208]{3,2,1,0:T(8,128)(2,1)S(1)} %get-tuple-element.69.ddepth_ref, bf16[64,208]{1,0:T(8,128)(2,1)S(1)} %collective-permute-done.9.near_ref, bf16[64,208]{1,0:T(8,128)(2,1)S(1)} %collective-permute-done.10.away_ref, ...), custom_call_target="tpu_custom_call" | custom-call | flops 2000000000 | bytes 8000000 | tf_op jit(solution)/shard_map/pallas_call | solution.py:392
  116.1 4.6 %all-to-all-done.2 = bf16[16,48,512]{2,1,0:T(8,128)(2,1)S(1)} async-done(((bf16[16,48,512]{2,1,0:T(8,128)(2,1)}), bf16[16,48,512]{2,1,0:T(8,128)(2,1)S(1)}, u32[]{:S(2)}, u32[]{:S(2)}) %all-to-all-start.2) | async-done | bytes 786464 | tf_op jit(solution)/shard_map/all_to_all | solution.py:508
  120.7 2.8 %collective-permute-start.13 = (bf16[768,512]{1,0:T(8,128)(2,1)S(1)}, bf16[768,512]{1,0:T(8,128)(2,1)S(1)}, u32[]{:S(2)}, u32[]{:S(2)}) collective-permute-start(bf16[768,512]{1,0:T(8,128)(2,1)S(1)} %bitcast.89), channel_id=1, source_target_pairs={{0,64},{64,0},{1,65},{65,1},{2,66},{66,2},{3,67},{67,3},{4,68},{68... | collective-permute-start | bytes 2359304 | tf_op jit(solution)/shard_map/ppermute | solution.py:510
  123.5 1.9 %collective-permute-done.13.far_ref = bf16[768,512]{1,0:T(8,128)(2,1)S(1)} collective-permute-done((bf16[768,512]{1,0:T(8,128)(2,1)S(1)}, bf16[768,512]{1,0:T(8,128)(2,1)S(1)}, u32[]{:S(2)}, u32[]{:S(2)}) %collective-permute-start.13) | collective-permute-done | bytes 786464 | tf_op jit(solution)/shard_map/ppermute | solution.py:510
  125.4 2.6 %shard_map.133 = (f32[3,3,208]{2,1,0:T(4,128)}, f32[208,208]{1,0:T(8,128)}, f32[416,832]{1,0:T(8,128)}, f32[5,5,416]{2,1,0:T(8,128)}, f32[416,416]{1,0:T(8,128)}) custom-call(s32[3]{0:T(128)S(1)} %pad_add_fusion.flags_ref, bf16[768,512]{1,0:T(8,128)(2,1)S(1)} %bitcast.90, bf16[768,512]{1,0:T(8,128)(2,1)S(1)} %collective-permute-done.13.far_ref), custom_call_target="tpu_custom_call" | custom-call | flops 1000000 | bytes 8000000 | tf_op jit(solution)/shard_map/pallas_call | solution.py:392
  (52 shorter events, 0.4 us)
Async XLA Ops:
  0.6 8.3 %copy-start = (bf16[16,32,416]{2,1,0:T(8,128)(2,1)S(1)}, bf16[16,32,416]{2,1,0:T(8,128)(2,1)}, u32[]{:S(2)}) copy-start(bf16[16,32,416]{2,1,0:T(8,128)(2,1)} %cot_ref.3) | copy-start | bytes 1277956
  0.6 8.6 %copy-start.10 = (bf16[832,416]{0,1:T(8,128)(2,1)S(1)}, bf16[832,416]{0,1:T(8,128)(2,1)}, u32[]{:S(2)}) copy-start(bf16[832,416]{0,1:T(8,128)(2,1)} %param.10) | copy-start | bytes 2076676
  2.6 7.5 %collective-permute-start.1 = (bf16[192,416]{1,0:T(8,128)(2,1)S(1)}, bf16[192,416]{1,0:T(8,128)(2,1)S(1)}, u32[]{:S(2)}, u32[]{:S(2)}) collective-permute-start(bf16[192,416]{1,0:T(8,128)(2,1)S(1)} %get-tuple-element.111), channel_id=1, source_target_pairs={{0,64},{64,0},{128,192},{192,128},{1,65},{65,1},{129,193},{193,129... | collective-permute-start | bytes 479240 | tf_op jit(solution)/shard_map/ppermute | solution.py:413
  5.9 7.0 %collective-permute-start = (bf16[192,416]{1,0:T(8,128)(2,1)S(1)}, bf16[192,416]{1,0:T(8,128)(2,1)S(1)}, u32[]{:S(2)}, u32[]{:S(2)}) collective-permute-start(bf16[192,416]{1,0:T(8,128)(2,1)S(1)} %get-tuple-element.112), channel_id=1, source_target_pairs={{64,128},{128,64},{65,129},{129,65},{66,130},{130,66},{67,131},{13... | collective-permute-start | bytes 479240 | tf_op jit(solution)/shard_map/ppermute | solution.py:414
  14.5 6.6 %copy-start.1 = (bf16[32,64,208]{2,1,0:T(8,128)(2,1)S(1)}, bf16[32,64,208]{2,1,0:T(8,128)(2,1)}, u32[]{:S(2)}) copy-start(bf16[32,64,208]{2,1,0:T(8,128)(2,1)} %slide_ref.3) | copy-start | bytes 2555908
  14.5 6.6 %copy-start.3 = (bf16[208,208]{1,0:T(8,128)(2,1)S(1)}, bf16[208,208]{1,0:T(8,128)(2,1)}, u32[]{:S(2)}) copy-start(bf16[208,208]{1,0:T(8,128)(2,1)} %mix_ref.4) | copy-start | bytes 259588
  14.5 6.6 %copy-start.5 = (f32[3,3,208]{2,1,0:T(4,128)S(1)}, f32[3,3,208]{2,1,0:T(4,128)}, u32[]{:S(2)}) copy-start(f32[3,3,208]{2,1,0:T(4,128)} %taps_ref.5) | copy-start | bytes 22468
  14.6 3.7 %collective-permute-start.2 = (bf16[130,416]{1,0:T(8,128)(2,1)S(1)}, bf16[130,416]{1,0:T(8,128)(2,1)S(1)}, u32[]{:S(2)}, u32[]{:S(2)}) collective-permute-start(bf16[130,416]{1,0:T(8,128)(2,1)S(1)} %get-tuple-element.115), channel_id=1, source_target_pairs={{1,2},{3,4},{5,6},{7,8},{9,10},{11,12},{13,14},{15,16},{17,18},{19... | collective-permute-start | bytes 324488 | tf_op jit(solution)/shard_map/ppermute | solution.py:414
  15.4 5.3 %collective-permute-start.3 = (bf16[130,416]{1,0:T(8,128)(2,1)S(1)}, bf16[130,416]{1,0:T(8,128)(2,1)S(1)}, u32[]{:S(2)}, u32[]{:S(2)}) collective-permute-start(bf16[130,416]{1,0:T(8,128)(2,1)S(1)} %get-tuple-element.116), channel_id=1, source_target_pairs={{0,1},{1,0},{2,3},{3,2},{4,5},{5,4},{6,7},{7,6},{8,9},{9,8},{10,11... | collective-permute-start | bytes 324488 | tf_op jit(solution)/shard_map/ppermute | solution.py:413
  21.1 8.2 %copy-start.2 = (bf16[416,416]{1,0:T(8,128)(2,1)S(1)}, bf16[416,416]{1,0:T(8,128)(2,1)}, u32[]{:S(2)}) copy-start(bf16[416,416]{1,0:T(8,128)(2,1)} %mix_ref.5) | copy-start | bytes 1038340
  21.1 8.2 %copy-start.4 = (f32[5,5,416]{2,1,0:T(8,128)S(1)}, f32[5,5,416]{2,1,0:T(8,128)}, u32[]{:S(2)}) copy-start(f32[5,5,416]{2,1,0:T(8,128)} %taps_ref.4) | copy-start | bytes 124804
  24.8 8.8 %copy-start.6 = (bf16[4,16,32,208]{3,2,1,0:T(8,128)(2,1)}, bf16[4,16,32,208]{3,2,1,0:T(8,128)(2,1)S(1)}, u32[]{:S(2)}) copy-start(bf16[4,16,32,208]{3,2,1,0:T(8,128)(2,1)S(1)} %get-tuple-element.83.slide_ref) | copy-start | bytes 2555908
  24.9 8.7 %collective-permute-start.4 = (bf16[128,416]{1,0:T(8,128)(2,1)S(1)}, bf16[128,416]{1,0:T(8,128)(2,1)S(1)}, u32[]{:S(2)}, u32[]{:S(2)}) collective-permute-start(bf16[128,416]{1,0:T(8,128)(2,1)S(1)} %bitcast.106), channel_id=1, source_target_pairs={{0,64},{64,0},{128,192},{192,128},{1,65},{65,1},{129,193},{193,129... | collective-permute-start | bytes 319496 | tf_op jit(solution)/shard_map/ppermute | solution.py:413
  25.0 8.7 %collective-permute-start.5 = (bf16[128,416]{1,0:T(8,128)(2,1)S(1)}, bf16[128,416]{1,0:T(8,128)(2,1)S(1)}, u32[]{:S(2)}, u32[]{:S(2)}) collective-permute-start(bf16[128,416]{1,0:T(8,128)(2,1)S(1)} %bitcast.105), channel_id=1, source_target_pairs={{64,128},{128,64},{65,129},{129,65},{66,130},{130,66},{67,131},{13... | collective-permute-start | bytes 319496 | tf_op jit(solution)/shard_map/ppermute | solution.py:414
  34.6 8.9 %collective-permute-start.6 = (bf16[96,416]{1,0:T(8,128)(2,1)S(1)}, bf16[96,416]{1,0:T(8,128)(2,1)S(1)}, u32[]{:S(2)}, u32[]{:S(2)}) collective-permute-start(bf16[96,416]{1,0:T(8,128)(2,1)S(1)} %get-tuple-element.54), channel_id=1, source_target_pairs={{0,1},{1,0},{2,3},{3,2},{4,5},{5,4},{6,7},{7,6},{8,9},{9,8},{10,11... | collective-permute-start | bytes 239624 | tf_op jit(solution)/shard_map/ppermute | solution.py:413
  36.4 7.1 %collective-permute-start.7 = (bf16[96,416]{1,0:T(8,128)(2,1)S(1)}, bf16[96,416]{1,0:T(8,128)(2,1)S(1)}, u32[]{:S(2)}, u32[]{:S(2)}) collective-permute-start(bf16[96,416]{1,0:T(8,128)(2,1)S(1)} %get-tuple-element.55), channel_id=1, source_target_pairs={{1,2},{3,4},{5,6},{7,8},{9,10},{11,12},{13,14},{15,16},{17,18},{19... | collective-permute-start | bytes 239624 | tf_op jit(solution)/shard_map/ppermute | solution.py:414
  42.5 1.0 copy-start.8
  50.7 2.3 %collective-permute-start.8 = (bf16[768,512]{1,0:T(8,128)(2,1)S(1)}, bf16[768,512]{1,0:T(8,128)(2,1)S(1)}, u32[]{:S(2)}, u32[]{:S(2)}) collective-permute-start(bf16[768,512]{1,0:T(8,128)(2,1)S(1)} %get-tuple-element.68), channel_id=1, source_target_pairs={{0,64},{64,0},{1,65},{65,1},{2,66},{66,2},{3,67},{67,3},{4,68},{68... | collective-permute-start | bytes 2359304 | tf_op jit(solution)/shard_map/ppermute | solution.py:496
  54.1 27.9 %all-to-all-start = ((bf16[16,48,512]{2,1,0:T(8,128)(2,1)}), bf16[16,48,512]{2,1,0:T(8,128)(2,1)S(1)}, u32[]{:S(2)}, u32[]{:S(2)}) async-start(bf16[16,48,512]{2,1,0:T(8,128)(2,1)} %bitcast.32), calls=%async_computation | async-start | bytes 1572864 | tf_op jit(solution)/shard_map/all_to_all | solution.py:500
  68.3 13.9 %collective-permute-start.10 = (bf16[64,208]{1,0:T(8,128)(2,1)S(1)}, bf16[64,208]{1,0:T(8,128)(2,1)S(1)}, u32[]{:S(2)}, u32[]{:S(2)}) collective-permute-start(bf16[64,208]{1,0:T(8,128)(2,1)S(1)} %get-tuple-element.137), channel_id=1, source_target_pairs={{64,128},{128,64},{65,129},{129,65},{66,130},{130,66},{67,131},{13... | collective-permute-start | bytes 79880 | tf_op jit(solution)/shard_map/ppermute | solution.py:414
  72.2 10.0 %collective-permute-start.9 = (bf16[64,208]{1,0:T(8,128)(2,1)S(1)}, bf16[64,208]{1,0:T(8,128)(2,1)S(1)}, u32[]{:S(2)}, u32[]{:S(2)}) collective-permute-start(bf16[64,208]{1,0:T(8,128)(2,1)S(1)} %get-tuple-element.138), channel_id=1, source_target_pairs={{0,64},{64,0},{128,192},{192,128},{1,65},{65,1},{129,193},{193,129... | collective-permute-start | bytes 79880 | tf_op jit(solution)/shard_map/ppermute | solution.py:413
  82.9 15.4 %all-to-all-start.1 = ((bf16[8,48,512]{2,1,0:T(8,128)(2,1)}), bf16[8,48,512]{2,1,0:T(8,128)(2,1)S(1)}, u32[]{:S(2)}, u32[]{:S(2)}) async-start(bf16[8,48,512]{2,1,0:T(8,128)(2,1)} %broadcast_in_dim.22), calls=%async_computation.1 | async-start | bytes 786432 | tf_op jit(solution)/shard_map/all_to_all | solution.py:504
  87.6 10.8 %collective-permute-start.11 = (bf16[48,208]{1,0:T(8,128)(2,1)S(1)}, bf16[48,208]{1,0:T(8,128)(2,1)S(1)}, u32[]{:S(2)}, u32[]{:S(2)}) collective-permute-start(bf16[48,208]{1,0:T(8,128)(2,1)S(1)} %get-tuple-element.75), channel_id=1, source_target_pairs={{0,1},{1,0},{2,3},{3,2},{4,5},{5,4},{6,7},{7,6},{8,9},{9,8},{10,11... | collective-permute-start | bytes 59912 | tf_op jit(solution)/shard_map/ppermute | solution.py:413
  89.2 9.2 %collective-permute-start.12 = (bf16[48,208]{1,0:T(8,128)(2,1)S(1)}, bf16[48,208]{1,0:T(8,128)(2,1)S(1)}, u32[]{:S(2)}, u32[]{:S(2)}) collective-permute-start(bf16[48,208]{1,0:T(8,128)(2,1)S(1)} %get-tuple-element.76), channel_id=1, source_target_pairs={{1,2},{3,4},{5,6},{7,8},{9,10},{11,12},{13,14},{15,16},{17,18},{19... | collective-permute-start | bytes 59912 | tf_op jit(solution)/shard_map/ppermute | solution.py:414
  99.4 21.3 %all-to-all-start.2 = ((bf16[16,48,512]{2,1,0:T(8,128)(2,1)}), bf16[16,48,512]{2,1,0:T(8,128)(2,1)S(1)}, u32[]{:S(2)}, u32[]{:S(2)}) async-start(bf16[16,48,512]{2,1,0:T(8,128)(2,1)} %broadcast_in_dim.23), calls=%async_computation.2 | async-start | bytes 1572864 | tf_op jit(solution)/shard_map/all_to_all | solution.py:508
  108.1 1.2 copy-start.7
  109.3 1.2 copy-start.9
  120.7 4.7 %collective-permute-start.13 = (bf16[768,512]{1,0:T(8,128)(2,1)S(1)}, bf16[768,512]{1,0:T(8,128)(2,1)S(1)}, u32[]{:S(2)}, u32[]{:S(2)}) collective-permute-start(bf16[768,512]{1,0:T(8,128)(2,1)S(1)} %bitcast.89), channel_id=1, source_target_pairs={{0,64},{64,0},{1,65},{65,1},{2,66},{66,2},{3,67},{67,3},{4,68},{68... | collective-permute-start | bytes 2359304 | tf_op jit(solution)/shard_map/ppermute | solution.py:510

commit v4 on v3

--- a/solution.py
+++ b/solution.py
@@ -13,7 +13,7 @@
 BF = jnp.bfloat16
 F4 = jnp.float32
 LIMIT = 28 * 1024 * 1024
-RED, MIXC, MIXF, TAPC, TAPF, TOTAL = 0, 832, 1248, 1456, 1488, 1536
+MIXC, TAPC, TOTAL, FINE = 832, 1248, 1280, 224
 LANES = 512
 SOURCE = ((2, 0, 1), (0, 1, 3))
 
@@ -213,6 +213,13 @@
         gtaps_out[at : at + 1, :] = jnp.sum(sums[at], axis=0, keepdims=True)
 
 
+def piece(j, chans, wide):
+    room = LANES - wide
+    return picker(
+        chans, LANES, lambda row: jnp.where(row // room == j, wide + row % room, -1)
+    )
+
+
 def edge_message(outs, source, bases, ats, near_ref, away_ref, middle):
     for out, at in zip(outs, ats):
         total = 0.0
@@ -235,6 +242,31 @@
     at = jnp.where(flags_ref[1] == 0, 28, 0)
     middle = act_ref[...].reshape(512, act_ref.shape[2])
     edge_message((near_out, away_out), source, (base, 20 - base), (at, 28 - at), near_ref, away_ref, middle)
+
+
+def input_message(flags_ref, near_ref, away_ref, cot_ref, slide_ref, near_out, away_out):
+    chans = slide_ref.shape[2]
+    tall = near_out.shape[0] - 48
+    edge = near_ref.shape[0] - 64
+
+    def source(at, base, row):
+        if base is None:
+            r = row - 1
+            return jnp.where(jnp.logical_and(r >= 0, r < 32), r * 64 + at * 63, -1)
+        return jnp.where(row == base, at * 63, -1)
+
+    coarse_message(
+        flags_ref, near_ref.at[:edge], away_ref.at[:edge], cot_ref, near_out.at[:tall], away_out.at[:tall]
+    )
+    base = jnp.where(flags_ref[0] == 0, 33, 0)
+    at = jnp.where(flags_ref[1] == 0, 1, 0)
+    middle = slide_ref[...].reshape(2048, chans)
+    for out in (near_out, away_out):
+        out[tall:, :] = jnp.zeros((48, out.shape[1]), BF)
+    edge_message(
+        (near_out.at[tall:, :chans], away_out.at[tall:, :chans]), source, (base, 33 - base), (at, 1 - at),
+        near_ref.at[edge:, :chans], away_ref.at[edge:, :chans], middle,
+    )
 
 
 def fine_message(flags_ref, near_ref, away_ref, ddepth_ref, near_out, away_out):
@@ -300,14 +332,17 @@
     lax.fori_loop(0, 16, conv, 0, unroll=2)
     flat = depth[...].reshape(512, wide)
     section_out[...] = (reduced_ref[...].reshape(512, wide).astype(F4) + dot(flat, mix_ref[...])).astype(BF).reshape(16, 32, wide)
-    fine = gmixf_ref.shape[0]
-    packed[...] = jnp.zeros_like(packed)
-    packed[RED:MIXC, 0:wide] = gred_ref[...]
-    packed[MIXC:MIXF, 0:wide] = dot_tn(flat, cot_ref[...].reshape(512, wide)).astype(BF)
-    packed[MIXF:TAPC, 0:fine] = gmixf_ref[...].astype(BF)
+    fine = jnp.concatenate([gmixf_ref[...], gtapsf_ref[...]], axis=0).astype(BF)
+    spread = picker(wide, LANES, lambda row: row)
+    for j in range(3):
+        rows_of = slice(j * FINE, (j + 1) * FINE)
+        both = dot(gred_ref[rows_of, :], spread) + dot(fine, piece(j, fine.shape[1], wide))
+        packed[rows_of, :] = both.astype(BF)
+    packed[3 * FINE :, :] = jnp.zeros((TOTAL - 3 * FINE, LANES), BF)
+    packed[3 * FINE : MIXC, 0:wide] = gred_ref[3 * FINE :, :]
+    packed[MIXC:TAPC, 0:wide] = dot_tn(flat, cot_ref[...].reshape(512, wide)).astype(BF)
     taps = jnp.concatenate([jnp.sum(sums[...], axis=1), jnp.zeros((7, wide), F4)], axis=0)
-    packed[TAPC:TAPF, 0:wide] = taps.astype(BF)
-    packed[TAPF : TAPF + 16, 0:fine] = gtapsf_ref[...].astype(BF)
+    packed[TAPC:TOTAL, 0:wide] = taps.astype(BF)
     core = flags_ref[2]
     half = TOTAL // 2
     mine_out[...] = packed[pl.ds(pl.multiple_of(core * half, half), half), :]
@@ -323,15 +358,18 @@
     packed[pl.ds(pl.multiple_of((1 - core) * half, half), half), :] = far_ref[...]
     chans = mixf_out.shape[0]
     wide = mixc_out.shape[0]
-    red_out[...] = (packed[RED:MIXC, 0:wide].astype(F4) * coarse).T
-    mixc_out[...] = packed[MIXC:MIXF, 0:wide].astype(F4) * coarse
-    mixf_out[...] = packed[MIXF:TAPC, 0:chans].astype(F4) * fine
-    taps = packed[TAPC:TAPF, 0:wide].astype(F4) * coarse
+    red_out[...] = (packed[0:MIXC, 0:wide].astype(F4) * coarse).T
+    mixc_out[...] = packed[MIXC:TAPC, 0:wide].astype(F4) * coarse
+    total = 0.0
+    for j in range(3):
+        total = total + dot_nt(packed[j * FINE : (j + 1) * FINE, :], piece(j, chans, wide))
+    mixf_out[...] = total[:chans] * fine
+    taps = total[chans:] * fine
+    for a in range(3):
+        tapsf_out[a] = taps[3 * a : 3 * a + 3]
+    taps = packed[TAPC:TOTAL, 0:wide].astype(F4) * coarse
     for a in range(5):
         tapsc_out[a] = taps[5 * a : 5 * a + 5]
-    taps = packed[TAPF : TAPF + 16, 0:chans].astype(F4) * fine
-    for a in range(3):
-        tapsf_out[a] = taps[3 * a : 3 * a + 3]
 
 
 def fine_backward(
@@ -415,30 +453,11 @@
     )
 
 
-def swap(first, last, axes):
-    even = lax.axis_index(axes) % 2 == 0
-    near, away = trade(first, last, axes)
-    return jnp.where(even, away, near), jnp.where(even, near, away)
-
-
 def coarse_edges(coarse):
     height, breadth, wide = coarse.shape
     return coarse[:4].reshape(4 * breadth, wide), coarse[-4:].reshape(4 * breadth, wide)
 
 
-def coarse_columns(top, coarse, bottom):
-    breadth = coarse.shape[1]
-
-    def pick(at):
-        parts = [
-            jnp.concatenate([top[:, at + s], coarse[:, at + s], bottom[:, at + s]], axis=0)
-            for s in range(4)
-        ]
-        return jnp.concatenate(parts, axis=0)
-
-    return pick(0), pick(breadth - 4)
-
-
 def coarse_sides(left, right):
     wide = left.shape[1]
 
@@ -446,13 +465,6 @@
         return block.reshape(4, -1, wide).transpose(1, 0, 2)
 
     return sides(spread(left), spread(right))
-
-
-def fine_columns(low, pixels_left, pixels_right, high):
-    end = low.shape[0] - 1
-    left = jnp.concatenate([low[:1], pixels_left, high[:1]], axis=0)
-    right = jnp.concatenate([low[end:], pixels_right, high[end:]], axis=0)
-    return left, right
 
 
 def fine_sides(left, right):
@@ -464,23 +476,26 @@
     return jnp.concatenate([coarse, widened], axis=0)
 
 
-def input_halos(coarse, fine):
+def input_halos(flags, coarse, fine):
     height, breadth, wide = coarse.shape
     chans = fine.shape[-1]
     first, last = coarse_edges(coarse)
     split = 4 * breadth
-    low, high = swap(stack_rows(first, fine[0]), stack_rows(last, fine[-1]), ROWS)
+    near, away = trade(stack_rows(first, fine[0]), stack_rows(last, fine[-1]), ROWS)
+    tall = 4 * (height + 8)
+    shape = (tall + 48, wide)
+    message = call(
+        input_message, [(shape, BF), (shape, BF)], [], 10_000_000, flags, near, away, coarse, fine
+    )
+    even = lax.axis_index(ROWS) % 2 == 0
+    low, high = jnp.where(even, away, near), jnp.where(even, near, away)
     top, bottom = low[:split].reshape(4, breadth, wide), high[:split].reshape(4, breadth, wide)
-    fine_low, fine_high = low[split:, :chans], high[split:, :chans]
-    coarse_first, coarse_last = coarse_columns(top, coarse, bottom)
-    fine_first, fine_last = fine_columns(fine_low, fine[:, 0], fine[:, -1], fine_high)
-    left, right = swap(
-        stack_rows(coarse_first, fine_first), stack_rows(coarse_last, fine_last), COLS
-    )
-    split = 4 * (height + 8)
-    side_coarse = coarse_sides(left[:split], right[:split])
-    side_fine = fine_sides(left[split:, :chans], right[split:, :chans])
-    return top, bottom, side_coarse, fine_low, fine_high, side_fine
+    near, away = send(*message, COLS)
+    even = lax.axis_index(COLS) % 2 == 0
+    left, right = jnp.where(even, away, near), jnp.where(even, near, away)
+    side_coarse = coarse_sides(left[:tall], right[:tall])
+    side_fine = fine_sides(left[tall : tall + 34, :chans], right[tall : tall + 34, :chans])
+    return top, bottom, side_coarse, low[split:, :chans], high[split:, :chans], side_fine
 
 
 def hold(value, *others):
@@ -524,7 +539,7 @@
     flags = jnp.stack(
         [lax.axis_index(ROWS) % 2, lax.axis_index(COLS) % 2, lax.axis_index("core")]
     ).astype(jnp.int32)
-    ctop, cbottom, clr, top, bottom, lr = input_halos(cotangent, slide_pixels)
+    ctop, cbottom, clr, top, bottom, lr = input_halos(flags, cotangent, slide_pixels)
     top, bottom = top[None], bottom[None]
 
     slide, depth, pre, reduced, act = call(

time: 129 us -> 123 us (0.953)
  local copies, waits for them, and re-layouts: 10.7 us -> 6.57 us
  waiting for transfers between devices: 32.3 us -> 29 us
  Pallas kernels: 30.5 us -> 32.6 us
    pallas_call x8 -> x9, Pallas kernels: 30.5 us -> 32.6 us  [call(): pl.pallas_call(body, out_shape=[jax.ShapeDtypeStruct(shape, kind) for sha...]
    unnamed x31 -> x21, local copies, waits for them, and re-layouts: 4.28 us -> 2.84 us
    slice x7 -> x2, local copies, waits for them, and re-layouts: 1.39 us -> 0.02 us  [input_halos(): side_coarse = coarse_sides(left[:tall], right[:tall])]
    all_to_all x1, waiting for transfers between devices: 8.5 us -> 7.13 us  [reduce_terms(): lax.all_to_all(jnp.broadcast_to(mine, (depth, chunk, lanes)), 'z', 0, 0,...]
    all_to_all x1, waiting for transfers between devices: 9.76 us -> 8.44 us  [reduce_terms(): got = lax.all_to_all(mine, PLANE, 0, 0, tiled=True)]
where the time goes in v4:
time: 123 us; the launch traced here: 122 us
  starting transfers between devices  51 us (41%)
  Pallas kernels  32.6 us (27%)
  waiting for transfers between devices  29 us (24%)
  local copies, waits for them, and re-layouts  6.57 us (5%)
  other arithmetic  1.64 us (1%)
    pallas_call x9, Pallas kernels, call(): pl.pallas_call(body, out_shape=[jax.ShapeDtypeStruct(shape, kind) for sha...  32.6 us
    all_to_all x1, starting transfers between devices, reduce_terms(): got = lax.all_to_all(mine, PLANE, 0, 0, tiled=True)  14.2 us
    ppermute x6, starting transfers between devices, send(): lax.ppermute(away, axes, far)  12.3 us
    ppermute x6, starting transfers between devices, send(): lax.ppermute(near, axes, [(i, i ^ 1) for i in range(count)])  9.76 us
    all_to_all x1, waiting for transfers between devices, reduce_terms(): got = lax.all_to_all(mine, PLANE, 0, 0, tiled=True)  8.44 us
    all_to_all x1, starting transfers between devices, reduce_terms(): lax.all_to_all(jnp.broadcast_to(mine, (plane, chunk, lanes)), PLANE, 0, 0...  7.78 us
    all_to_all x1, waiting for transfers between devices, reduce_terms(): lax.all_to_all(jnp.broadcast_to(mine, (depth, chunk, lanes)), 'z', 0, 0,...  7.13 us
    all_to_all x1, waiting for transfers between devices, reduce_terms(): lax.all_to_all(jnp.broadcast_to(mine, (plane, chunk, lanes)), PLANE, 0, 0...  3.8 us
  transfers between devices with their start and end apart: 17, of which 7 were waited for; matrix products, arithmetic and copies ran while one was open for 2% of the time, Pallas kernels for 13%

profile of v4, /device:TPU:1, one launch (start us, length us, event | category | flops | bytes accessed | tf_op | source)
XLA Modules:
  0.0 121.9 jit_solution(3990396013224981597)
XLA Ops:
  0.7 0.0 copy-start.1
  0.7 0.9 slice_bitcast_fusion.3
  1.6 1.0 fusion.11
  2.6 0.1 broadcast_select_fusion.2
  2.6 3.3 %collective-permute-start.1 = (bf16[192,416]{1,0:T(8,128)(2,1)S(1)}, bf16[192,416]{1,0:T(8,128)(2,1)S(1)}, u32[]{:S(2)}, u32[]{:S(2)}) collective-permute-start(bf16[192,416]{1,0:T(8,128)(2,1)S(1)} %get-tuple-element.105), channel_id=1, source_target_pairs={{0,64},{64,0},{128,192},{192,128},{1,65},{65,1},{129,193},{193,129... | collective-permute-start | bytes 479240 | tf_op jit(solution)/shard_map/ppermute | solution.py:451
  6.0 1.9 %collective-permute-start = (bf16[192,416]{1,0:T(8,128)(2,1)S(1)}, bf16[192,416]{1,0:T(8,128)(2,1)S(1)}, u32[]{:S(2)}, u32[]{:S(2)}) collective-permute-start(bf16[192,416]{1,0:T(8,128)(2,1)S(1)} %get-tuple-element.106), channel_id=1, source_target_pairs={{64,128},{128,64},{65,129},{129,65},{66,130},{130,66},{67,131},{13... | collective-permute-start | bytes 479240 | tf_op jit(solution)/shard_map/ppermute | solution.py:452
  7.9 1.6 %copy.36.weight_ref = bf16[832,416]{1,0:T(8,128)(2,1)S(1)} copy(bf16[832,416]{0,1:T(8,128)(2,1)} %param.10) | data formatting | bytes 1384448 | tf_op args[3]
  9.5 0.1 pad_add_fusion.flags_ref
  9.5 0.0 collective-permute-done.1.near_ref
  9.6 3.4 %collective-permute-done.away_ref = bf16[192,416]{1,0:T(8,128)(2,1)S(1)} collective-permute-done((bf16[192,416]{1,0:T(8,128)(2,1)S(1)}, bf16[192,416]{1,0:T(8,128)(2,1)S(1)}, u32[]{:S(2)}, u32[]{:S(2)}) %collective-permute-start) | collective-permute-done | bytes 159776 | tf_op jit(solution)/shard_map/ppermute | solution.py:452
  12.9 1.3 %shard_map.126 = (bf16[144,416]{1,0:T(8,128)(2,1)S(1)}, bf16[144,416]{1,0:T(8,128)(2,1)S(1)}) custom-call(s32[3]{0:T(128)S(1)} %pad_add_fusion.flags_ref, bf16[192,416]{1,0:T(8,128)(2,1)S(1)} %collective-permute-done.1.near_ref, bf16[192,416]{1,0:T(8,128)(2,1)S(1)} %collective-permute-done.away_ref, bf16[16,32,416]{2,1,0:T(8,128)(2,1)S(1)} %copy-done.1, ...), custom_call_target="tpu_custom_call" | custom-call | flops 10000000 | bytes 8000000 | tf_op jit(solution)/shard_map/pallas_call | solution.py:430
  14.3 0.7 collective-permute-start.2
  15.0 2.9 %collective-permute-start.3 = (bf16[144,416]{1,0:T(8,128)(2,1)S(1)}, bf16[144,416]{1,0:T(8,128)(2,1)S(1)}, u32[]{:S(2)}, u32[]{:S(2)}) collective-permute-start(bf16[144,416]{1,0:T(8,128)(2,1)S(1)} %get-tuple-element.52), channel_id=1, source_target_pairs={{0,1},{1,0},{2,3},{3,2},{4,5},{5,4},{6,7},{7,6},{8,9},{9,8},{10,11... | collective-permute-start | bytes 359432 | tf_op jit(solution)/shard_map/ppermute | solution.py:451
  17.9 0.0 copy-start.3
  17.9 0.0 copy-start.5
  18.0 0.0 collective-permute-done.2
  18.0 2.4 %collective-permute-done.3 = bf16[144,416]{1,0:T(8,128)(2,1)S(1)} collective-permute-done((bf16[144,416]{1,0:T(8,128)(2,1)S(1)}, bf16[144,416]{1,0:T(8,128)(2,1)S(1)}, u32[]{:S(2)}, u32[]{:S(2)}) %collective-permute-start.3) | collective-permute-done | bytes 119840 | tf_op jit(solution)/shard_map/ppermute | solution.py:451
  20.5 0.1 fusion.7.lr_ref.lrf_ref
  20.7 3.7 %shard_map.127 = (bf16[4,16,32,208]{3,2,1,0:T(8,128)(2,1)S(1)}, bf16[4,16,32,208]{3,2,1,0:T(8,128)(2,1)S(1)}, bf16[4,512,208]{2,1,0:T(8,128)(2,1)S(1)}, bf16[512...) custom-call(bf16[32,64,208]{2,1,0:T(8,128)(2,1)S(1)} %copy-done, bf16[1,64,208]{2,1,0:T(8,128)(2,1)S(1)} %get-tuple-element.112.top_ref, ...), custom_call_target="tpu_custom_call" | custom-call | flops 4000000000 | bytes 8000000 | tf_op jit(solution)/shard_map/pallas_call | solution.py:430
  24.3 0.0 copy-start.6
  24.3 0.0 copy-start.2
  24.4 0.0 copy-start.4
  24.4 0.1 collective-permute-start.4
  24.5 4.4 %collective-permute-start.5 = (bf16[128,416]{1,0:T(8,128)(2,1)S(1)}, bf16[128,416]{1,0:T(8,128)(2,1)S(1)}, u32[]{:S(2)}, u32[]{:S(2)}) collective-permute-start(bf16[128,416]{1,0:T(8,128)(2,1)S(1)} %bitcast.48), channel_id=1, source_target_pairs={{64,128},{128,64},{65,129},{129,65},{66,130},{130,66},{67,131},{13... | collective-permute-start | bytes 319496 | tf_op jit(solution)/shard_map/ppermute | solution.py:452
  28.9 0.1 copy_bitcast_fusion
  29.0 0.1 fusion.4.lr_ref
  29.1 4.3 %shard_map.128 = (bf16[16,32,416]{2,1,0:T(8,128)(2,1)S(1)}, bf16[16,32,416]{2,1,0:T(8,128)(2,1)S(1)}) custom-call(bf16[16,32,416]{2,1,0:T(8,128)(2,1)S(1)} %copy-done.1, bf16[8,32,416]{2,1,0:T(8,128)(2,1)S(1)} %pad_maximum_fusion.tb_ref, bf16[24,16,416]{2,1,0:T(8,128)(2,1)S(1)} %fusion.4.lr_ref, bf16[416,416]{1,0:T(8,128)(2,1)S(1)} %copy-done.2, ...), custom_call_target="tpu_custom_call" | custom-call | flops 8000000000 | bytes 8000000 | tf_op jit(solution)/shard_map/pallas_call | solution.py:430
  33.4 0.0 collective-permute-done.4.near_ref
  33.4 0.0 collective-permute-done.5.away_ref
  33.5 1.0 shard_map.129
  34.4 1.8 %collective-permute-start.6 = (bf16[96,416]{1,0:T(8,128)(2,1)S(1)}, bf16[96,416]{1,0:T(8,128)(2,1)S(1)}, u32[]{:S(2)}, u32[]{:S(2)}) collective-permute-start(bf16[96,416]{1,0:T(8,128)(2,1)S(1)} %get-tuple-element.58), channel_id=1, source_target_pairs={{0,1},{1,0},{2,3},{3,2},{4,5},{5,4},{6,7},{7,6},{8,9},{9,8},{10,11... | collective-permute-start | bytes 239624 | tf_op jit(solution)/shard_map/ppermute | solution.py:451
  36.3 0.8 collective-permute-start.7
  37.1 5.3 %shard_map.130 = (bf16[4,16,32,208]{3,2,1,0:T(8,128)(2,1)S(1)}, bf16[4,16,32,208]{3,2,1,0:T(8,128)(2,1)S(1)}, bf16[832,416]{1,0:T(8,128)(2,1)S(1)}, f32[208,208]{1,0:T(8,128)S(1)}, f32[16,208]{1,0:T(8,128)S(1)}) custom-call(bf16[512,416]{1,0:T(8,128)(2,1)S(1)} %bitcast.40, bf16[4,512,208]{2,1,0:T(8,128)(2,1)S(1)} %get-tuple-element.61.pre_ref, ...), custom_call_target="tpu_custom_call" | custom-call | flops 8000000000 | bytes 8000000 | tf_op jit(solution)/shard_map/pallas_call | solution.py:430
  42.4 0.0 copy-start.8
  42.4 0.0 collective-permute-done.6.nside_ref
  42.4 0.0 collective-permute-done.7.aside_ref
  42.4 7.8 %shard_map.131 = (bf16[16,32,416]{2,1,0:T(8,128)(2,1)}, bf16[640,512]{1,0:T(8,128)(2,1)S(1)}, bf16[640,512]{1,0:T(8,128)(2,1)S(1)}) custom-call(s32[3]{0:T(128)S(1)} %pad_add_fusion.flags_ref, bf16[16,32,416]{2,1,0:T(8,128)(2,1)S(1)} %get-tuple-element.53.act_ref, bf16[128,416]{1,0:T(8,128)(2,1)S(1)} %collective-permute-done.4.near_ref, ...), custom_call_target="tpu_custom_call" | custom-call | flops 4000000000 | bytes 8000000 | tf_op jit(solution)/shard_map/pallas_call | solution.py:430
  50.2 0.0 collective-permute-start.8
  50.2 2.1 %collective-permute-done.8 = bf16[640,512]{1,0:T(8,128)(2,1)S(1)} collective-permute-done((bf16[640,512]{1,0:T(8,128)(2,1)S(1)}, bf16[640,512]{1,0:T(8,128)(2,1)S(1)}, u32[]{:S(2)}, u32[]{:S(2)}) %collective-permute-start.8) | collective-permute-done | bytes 655392 | tf_op jit(solution)/shard_map/ppermute | solution.py:511
  52.3 1.0 add.43
  53.3 14.2 %all-to-all-start = ((bf16[16,40,512]{2,1,0:T(8,128)(2,1)}), bf16[16,40,512]{2,1,0:T(8,128)(2,1)S(1)}, u32[]{:S(2)}, u32[]{:S(2)}) async-start(bf16[16,40,512]{2,1,0:T(8,128)(2,1)} %bitcast.41), calls=%async_computation | async-start | bytes 1310720 | tf_op jit(solution)/shard_map/all_to_all | solution.py:515
  67.5 3.9 %collective-permute-start.10 = (bf16[64,208]{1,0:T(8,128)(2,1)S(1)}, bf16[64,208]{1,0:T(8,128)(2,1)S(1)}, u32[]{:S(2)}, u32[]{:S(2)}) collective-permute-start(bf16[64,208]{1,0:T(8,128)(2,1)S(1)} %get-tuple-element.109), channel_id=1, source_target_pairs={{64,128},{128,64},{65,129},{129,65},{66,130},{130,66},{67,131},{13... | collective-permute-start | bytes 79880 | tf_op jit(solution)/shard_map/ppermute | solution.py:452
  71.4 0.1 collective-permute-start.9
  71.5 8.4 %all-to-all-done = bf16[16,40,512]{2,1,0:T(8,128)(2,1)S(1)} async-done(((bf16[16,40,512]{2,1,0:T(8,128)(2,1)}), bf16[16,40,512]{2,1,0:T(8,128)(2,1)S(1)}, u32[]{:S(2)}, u32[]{:S(2)}) %all-to-all-start) | async-done | bytes 655392 | tf_op jit(solution)/shard_map/all_to_all | solution.py:515
  79.9 0.1 reduce_sum.24
  80.0 0.0 collective-permute-done.10.away_ref
  80.0 0.0 collective-permute-done.9.near_ref
  80.0 0.7 broadcast_in_dim.22
  80.8 3.7 %all-to-all-start.1 = ((bf16[8,40,512]{2,1,0:T(8,128)(2,1)}), bf16[8,40,512]{2,1,0:T(8,128)(2,1)S(1)}, u32[]{:S(2)}, u32[]{:S(2)}) async-start(bf16[8,40,512]{2,1,0:T(8,128)(2,1)} %broadcast_in_dim.22), calls=%async_computation.1 | async-start | bytes 655360 | tf_op jit(solution)/shard_map/all_to_all | solution.py:519
  84.5 1.1 shard_map.132
  85.6 1.5 %collective-permute-start.11 = (bf16[48,208]{1,0:T(8,128)(2,1)S(1)}, bf16[48,208]{1,0:T(8,128)(2,1)S(1)}, u32[]{:S(2)}, u32[]{:S(2)}) collective-permute-start(bf16[48,208]{1,0:T(8,128)(2,1)S(1)} %get-tuple-element.79), channel_id=1, source_target_pairs={{0,1},{1,0},{2,3},{3,2},{4,5},{5,4},{6,7},{7,6},{8,9},{9,8},{10,11... | collective-permute-start | bytes 59912 | tf_op jit(solution)/shard_map/ppermute | solution.py:451
  87.1 0.7 collective-permute-start.12
  87.8 7.1 %all-to-all-done.1 = bf16[8,40,512]{2,1,0:T(8,128)(2,1)S(1)} async-done(((bf16[8,40,512]{2,1,0:T(8,128)(2,1)}), bf16[8,40,512]{2,1,0:T(8,128)(2,1)S(1)}, u32[]{:S(2)}, u32[]{:S(2)}) %all-to-all-start.1) | async-done | bytes 327712 | tf_op jit(solution)/shard_map/all_to_all | solution.py:519
  95.0 0.0 collective-permute-done.11.nside_ref
  95.0 0.0 collective-permute-done.12.aside_ref
  95.0 0.9 broadcast_in_dim.23
  95.9 7.8 %all-to-all-start.2 = ((bf16[16,40,512]{2,1,0:T(8,128)(2,1)}), bf16[16,40,512]{2,1,0:T(8,128)(2,1)S(1)}, u32[]{:S(2)}, u32[]{:S(2)}) async-start(bf16[16,40,512]{2,1,0:T(8,128)(2,1)} %broadcast_in_dim.23), calls=%async_computation.2 | async-start | bytes 1310720 | tf_op jit(solution)/shard_map/all_to_all | solution.py:523
  103.7 0.0 copy-start.9
  103.7 1.2 copy-done.9
  104.9 5.6 %shard_map.133 = bf16[32,64,208]{2,1,0:T(8,128)(2,1)} custom-call(s32[3]{0:T(128)S(1)} %pad_add_fusion.flags_ref, bf16[4,16,32,208]{3,2,1,0:T(8,128)(2,1)S(1)} %get-tuple-element.73.ddepth_ref, bf16[64,208]{1,0:T(8,128)(2,1)S(1)} %collective-permute-done.9.near_ref, bf16[64,208]{1,0:T(8,128)(2,1)S(1)} %collective-permute-done.10.away_ref, ...), custom_call_target="tpu_custom_call" | custom-call | flops 2000000000 | bytes 8000000 | tf_op jit(solution)/shard_map/pallas_call | solution.py:430
  110.5 3.8 %all-to-all-done.2 = bf16[16,40,512]{2,1,0:T(8,128)(2,1)S(1)} async-done(((bf16[16,40,512]{2,1,0:T(8,128)(2,1)}), bf16[16,40,512]{2,1,0:T(8,128)(2,1)S(1)}, u32[]{:S(2)}, u32[]{:S(2)}) %all-to-all-start.2) | async-done | bytes 655392 | tf_op jit(solution)/shard_map/all_to_all | solution.py:523
  114.2 3.3 %collective-permute-start.13 = (bf16[640,512]{1,0:T(8,128)(2,1)S(1)}, bf16[640,512]{1,0:T(8,128)(2,1)S(1)}, u32[]{:S(2)}, u32[]{:S(2)}) collective-permute-start(bf16[640,512]{1,0:T(8,128)(2,1)S(1)} %bitcast.35), channel_id=1, source_target_pairs={{0,64},{64,0},{1,65},{65,1},{2,66},{66,2},{3,67},{67,3},{4,68},{68... | collective-permute-start | bytes 1966088 | tf_op jit(solution)/shard_map/ppermute | solution.py:525
  117.5 1.7 %collective-permute-done.13.far_ref = bf16[640,512]{1,0:T(8,128)(2,1)S(1)} collective-permute-done((bf16[640,512]{1,0:T(8,128)(2,1)S(1)}, bf16[640,512]{1,0:T(8,128)(2,1)S(1)}, u32[]{:S(2)}, u32[]{:S(2)}) %collective-permute-start.13) | collective-permute-done | bytes 655392 | tf_op jit(solution)/shard_map/ppermute | solution.py:525
  119.2 2.7 %shard_map.134 = (f32[3,3,208]{2,1,0:T(4,128)}, f32[208,208]{1,0:T(8,128)}, f32[416,832]{1,0:T(8,128)}, f32[5,5,416]{2,1,0:T(8,128)}, f32[416,416]{1,0:T(8,128)}) custom-call(s32[3]{0:T(128)S(1)} %pad_add_fusion.flags_ref, bf16[640,512]{1,0:T(8,128)(2,1)S(1)} %bitcast.36, bf16[640,512]{1,0:T(8,128)(2,1)S(1)} %collective-permute-done.13.far_ref), custom_call_target="tpu_custom_call" | custom-call | flops 1000000 | bytes 8000000 | tf_op jit(solution)/shard_map/pallas_call | solution.py:430
  (26 shorter events, 0.3 us)
Async XLA Ops:
  0.6 12.3 %copy-start = (bf16[32,64,208]{2,1,0:T(8,128)(2,1)S(1)}, bf16[32,64,208]{2,1,0:T(8,128)(2,1)}, u32[]{:S(2)}) copy-start(bf16[32,64,208]{2,1,0:T(8,128)(2,1)} %slide_ref.5) | copy-start | bytes 2555908
  0.7 12.3 %copy-start.1 = (bf16[16,32,416]{2,1,0:T(8,128)(2,1)S(1)}, bf16[16,32,416]{2,1,0:T(8,128)(2,1)}, u32[]{:S(2)}) copy-start(bf16[16,32,416]{2,1,0:T(8,128)(2,1)} %cot_ref.5) | copy-start | bytes 1277956
  2.6 6.9 %collective-permute-start.1 = (bf16[192,416]{1,0:T(8,128)(2,1)S(1)}, bf16[192,416]{1,0:T(8,128)(2,1)S(1)}, u32[]{:S(2)}, u32[]{:S(2)}) collective-permute-start(bf16[192,416]{1,0:T(8,128)(2,1)S(1)} %get-tuple-element.105), channel_id=1, source_target_pairs={{0,64},{64,0},{128,192},{192,128},{1,65},{65,1},{129,193},{193,129... | collective-permute-start | bytes 479240 | tf_op jit(solution)/shard_map/ppermute | solution.py:451
  6.0 7.0 %collective-permute-start = (bf16[192,416]{1,0:T(8,128)(2,1)S(1)}, bf16[192,416]{1,0:T(8,128)(2,1)S(1)}, u32[]{:S(2)}, u32[]{:S(2)}) collective-permute-start(bf16[192,416]{1,0:T(8,128)(2,1)S(1)} %get-tuple-element.106), channel_id=1, source_target_pairs={{64,128},{128,64},{65,129},{129,65},{66,130},{130,66},{67,131},{13... | collective-permute-start | bytes 479240 | tf_op jit(solution)/shard_map/ppermute | solution.py:452
  14.3 3.7 %collective-permute-start.2 = (bf16[144,416]{1,0:T(8,128)(2,1)S(1)}, bf16[144,416]{1,0:T(8,128)(2,1)S(1)}, u32[]{:S(2)}, u32[]{:S(2)}) collective-permute-start(bf16[144,416]{1,0:T(8,128)(2,1)S(1)} %get-tuple-element.51), channel_id=1, source_target_pairs={{1,2},{3,4},{5,6},{7,8},{9,10},{11,12},{13,14},{15,16},{17,18},{19... | collective-permute-start | bytes 359432 | tf_op jit(solution)/shard_map/ppermute | solution.py:452
  15.0 5.4 %collective-permute-start.3 = (bf16[144,416]{1,0:T(8,128)(2,1)S(1)}, bf16[144,416]{1,0:T(8,128)(2,1)S(1)}, u32[]{:S(2)}, u32[]{:S(2)}) collective-permute-start(bf16[144,416]{1,0:T(8,128)(2,1)S(1)} %get-tuple-element.52), channel_id=1, source_target_pairs={{0,1},{1,0},{2,3},{3,2},{4,5},{5,4},{6,7},{7,6},{8,9},{9,8},{10,11... | collective-permute-start | bytes 359432 | tf_op jit(solution)/shard_map/ppermute | solution.py:451
  17.9 2.8 %copy-start.3 = (bf16[208,208]{1,0:T(8,128)(2,1)S(1)}, bf16[208,208]{1,0:T(8,128)(2,1)}, u32[]{:S(2)}) copy-start(bf16[208,208]{1,0:T(8,128)(2,1)} %mix_ref.4) | copy-start | bytes 259588
  17.9 2.8 %copy-start.5 = (f32[3,3,208]{2,1,0:T(4,128)S(1)}, f32[3,3,208]{2,1,0:T(4,128)}, u32[]{:S(2)}) copy-start(f32[3,3,208]{2,1,0:T(4,128)} %taps_ref.5) | copy-start | bytes 22468
  24.3 9.1 %copy-start.6 = (bf16[4,16,32,208]{3,2,1,0:T(8,128)(2,1)}, bf16[4,16,32,208]{3,2,1,0:T(8,128)(2,1)S(1)}, u32[]{:S(2)}) copy-start(bf16[4,16,32,208]{3,2,1,0:T(8,128)(2,1)S(1)} %get-tuple-element.87.slide_ref) | copy-start | bytes 2555908
  24.3 4.8 %copy-start.2 = (bf16[416,416]{1,0:T(8,128)(2,1)S(1)}, bf16[416,416]{1,0:T(8,128)(2,1)}, u32[]{:S(2)}) copy-start(bf16[416,416]{1,0:T(8,128)(2,1)} %mix_ref.5) | copy-start | bytes 1038340
  24.4 4.8 %copy-start.4 = (f32[5,5,416]{2,1,0:T(8,128)S(1)}, f32[5,5,416]{2,1,0:T(8,128)}, u32[]{:S(2)}) copy-start(f32[5,5,416]{2,1,0:T(8,128)} %taps_ref.4) | copy-start | bytes 124804
  24.4 9.0 %collective-permute-start.4 = (bf16[128,416]{1,0:T(8,128)(2,1)S(1)}, bf16[128,416]{1,0:T(8,128)(2,1)S(1)}, u32[]{:S(2)}, u32[]{:S(2)}) collective-permute-start(bf16[128,416]{1,0:T(8,128)(2,1)S(1)} %bitcast.49), channel_id=1, source_target_pairs={{0,64},{64,0},{128,192},{192,128},{1,65},{65,1},{129,193},{193,129... | collective-permute-start | bytes 319496 | tf_op jit(solution)/shard_map/ppermute | solution.py:451
  24.5 8.9 %collective-permute-start.5 = (bf16[128,416]{1,0:T(8,128)(2,1)S(1)}, bf16[128,416]{1,0:T(8,128)(2,1)S(1)}, u32[]{:S(2)}, u32[]{:S(2)}) collective-permute-start(bf16[128,416]{1,0:T(8,128)(2,1)S(1)} %bitcast.48), channel_id=1, source_target_pairs={{64,128},{128,64},{65,129},{129,65},{66,130},{130,66},{67,131},{13... | collective-permute-start | bytes 319496 | tf_op jit(solution)/shard_map/ppermute | solution.py:452
  34.4 8.0 %collective-permute-start.6 = (bf16[96,416]{1,0:T(8,128)(2,1)S(1)}, bf16[96,416]{1,0:T(8,128)(2,1)S(1)}, u32[]{:S(2)}, u32[]{:S(2)}) collective-permute-start(bf16[96,416]{1,0:T(8,128)(2,1)S(1)} %get-tuple-element.58), channel_id=1, source_target_pairs={{0,1},{1,0},{2,3},{3,2},{4,5},{5,4},{6,7},{7,6},{8,9},{9,8},{10,11... | collective-permute-start | bytes 239624 | tf_op jit(solution)/shard_map/ppermute | solution.py:451
  36.3 6.1 %collective-permute-start.7 = (bf16[96,416]{1,0:T(8,128)(2,1)S(1)}, bf16[96,416]{1,0:T(8,128)(2,1)S(1)}, u32[]{:S(2)}, u32[]{:S(2)}) collective-permute-start(bf16[96,416]{1,0:T(8,128)(2,1)S(1)} %get-tuple-element.59), channel_id=1, source_target_pairs={{1,2},{3,4},{5,6},{7,8},{9,10},{11,12},{13,14},{15,16},{17,18},{19... | collective-permute-start | bytes 239624 | tf_op jit(solution)/shard_map/ppermute | solution.py:452
  42.4 7.8 %copy-start.8 = (bf16[4,16,32,208]{3,2,1,0:T(8,128)(2,1)}, bf16[4,16,32,208]{3,2,1,0:T(8,128)(2,1)S(1)}, u32[]{:S(2)}) copy-start(bf16[4,16,32,208]{3,2,1,0:T(8,128)(2,1)S(1)} %get-tuple-element.86.dfine_ref) | copy-start | bytes 2555908
  50.2 2.1 %collective-permute-start.8 = (bf16[640,512]{1,0:T(8,128)(2,1)S(1)}, bf16[640,512]{1,0:T(8,128)(2,1)S(1)}, u32[]{:S(2)}, u32[]{:S(2)}) collective-permute-start(bf16[640,512]{1,0:T(8,128)(2,1)S(1)} %get-tuple-element.72), channel_id=1, source_target_pairs={{0,64},{64,0},{1,65},{65,1},{2,66},{66,2},{3,67},{67,3},{4,68},{68... | collective-permute-start | bytes 1966088 | tf_op jit(solution)/shard_map/ppermute | solution.py:511
  53.3 26.6 %all-to-all-start = ((bf16[16,40,512]{2,1,0:T(8,128)(2,1)}), bf16[16,40,512]{2,1,0:T(8,128)(2,1)S(1)}, u32[]{:S(2)}, u32[]{:S(2)}) async-start(bf16[16,40,512]{2,1,0:T(8,128)(2,1)} %bitcast.41), calls=%async_computation | async-start | bytes 1310720 | tf_op jit(solution)/shard_map/all_to_all | solution.py:515
  67.5 12.5 %collective-permute-start.10 = (bf16[64,208]{1,0:T(8,128)(2,1)S(1)}, bf16[64,208]{1,0:T(8,128)(2,1)S(1)}, u32[]{:S(2)}, u32[]{:S(2)}) collective-permute-start(bf16[64,208]{1,0:T(8,128)(2,1)S(1)} %get-tuple-element.109), channel_id=1, source_target_pairs={{64,128},{128,64},{65,129},{129,65},{66,130},{130,66},{67,131},{13... | collective-permute-start | bytes 79880 | tf_op jit(solution)/shard_map/ppermute | solution.py:452
  71.4 8.6 %collective-permute-start.9 = (bf16[64,208]{1,0:T(8,128)(2,1)S(1)}, bf16[64,208]{1,0:T(8,128)(2,1)S(1)}, u32[]{:S(2)}, u32[]{:S(2)}) collective-permute-start(bf16[64,208]{1,0:T(8,128)(2,1)S(1)} %get-tuple-element.110), channel_id=1, source_target_pairs={{0,64},{64,0},{128,192},{192,128},{1,65},{65,1},{129,193},{193,129... | collective-permute-start | bytes 79880 | tf_op jit(solution)/shard_map/ppermute | solution.py:451
  80.8 14.1 %all-to-all-start.1 = ((bf16[8,40,512]{2,1,0:T(8,128)(2,1)}), bf16[8,40,512]{2,1,0:T(8,128)(2,1)S(1)}, u32[]{:S(2)}, u32[]{:S(2)}) async-start(bf16[8,40,512]{2,1,0:T(8,128)(2,1)} %broadcast_in_dim.22), calls=%async_computation.1 | async-start | bytes 655360 | tf_op jit(solution)/shard_map/all_to_all | solution.py:519
  84.5 19.1 %copy-start.7 = (bf16[4,16,32,208]{3,2,1,0:T(8,128)(2,1)S(1)}, bf16[4,16,32,208]{3,2,1,0:T(8,128)(2,1)}, u32[]{:S(2)}) copy-start(bf16[4,16,32,208]{3,2,1,0:T(8,128)(2,1)} %copy-done.6) | copy-start | bytes 2555908
  85.6 9.4 %collective-permute-start.11 = (bf16[48,208]{1,0:T(8,128)(2,1)S(1)}, bf16[48,208]{1,0:T(8,128)(2,1)S(1)}, u32[]{:S(2)}, u32[]{:S(2)}) collective-permute-start(bf16[48,208]{1,0:T(8,128)(2,1)S(1)} %get-tuple-element.79), channel_id=1, source_target_pairs={{0,1},{1,0},{2,3},{3,2},{4,5},{5,4},{6,7},{7,6},{8,9},{9,8},{10,11... | collective-permute-start | bytes 59912 | tf_op jit(solution)/shard_map/ppermute | solution.py:451
  87.1 7.9 %collective-permute-start.12 = (bf16[48,208]{1,0:T(8,128)(2,1)S(1)}, bf16[48,208]{1,0:T(8,128)(2,1)S(1)}, u32[]{:S(2)}, u32[]{:S(2)}) collective-permute-start(bf16[48,208]{1,0:T(8,128)(2,1)S(1)} %get-tuple-element.80), channel_id=1, source_target_pairs={{1,2},{3,4},{5,6},{7,8},{9,10},{11,12},{13,14},{15,16},{17,18},{19... | collective-permute-start | bytes 59912 | tf_op jit(solution)/shard_map/ppermute | solution.py:452
  95.9 18.4 %all-to-all-start.2 = ((bf16[16,40,512]{2,1,0:T(8,128)(2,1)}), bf16[16,40,512]{2,1,0:T(8,128)(2,1)S(1)}, u32[]{:S(2)}, u32[]{:S(2)}) async-start(bf16[16,40,512]{2,1,0:T(8,128)(2,1)} %broadcast_in_dim.23), calls=%async_computation.2 | async-start | bytes 1310720 | tf_op jit(solution)/shard_map/all_to_all | solution.py:523
  103.7 1.2 %copy-start.9 = (bf16[4,16,32,208]{3,2,1,0:T(8,128)(2,1)S(1)}, bf16[4,16,32,208]{3,2,1,0:T(8,128)(2,1)}, u32[]{:S(2)}) copy-start(bf16[4,16,32,208]{3,2,1,0:T(8,128)(2,1)} %copy-done.8) | copy-start | bytes 2555908
  114.2 5.0 %collective-permute-start.13 = (bf16[640,512]{1,0:T(8,128)(2,1)S(1)}, bf16[640,512]{1,0:T(8,128)(2,1)S(1)}, u32[]{:S(2)}, u32[]{:S(2)}) collective-permute-start(bf16[640,512]{1,0:T(8,128)(2,1)S(1)} %bitcast.35), channel_id=1, source_target_pairs={{0,64},{64,0},{1,65},{65,1},{2,66},{66,2},{3,67},{67,3},{4,68},{68... | collective-permute-start | bytes 1966088 | tf_op jit(solution)/shard_map/ppermute | solution.py:525

commit v5 on v4

--- a/solution.py
+++ b/solution.py
@@ -112,7 +112,7 @@
         fine_conv(i, shifted, taps_ref, False, put)
         return carry
 
-    lax.fori_loop(0, 16, conv, 0, unroll=2)
+    lax.fori_loop(0, 16, conv, 0, unroll=4)
     chans = mix_ref.shape[0]
     wide = weight_ref.shape[1]
     for k in range(4):
@@ -170,7 +170,7 @@
         delta_red[i] = (cot_ref[i].astype(F4) + back * slope).astype(BF)
         return carry
 
-    lax.fori_loop(0, 16, conv, 0, unroll=2)
+    lax.fori_loop(0, 16, conv, 0, unroll=4)
 
 
 def fine_terms(
@@ -216,7 +216,7 @@
 def piece(j, chans, wide):
     room = LANES - wide
     return picker(
-        chans, LANES, lambda row: jnp.where(row // room == j, wide + row % room, -1)
+        chans, 128, lambda row: jnp.where(row // room == j, 128 - room + row % room, -1)
     )
 
 
@@ -329,15 +329,17 @@
         depth[i] = total.astype(BF)
         return carry
 
-    lax.fori_loop(0, 16, conv, 0, unroll=2)
+    lax.fori_loop(0, 16, conv, 0, unroll=4)
     flat = depth[...].reshape(512, wide)
     section_out[...] = (reduced_ref[...].reshape(512, wide).astype(F4) + dot(flat, mix_ref[...])).astype(BF).reshape(16, 32, wide)
     fine = jnp.concatenate([gmixf_ref[...], gtapsf_ref[...]], axis=0).astype(BF)
-    spread = picker(wide, LANES, lambda row: row)
+    full = LANES - 128
+    spread = picker(wide - full, 128, lambda row: row)
     for j in range(3):
         rows_of = slice(j * FINE, (j + 1) * FINE)
-        both = dot(gred_ref[rows_of, :], spread) + dot(fine, piece(j, fine.shape[1], wide))
-        packed[rows_of, :] = both.astype(BF)
+        both = dot(gred_ref[rows_of, full:], spread) + dot(fine, piece(j, fine.shape[1], wide))
+        packed[rows_of, :full] = gred_ref[rows_of, :full]
+        packed[rows_of, full:] = both.astype(BF)
     packed[3 * FINE :, :] = jnp.zeros((TOTAL - 3 * FINE, LANES), BF)
     packed[3 * FINE : MIXC, 0:wide] = gred_ref[3 * FINE :, :]
     packed[MIXC:TAPC, 0:wide] = dot_tn(flat, cot_ref[...].reshape(512, wide)).astype(BF)
@@ -362,7 +364,7 @@
     mixc_out[...] = packed[MIXC:TAPC, 0:wide].astype(F4) * coarse
     total = 0.0
     for j in range(3):
-        total = total + dot_nt(packed[j * FINE : (j + 1) * FINE, :], piece(j, chans, wide))
+        total = total + dot_nt(packed[j * FINE : (j + 1) * FINE, LANES - 128 :], piece(j, chans, wide))
     mixf_out[...] = total[:chans] * fine
     taps = total[chans:] * fine
     for a in range(3):
@@ -420,7 +422,7 @@
             out_ref[2 * i + p] = dot(weave, both).astype(BF)
         return carry
 
-    lax.fori_loop(0, 16, conv, 0, unroll=2)
+    lax.fori_loop(0, 16, conv, 0, unroll=4)
 
 
 def call(body, outs, scratch, flops, *operands):

time: 123 us -> 122 us (level)
  no operation moved by 1% of the time
where the time goes in v5:
time: 122 us; the launch traced here: 121 us
  starting transfers between devices  51 us (42%)
  Pallas kernels  31.5 us (26%)
  waiting for transfers between devices  29.5 us (24%)
  local copies, waits for them, and re-layouts  6.57 us (5%)
  other arithmetic  1.64 us (1%)
    pallas_call x9, Pallas kernels, call(): pl.pallas_call(body, out_shape=[jax.ShapeDtypeStruct(shape, kind) for sha...  31.5 us
    all_to_all x1, starting transfers between devices, reduce_terms(): got = lax.all_to_all(mine, PLANE, 0, 0, tiled=True)  14.2 us
    ppermute x6, starting transfers between devices, send(): lax.ppermute(away, axes, far)  12.3 us
    ppermute x6, starting transfers between devices, send(): lax.ppermute(near, axes, [(i, i ^ 1) for i in range(count)])  9.76 us
    all_to_all x1, waiting for transfers between devices, reduce_terms(): got = lax.all_to_all(mine, PLANE, 0, 0, tiled=True)  8.44 us
    all_to_all x1, starting transfers between devices, reduce_terms(): lax.all_to_all(jnp.broadcast_to(mine, (plane, chunk, lanes)), PLANE, 0, 0...  7.78 us
    all_to_all x1, waiting for transfers between devices, reduce_terms(): lax.all_to_all(jnp.broadcast_to(mine, (depth, chunk, lanes)), 'z', 0, 0,...  7.13 us
    all_to_all x1, waiting for transfers between devices, reduce_terms(): lax.all_to_all(jnp.broadcast_to(mine, (plane, chunk, lanes)), PLANE, 0, 0...  4.33 us
  transfers between devices with their start and end apart: 17, of which 7 were waited for; matrix products, arithmetic and copies ran while one was open for 2% of the time, Pallas kernels for 13%

profile of v5, /device:TPU:1, one launch (start us, length us, event | category | flops | bytes accessed | tf_op | source)
XLA Modules:
  0.0 121.4 jit_solution(637989581012720560)
XLA Ops:
  0.7 0.0 copy-start.1
  0.7 0.9 slice_bitcast_fusion.3
  1.6 1.0 fusion.11
  2.6 0.1 broadcast_select_fusion.2
  2.6 3.3 %collective-permute-start.1 = (bf16[192,416]{1,0:T(8,128)(2,1)S(1)}, bf16[192,416]{1,0:T(8,128)(2,1)S(1)}, u32[]{:S(2)}, u32[]{:S(2)}) collective-permute-start(bf16[192,416]{1,0:T(8,128)(2,1)S(1)} %get-tuple-element.105), channel_id=1, source_target_pairs={{0,64},{64,0},{128,192},{192,128},{1,65},{65,1},{129,193},{193,129... | collective-permute-start | bytes 479240 | tf_op jit(solution)/shard_map/ppermute | solution.py:453
  6.0 1.9 %collective-permute-start = (bf16[192,416]{1,0:T(8,128)(2,1)S(1)}, bf16[192,416]{1,0:T(8,128)(2,1)S(1)}, u32[]{:S(2)}, u32[]{:S(2)}) collective-permute-start(bf16[192,416]{1,0:T(8,128)(2,1)S(1)} %get-tuple-element.106), channel_id=1, source_target_pairs={{64,128},{128,64},{65,129},{129,65},{66,130},{130,66},{67,131},{13... | collective-permute-start | bytes 479240 | tf_op jit(solution)/shard_map/ppermute | solution.py:454
  7.9 1.6 %copy.36.weight_ref = bf16[832,416]{1,0:T(8,128)(2,1)S(1)} copy(bf16[832,416]{0,1:T(8,128)(2,1)} %param.10) | data formatting | bytes 1384448 | tf_op args[3]
  9.5 0.1 pad_add_fusion.flags_ref
  9.5 0.0 collective-permute-done.1.near_ref
  9.6 3.4 %collective-permute-done.away_ref = bf16[192,416]{1,0:T(8,128)(2,1)S(1)} collective-permute-done((bf16[192,416]{1,0:T(8,128)(2,1)S(1)}, bf16[192,416]{1,0:T(8,128)(2,1)S(1)}, u32[]{:S(2)}, u32[]{:S(2)}) %collective-permute-start) | collective-permute-done | bytes 159776 | tf_op jit(solution)/shard_map/ppermute | solution.py:454
  12.9 1.3 %shard_map.126 = (bf16[144,416]{1,0:T(8,128)(2,1)S(1)}, bf16[144,416]{1,0:T(8,128)(2,1)S(1)}) custom-call(s32[3]{0:T(128)S(1)} %pad_add_fusion.flags_ref, bf16[192,416]{1,0:T(8,128)(2,1)S(1)} %collective-permute-done.1.near_ref, bf16[192,416]{1,0:T(8,128)(2,1)S(1)} %collective-permute-done.away_ref, bf16[16,32,416]{2,1,0:T(8,128)(2,1)S(1)} %copy-done.1, ...), custom_call_target="tpu_custom_call" | custom-call | flops 10000000 | bytes 8000000 | tf_op jit(solution)/shard_map/pallas_call | solution.py:432
  14.3 0.7 collective-permute-start.2
  15.0 2.9 %collective-permute-start.3 = (bf16[144,416]{1,0:T(8,128)(2,1)S(1)}, bf16[144,416]{1,0:T(8,128)(2,1)S(1)}, u32[]{:S(2)}, u32[]{:S(2)}) collective-permute-start(bf16[144,416]{1,0:T(8,128)(2,1)S(1)} %get-tuple-element.52), channel_id=1, source_target_pairs={{0,1},{1,0},{2,3},{3,2},{4,5},{5,4},{6,7},{7,6},{8,9},{9,8},{10,11... | collective-permute-start | bytes 359432 | tf_op jit(solution)/shard_map/ppermute | solution.py:453
  17.9 0.0 copy-start.3
  17.9 0.0 copy-start.5
  18.0 0.0 collective-permute-done.2
  18.0 2.4 %collective-permute-done.3 = bf16[144,416]{1,0:T(8,128)(2,1)S(1)} collective-permute-done((bf16[144,416]{1,0:T(8,128)(2,1)S(1)}, bf16[144,416]{1,0:T(8,128)(2,1)S(1)}, u32[]{:S(2)}, u32[]{:S(2)}) %collective-permute-start.3) | collective-permute-done | bytes 119840 | tf_op jit(solution)/shard_map/ppermute | solution.py:453
  20.5 0.1 fusion.7.lr_ref.lrf_ref
  20.7 3.6 %shard_map.127 = (bf16[4,16,32,208]{3,2,1,0:T(8,128)(2,1)S(1)}, bf16[4,16,32,208]{3,2,1,0:T(8,128)(2,1)S(1)}, bf16[4,512,208]{2,1,0:T(8,128)(2,1)S(1)}, bf16[512...) custom-call(bf16[32,64,208]{2,1,0:T(8,128)(2,1)S(1)} %copy-done, bf16[1,64,208]{2,1,0:T(8,128)(2,1)S(1)} %get-tuple-element.112.top_ref, ...), custom_call_target="tpu_custom_call" | custom-call | flops 4000000000 | bytes 8000000 | tf_op jit(solution)/shard_map/pallas_call | solution.py:432
  24.3 0.0 copy-start.6
  24.3 0.0 copy-start.2
  24.3 0.0 copy-start.4
  24.3 0.1 collective-permute-start.4
  24.4 4.4 %collective-permute-start.5 = (bf16[128,416]{1,0:T(8,128)(2,1)S(1)}, bf16[128,416]{1,0:T(8,128)(2,1)S(1)}, u32[]{:S(2)}, u32[]{:S(2)}) collective-permute-start(bf16[128,416]{1,0:T(8,128)(2,1)S(1)} %bitcast.48), channel_id=1, source_target_pairs={{64,128},{128,64},{65,129},{129,65},{66,130},{130,66},{67,131},{13... | collective-permute-start | bytes 319496 | tf_op jit(solution)/shard_map/ppermute | solution.py:454
  28.8 0.1 copy_bitcast_fusion
  28.9 0.1 fusion.4.lr_ref
  29.1 4.2 %shard_map.128 = (bf16[16,32,416]{2,1,0:T(8,128)(2,1)S(1)}, bf16[16,32,416]{2,1,0:T(8,128)(2,1)S(1)}) custom-call(bf16[16,32,416]{2,1,0:T(8,128)(2,1)S(1)} %copy-done.1, bf16[8,32,416]{2,1,0:T(8,128)(2,1)S(1)} %pad_maximum_fusion.tb_ref, bf16[24,16,416]{2,1,0:T(8,128)(2,1)S(1)} %fusion.4.lr_ref, bf16[416,416]{1,0:T(8,128)(2,1)S(1)} %copy-done.2, ...), custom_call_target="tpu_custom_call" | custom-call | flops 8000000000 | bytes 8000000 | tf_op jit(solution)/shard_map/pallas_call | solution.py:432
  33.3 0.0 collective-permute-done.4.near_ref
  33.3 0.0 collective-permute-done.5.away_ref
  33.3 1.0 shard_map.129
  34.3 1.8 %collective-permute-start.6 = (bf16[96,416]{1,0:T(8,128)(2,1)S(1)}, bf16[96,416]{1,0:T(8,128)(2,1)S(1)}, u32[]{:S(2)}, u32[]{:S(2)}) collective-permute-start(bf16[96,416]{1,0:T(8,128)(2,1)S(1)} %get-tuple-element.58), channel_id=1, source_target_pairs={{0,1},{1,0},{2,3},{3,2},{4,5},{5,4},{6,7},{7,6},{8,9},{9,8},{10,11... | collective-permute-start | bytes 239624 | tf_op jit(solution)/shard_map/ppermute | solution.py:453
  36.1 0.8 collective-permute-start.7
  37.0 5.3 %shard_map.130 = (bf16[4,16,32,208]{3,2,1,0:T(8,128)(2,1)S(1)}, bf16[4,16,32,208]{3,2,1,0:T(8,128)(2,1)S(1)}, bf16[832,416]{1,0:T(8,128)(2,1)S(1)}, f32[208,208]{1,0:T(8,128)S(1)}, f32[16,208]{1,0:T(8,128)S(1)}) custom-call(bf16[512,416]{1,0:T(8,128)(2,1)S(1)} %bitcast.40, bf16[4,512,208]{2,1,0:T(8,128)(2,1)S(1)} %get-tuple-element.61.pre_ref, ...), custom_call_target="tpu_custom_call" | custom-call | flops 8000000000 | bytes 8000000 | tf_op jit(solution)/shard_map/pallas_call | solution.py:432
  42.3 0.0 copy-start.8
  42.3 0.0 collective-permute-done.6.nside_ref
  42.3 0.0 collective-permute-done.7.aside_ref
  42.3 7.4 %shard_map.131 = (bf16[16,32,416]{2,1,0:T(8,128)(2,1)}, bf16[640,512]{1,0:T(8,128)(2,1)S(1)}, bf16[640,512]{1,0:T(8,128)(2,1)S(1)}) custom-call(s32[3]{0:T(128)S(1)} %pad_add_fusion.flags_ref, bf16[16,32,416]{2,1,0:T(8,128)(2,1)S(1)} %get-tuple-element.53.act_ref, bf16[128,416]{1,0:T(8,128)(2,1)S(1)} %collective-permute-done.4.near_ref, ...), custom_call_target="tpu_custom_call" | custom-call | flops 4000000000 | bytes 8000000 | tf_op jit(solution)/shard_map/pallas_call | solution.py:432
  49.7 0.0 collective-permute-start.8
  49.7 2.1 %collective-permute-done.8 = bf16[640,512]{1,0:T(8,128)(2,1)S(1)} collective-permute-done((bf16[640,512]{1,0:T(8,128)(2,1)S(1)}, bf16[640,512]{1,0:T(8,128)(2,1)S(1)}, u32[]{:S(2)}, u32[]{:S(2)}) %collective-permute-start.8) | collective-permute-done | bytes 655392 | tf_op jit(solution)/shard_map/ppermute | solution.py:513
  51.8 1.0 add.43
  52.8 14.2 %all-to-all-start = ((bf16[16,40,512]{2,1,0:T(8,128)(2,1)}), bf16[16,40,512]{2,1,0:T(8,128)(2,1)S(1)}, u32[]{:S(2)}, u32[]{:S(2)}) async-start(bf16[16,40,512]{2,1,0:T(8,128)(2,1)} %bitcast.41), calls=%async_computation | async-start | bytes 1310720 | tf_op jit(solution)/shard_map/all_to_all | solution.py:517
  67.0 3.9 %collective-permute-start.10 = (bf16[64,208]{1,0:T(8,128)(2,1)S(1)}, bf16[64,208]{1,0:T(8,128)(2,1)S(1)}, u32[]{:S(2)}, u32[]{:S(2)}) collective-permute-start(bf16[64,208]{1,0:T(8,128)(2,1)S(1)} %get-tuple-element.109), channel_id=1, source_target_pairs={{64,128},{128,64},{65,129},{129,65},{66,130},{130,66},{67,131},{13... | collective-permute-start | bytes 79880 | tf_op jit(solution)/shard_map/ppermute | solution.py:454
  70.9 0.1 collective-permute-start.9
  71.0 8.4 %all-to-all-done = bf16[16,40,512]{2,1,0:T(8,128)(2,1)S(1)} async-done(((bf16[16,40,512]{2,1,0:T(8,128)(2,1)}), bf16[16,40,512]{2,1,0:T(8,128)(2,1)S(1)}, u32[]{:S(2)}, u32[]{:S(2)}) %all-to-all-start) | async-done | bytes 655392 | tf_op jit(solution)/shard_map/all_to_all | solution.py:517
  79.4 0.1 reduce_sum.24
  79.5 0.0 collective-permute-done.10.away_ref
  79.6 0.0 collective-permute-done.9.near_ref
  79.6 0.7 broadcast_in_dim.22
  80.3 3.7 %all-to-all-start.1 = ((bf16[8,40,512]{2,1,0:T(8,128)(2,1)}), bf16[8,40,512]{2,1,0:T(8,128)(2,1)S(1)}, u32[]{:S(2)}, u32[]{:S(2)}) async-start(bf16[8,40,512]{2,1,0:T(8,128)(2,1)} %broadcast_in_dim.22), calls=%async_computation.1 | async-start | bytes 655360 | tf_op jit(solution)/shard_map/all_to_all | solution.py:521
  84.0 1.1 shard_map.132
  85.1 1.5 %collective-permute-start.11 = (bf16[48,208]{1,0:T(8,128)(2,1)S(1)}, bf16[48,208]{1,0:T(8,128)(2,1)S(1)}, u32[]{:S(2)}, u32[]{:S(2)}) collective-permute-start(bf16[48,208]{1,0:T(8,128)(2,1)S(1)} %get-tuple-element.79), channel_id=1, source_target_pairs={{0,1},{1,0},{2,3},{3,2},{4,5},{5,4},{6,7},{7,6},{8,9},{9,8},{10,11... | collective-permute-start | bytes 59912 | tf_op jit(solution)/shard_map/ppermute | solution.py:453
  86.6 0.7 collective-permute-start.12
  87.3 7.1 %all-to-all-done.1 = bf16[8,40,512]{2,1,0:T(8,128)(2,1)S(1)} async-done(((bf16[8,40,512]{2,1,0:T(8,128)(2,1)}), bf16[8,40,512]{2,1,0:T(8,128)(2,1)S(1)}, u32[]{:S(2)}, u32[]{:S(2)}) %all-to-all-start.1) | async-done | bytes 327712 | tf_op jit(solution)/shard_map/all_to_all | solution.py:521
  94.5 0.0 collective-permute-done.11.nside_ref
  94.5 0.0 collective-permute-done.12.aside_ref
  94.5 0.9 broadcast_in_dim.23
  95.4 7.8 %all-to-all-start.2 = ((bf16[16,40,512]{2,1,0:T(8,128)(2,1)}), bf16[16,40,512]{2,1,0:T(8,128)(2,1)S(1)}, u32[]{:S(2)}, u32[]{:S(2)}) async-start(bf16[16,40,512]{2,1,0:T(8,128)(2,1)} %broadcast_in_dim.23), calls=%async_computation.2 | async-start | bytes 1310720 | tf_op jit(solution)/shard_map/all_to_all | solution.py:525
  103.2 0.0 copy-start.9
  103.2 1.2 %copy-done.9 = bf16[4,16,32,208]{3,2,1,0:T(8,128)(2,1)S(1)} copy-done((bf16[4,16,32,208]{3,2,1,0:T(8,128)(2,1)S(1)}, bf16[4,16,32,208]{3,2,1,0:T(8,128)(2,1)}, u32[]{:S(2)}) %copy-start.9) | copy-done | bytes 851992
  104.4 5.0 %shard_map.133 = bf16[32,64,208]{2,1,0:T(8,128)(2,1)} custom-call(s32[3]{0:T(128)S(1)} %pad_add_fusion.flags_ref, bf16[4,16,32,208]{3,2,1,0:T(8,128)(2,1)S(1)} %get-tuple-element.73.ddepth_ref, bf16[64,208]{1,0:T(8,128)(2,1)S(1)} %collective-permute-done.9.near_ref, bf16[64,208]{1,0:T(8,128)(2,1)S(1)} %collective-permute-done.10.away_ref, ...), custom_call_target="tpu_custom_call" | custom-call | flops 2000000000 | bytes 8000000 | tf_op jit(solution)/shard_map/pallas_call | solution.py:432
  109.4 4.3 %all-to-all-done.2 = bf16[16,40,512]{2,1,0:T(8,128)(2,1)S(1)} async-done(((bf16[16,40,512]{2,1,0:T(8,128)(2,1)}), bf16[16,40,512]{2,1,0:T(8,128)(2,1)S(1)}, u32[]{:S(2)}, u32[]{:S(2)}) %all-to-all-start.2) | async-done | bytes 655392 | tf_op jit(solution)/shard_map/all_to_all | solution.py:525
  113.8 3.3 %collective-permute-start.13 = (bf16[640,512]{1,0:T(8,128)(2,1)S(1)}, bf16[640,512]{1,0:T(8,128)(2,1)S(1)}, u32[]{:S(2)}, u32[]{:S(2)}) collective-permute-start(bf16[640,512]{1,0:T(8,128)(2,1)S(1)} %bitcast.35), channel_id=1, source_target_pairs={{0,64},{64,0},{1,65},{65,1},{2,66},{66,2},{3,67},{67,3},{4,68},{68... | collective-permute-start | bytes 1966088 | tf_op jit(solution)/shard_map/ppermute | solution.py:527
  117.0 1.7 %collective-permute-done.13.far_ref = bf16[640,512]{1,0:T(8,128)(2,1)S(1)} collective-permute-done((bf16[640,512]{1,0:T(8,128)(2,1)S(1)}, bf16[640,512]{1,0:T(8,128)(2,1)S(1)}, u32[]{:S(2)}, u32[]{:S(2)}) %collective-permute-start.13) | collective-permute-done | bytes 655392 | tf_op jit(solution)/shard_map/ppermute | solution.py:527
  118.7 2.6 %shard_map.134 = (f32[3,3,208]{2,1,0:T(4,128)}, f32[208,208]{1,0:T(8,128)}, f32[416,832]{1,0:T(8,128)}, f32[5,5,416]{2,1,0:T(8,128)}, f32[416,416]{1,0:T(8,128)}) custom-call(s32[3]{0:T(128)S(1)} %pad_add_fusion.flags_ref, bf16[640,512]{1,0:T(8,128)(2,1)S(1)} %bitcast.36, bf16[640,512]{1,0:T(8,128)(2,1)S(1)} %collective-permute-done.13.far_ref), custom_call_target="tpu_custom_call" | custom-call | flops 1000000 | bytes 8000000 | tf_op jit(solution)/shard_map/pallas_call | solution.py:432
  (26 shorter events, 0.3 us)
Async XLA Ops:
  0.6 12.3 %copy-start = (bf16[32,64,208]{2,1,0:T(8,128)(2,1)S(1)}, bf16[32,64,208]{2,1,0:T(8,128)(2,1)}, u32[]{:S(2)}) copy-start(bf16[32,64,208]{2,1,0:T(8,128)(2,1)} %slide_ref.5) | copy-start | bytes 2555908
  0.7 12.3 %copy-start.1 = (bf16[16,32,416]{2,1,0:T(8,128)(2,1)S(1)}, bf16[16,32,416]{2,1,0:T(8,128)(2,1)}, u32[]{:S(2)}) copy-start(bf16[16,32,416]{2,1,0:T(8,128)(2,1)} %cot_ref.5) | copy-start | bytes 1277956
  2.6 6.9 %collective-permute-start.1 = (bf16[192,416]{1,0:T(8,128)(2,1)S(1)}, bf16[192,416]{1,0:T(8,128)(2,1)S(1)}, u32[]{:S(2)}, u32[]{:S(2)}) collective-permute-start(bf16[192,416]{1,0:T(8,128)(2,1)S(1)} %get-tuple-element.105), channel_id=1, source_target_pairs={{0,64},{64,0},{128,192},{192,128},{1,65},{65,1},{129,193},{193,129... | collective-permute-start | bytes 479240 | tf_op jit(solution)/shard_map/ppermute | solution.py:453
  6.0 7.0 %collective-permute-start = (bf16[192,416]{1,0:T(8,128)(2,1)S(1)}, bf16[192,416]{1,0:T(8,128)(2,1)S(1)}, u32[]{:S(2)}, u32[]{:S(2)}) collective-permute-start(bf16[192,416]{1,0:T(8,128)(2,1)S(1)} %get-tuple-element.106), channel_id=1, source_target_pairs={{64,128},{128,64},{65,129},{129,65},{66,130},{130,66},{67,131},{13... | collective-permute-start | bytes 479240 | tf_op jit(solution)/shard_map/ppermute | solution.py:454
  14.3 3.7 %collective-permute-start.2 = (bf16[144,416]{1,0:T(8,128)(2,1)S(1)}, bf16[144,416]{1,0:T(8,128)(2,1)S(1)}, u32[]{:S(2)}, u32[]{:S(2)}) collective-permute-start(bf16[144,416]{1,0:T(8,128)(2,1)S(1)} %get-tuple-element.51), channel_id=1, source_target_pairs={{1,2},{3,4},{5,6},{7,8},{9,10},{11,12},{13,14},{15,16},{17,18},{19... | collective-permute-start | bytes 359432 | tf_op jit(solution)/shard_map/ppermute | solution.py:454
  15.0 5.4 %collective-permute-start.3 = (bf16[144,416]{1,0:T(8,128)(2,1)S(1)}, bf16[144,416]{1,0:T(8,128)(2,1)S(1)}, u32[]{:S(2)}, u32[]{:S(2)}) collective-permute-start(bf16[144,416]{1,0:T(8,128)(2,1)S(1)} %get-tuple-element.52), channel_id=1, source_target_pairs={{0,1},{1,0},{2,3},{3,2},{4,5},{5,4},{6,7},{7,6},{8,9},{9,8},{10,11... | collective-permute-start | bytes 359432 | tf_op jit(solution)/shard_map/ppermute | solution.py:453
  17.9 2.8 %copy-start.3 = (bf16[208,208]{1,0:T(8,128)(2,1)S(1)}, bf16[208,208]{1,0:T(8,128)(2,1)}, u32[]{:S(2)}) copy-start(bf16[208,208]{1,0:T(8,128)(2,1)} %mix_ref.4) | copy-start | bytes 259588
  17.9 2.8 %copy-start.5 = (f32[3,3,208]{2,1,0:T(4,128)S(1)}, f32[3,3,208]{2,1,0:T(4,128)}, u32[]{:S(2)}) copy-start(f32[3,3,208]{2,1,0:T(4,128)} %taps_ref.5) | copy-start | bytes 22468
  24.3 9.0 %copy-start.6 = (bf16[4,16,32,208]{3,2,1,0:T(8,128)(2,1)}, bf16[4,16,32,208]{3,2,1,0:T(8,128)(2,1)S(1)}, u32[]{:S(2)}) copy-start(bf16[4,16,32,208]{3,2,1,0:T(8,128)(2,1)S(1)} %get-tuple-element.87.slide_ref) | copy-start | bytes 2555908
  24.3 4.8 %copy-start.2 = (bf16[416,416]{1,0:T(8,128)(2,1)S(1)}, bf16[416,416]{1,0:T(8,128)(2,1)}, u32[]{:S(2)}) copy-start(bf16[416,416]{1,0:T(8,128)(2,1)} %mix_ref.5) | copy-start | bytes 1038340
  24.3 4.8 %copy-start.4 = (f32[5,5,416]{2,1,0:T(8,128)S(1)}, f32[5,5,416]{2,1,0:T(8,128)}, u32[]{:S(2)}) copy-start(f32[5,5,416]{2,1,0:T(8,128)} %taps_ref.4) | copy-start | bytes 124804
  24.3 9.0 %collective-permute-start.4 = (bf16[128,416]{1,0:T(8,128)(2,1)S(1)}, bf16[128,416]{1,0:T(8,128)(2,1)S(1)}, u32[]{:S(2)}, u32[]{:S(2)}) collective-permute-start(bf16[128,416]{1,0:T(8,128)(2,1)S(1)} %bitcast.49), channel_id=1, source_target_pairs={{0,64},{64,0},{128,192},{192,128},{1,65},{65,1},{129,193},{193,129... | collective-permute-start | bytes 319496 | tf_op jit(solution)/shard_map/ppermute | solution.py:453
  24.4 8.9 %collective-permute-start.5 = (bf16[128,416]{1,0:T(8,128)(2,1)S(1)}, bf16[128,416]{1,0:T(8,128)(2,1)S(1)}, u32[]{:S(2)}, u32[]{:S(2)}) collective-permute-start(bf16[128,416]{1,0:T(8,128)(2,1)S(1)} %bitcast.48), channel_id=1, source_target_pairs={{64,128},{128,64},{65,129},{129,65},{66,130},{130,66},{67,131},{13... | collective-permute-start | bytes 319496 | tf_op jit(solution)/shard_map/ppermute | solution.py:454
  34.3 8.0 %collective-permute-start.6 = (bf16[96,416]{1,0:T(8,128)(2,1)S(1)}, bf16[96,416]{1,0:T(8,128)(2,1)S(1)}, u32[]{:S(2)}, u32[]{:S(2)}) collective-permute-start(bf16[96,416]{1,0:T(8,128)(2,1)S(1)} %get-tuple-element.58), channel_id=1, source_target_pairs={{0,1},{1,0},{2,3},{3,2},{4,5},{5,4},{6,7},{7,6},{8,9},{9,8},{10,11... | collective-permute-start | bytes 239624 | tf_op jit(solution)/shard_map/ppermute | solution.py:453
  36.1 6.1 %collective-permute-start.7 = (bf16[96,416]{1,0:T(8,128)(2,1)S(1)}, bf16[96,416]{1,0:T(8,128)(2,1)S(1)}, u32[]{:S(2)}, u32[]{:S(2)}) collective-permute-start(bf16[96,416]{1,0:T(8,128)(2,1)S(1)} %get-tuple-element.59), channel_id=1, source_target_pairs={{1,2},{3,4},{5,6},{7,8},{9,10},{11,12},{13,14},{15,16},{17,18},{19... | collective-permute-start | bytes 239624 | tf_op jit(solution)/shard_map/ppermute | solution.py:454
  42.3 7.5 %copy-start.8 = (bf16[4,16,32,208]{3,2,1,0:T(8,128)(2,1)}, bf16[4,16,32,208]{3,2,1,0:T(8,128)(2,1)S(1)}, u32[]{:S(2)}) copy-start(bf16[4,16,32,208]{3,2,1,0:T(8,128)(2,1)S(1)} %get-tuple-element.86.dfine_ref) | copy-start | bytes 2555908
  49.7 2.1 %collective-permute-start.8 = (bf16[640,512]{1,0:T(8,128)(2,1)S(1)}, bf16[640,512]{1,0:T(8,128)(2,1)S(1)}, u32[]{:S(2)}, u32[]{:S(2)}) collective-permute-start(bf16[640,512]{1,0:T(8,128)(2,1)S(1)} %get-tuple-element.72), channel_id=1, source_target_pairs={{0,64},{64,0},{1,65},{65,1},{2,66},{66,2},{3,67},{67,3},{4,68},{68... | collective-permute-start | bytes 1966088 | tf_op jit(solution)/shard_map/ppermute | solution.py:513
  52.8 26.6 %all-to-all-start = ((bf16[16,40,512]{2,1,0:T(8,128)(2,1)}), bf16[16,40,512]{2,1,0:T(8,128)(2,1)S(1)}, u32[]{:S(2)}, u32[]{:S(2)}) async-start(bf16[16,40,512]{2,1,0:T(8,128)(2,1)} %bitcast.41), calls=%async_computation | async-start | bytes 1310720 | tf_op jit(solution)/shard_map/all_to_all | solution.py:517
  67.0 12.5 %collective-permute-start.10 = (bf16[64,208]{1,0:T(8,128)(2,1)S(1)}, bf16[64,208]{1,0:T(8,128)(2,1)S(1)}, u32[]{:S(2)}, u32[]{:S(2)}) collective-permute-start(bf16[64,208]{1,0:T(8,128)(2,1)S(1)} %get-tuple-element.109), channel_id=1, source_target_pairs={{64,128},{128,64},{65,129},{129,65},{66,130},{130,66},{67,131},{13... | collective-permute-start | bytes 79880 | tf_op jit(solution)/shard_map/ppermute | solution.py:454
  70.9 8.6 %collective-permute-start.9 = (bf16[64,208]{1,0:T(8,128)(2,1)S(1)}, bf16[64,208]{1,0:T(8,128)(2,1)S(1)}, u32[]{:S(2)}, u32[]{:S(2)}) collective-permute-start(bf16[64,208]{1,0:T(8,128)(2,1)S(1)} %get-tuple-element.110), channel_id=1, source_target_pairs={{0,64},{64,0},{128,192},{192,128},{1,65},{65,1},{129,193},{193,129... | collective-permute-start | bytes 79880 | tf_op jit(solution)/shard_map/ppermute | solution.py:453
  80.3 14.1 %all-to-all-start.1 = ((bf16[8,40,512]{2,1,0:T(8,128)(2,1)}), bf16[8,40,512]{2,1,0:T(8,128)(2,1)S(1)}, u32[]{:S(2)}, u32[]{:S(2)}) async-start(bf16[8,40,512]{2,1,0:T(8,128)(2,1)} %broadcast_in_dim.22), calls=%async_computation.1 | async-start | bytes 655360 | tf_op jit(solution)/shard_map/all_to_all | solution.py:521
  84.0 19.1 %copy-start.7 = (bf16[4,16,32,208]{3,2,1,0:T(8,128)(2,1)S(1)}, bf16[4,16,32,208]{3,2,1,0:T(8,128)(2,1)}, u32[]{:S(2)}) copy-start(bf16[4,16,32,208]{3,2,1,0:T(8,128)(2,1)} %copy-done.6) | copy-start | bytes 2555908
  85.1 9.4 %collective-permute-start.11 = (bf16[48,208]{1,0:T(8,128)(2,1)S(1)}, bf16[48,208]{1,0:T(8,128)(2,1)S(1)}, u32[]{:S(2)}, u32[]{:S(2)}) collective-permute-start(bf16[48,208]{1,0:T(8,128)(2,1)S(1)} %get-tuple-element.79), channel_id=1, source_target_pairs={{0,1},{1,0},{2,3},{3,2},{4,5},{5,4},{6,7},{7,6},{8,9},{9,8},{10,11... | collective-permute-start | bytes 59912 | tf_op jit(solution)/shard_map/ppermute | solution.py:453
  86.6 7.9 %collective-permute-start.12 = (bf16[48,208]{1,0:T(8,128)(2,1)S(1)}, bf16[48,208]{1,0:T(8,128)(2,1)S(1)}, u32[]{:S(2)}, u32[]{:S(2)}) collective-permute-start(bf16[48,208]{1,0:T(8,128)(2,1)S(1)} %get-tuple-element.80), channel_id=1, source_target_pairs={{1,2},{3,4},{5,6},{7,8},{9,10},{11,12},{13,14},{15,16},{17,18},{19... | collective-permute-start | bytes 59912 | tf_op jit(solution)/shard_map/ppermute | solution.py:454
  95.4 18.4 %all-to-all-start.2 = ((bf16[16,40,512]{2,1,0:T(8,128)(2,1)}), bf16[16,40,512]{2,1,0:T(8,128)(2,1)S(1)}, u32[]{:S(2)}, u32[]{:S(2)}) async-start(bf16[16,40,512]{2,1,0:T(8,128)(2,1)} %broadcast_in_dim.23), calls=%async_computation.2 | async-start | bytes 1310720 | tf_op jit(solution)/shard_map/all_to_all | solution.py:525
  103.2 1.2 %copy-start.9 = (bf16[4,16,32,208]{3,2,1,0:T(8,128)(2,1)S(1)}, bf16[4,16,32,208]{3,2,1,0:T(8,128)(2,1)}, u32[]{:S(2)}) copy-start(bf16[4,16,32,208]{3,2,1,0:T(8,128)(2,1)} %copy-done.8) | copy-start | bytes 2555908
  113.8 5.0 %collective-permute-start.13 = (bf16[640,512]{1,0:T(8,128)(2,1)S(1)}, bf16[640,512]{1,0:T(8,128)(2,1)S(1)}, u32[]{:S(2)}, u32[]{:S(2)}) collective-permute-start(bf16[640,512]{1,0:T(8,128)(2,1)S(1)} %bitcast.35), channel_id=1, source_target_pairs={{0,64},{64,0},{1,65},{65,1},{2,66},{66,2},{3,67},{67,3},{4,68},{68... | collective-permute-start | bytes 1966088 | tf_op jit(solution)/shard_map/ppermute | solution.py:527
